TPU v7x, 128 devices: a whole 4x4x4 slice. The times are simulated.
128 devices in a mesh: dp: 4 (over x), seq: 32 (over z, y, core).
Axes of the slice: x: 4, y: 4, z: 4, core: 2. Of those that a mesh axis runs over, the one named last changes fastest.
Arguments:
- log_rows: bfloat16 [32768, 1024], P(('dp', 'seq')), may hold values from -6 to 6
- send_order: int32 [128, 256], P(('dp', 'seq')), may hold values from 0 to 255, each once within a row
- place: int32 [128, 256], P(('dp', 'seq')), may hold values from 0 to 255, each once within a row
- hist_len: int32 [4, 2], P('dp'), may hold values from 256 to 4096, as said below
- w_in: bfloat16 [1024, 4096], replicated, may hold values from -0.1875 to 0.1875
- w_out: bfloat16 [1024, 1024], replicated, may hold values from -0.1875 to 0.1875
- cotangent: bfloat16 [32768, 1024], P(('dp', 'seq')), may hold values from -6 to 6
Outputs:
- mixed: bfloat16 [32768, 1024], P(('dp', 'seq'))
- log_grad: float32 [32768, 1024], P(('dp', 'seq'))
Inputs may be any that keep to these rules, and one draw needn't show every extreme that they name: `send_order`: each row holds every number of 0 to 255 once. `place`: each row holds every number of 0 to 255 once. `hist_len`: at least one history has all 4096 events.
All inputs are finite; a program needn't handle non-finite values.
Results may differ from a plain program's by a relative error of at most 0.0075.
Values may be sent and summed in bfloat16 or wider, within the bound.
No kernel may reach another device: no remote copies, remote signals or barrier semaphores. Data moves between devices by JAX's collectives and lax.ppermute only.
A program may use at most 192 MiB of HBM per device.

v0:
```python
import math

import jax
import jax.numpy as jnp
from jax import lax
from jax.sharding import PartitionSpec as P

HEADS = 8


EPSILON = 1e-05


def shifted(block, axis, distance):
    devices = range(lax.axis_size(axis))
    route = [(i - distance, i) for i in devices if i - distance in devices]
    return lax.ppermute(block, axis, route)


def silu_grad(inputs):
    sigmoid = jax.nn.sigmoid(inputs)
    return sigmoid * (1.0 + inputs * (1.0 - sigmoid))


def normalize(inputs):
    centred = inputs - jnp.mean(inputs, axis=-1, keepdims=True)
    variance = jnp.mean(centred * centred, axis=-1, keepdims=True)
    inverse = lax.rsqrt(variance + EPSILON)
    return (centred * inverse, inverse)


def norm_back(upstream, normed, inverse):
    return inverse * (
        upstream
        - jnp.mean(upstream, axis=-1, keepdims=True)
        - normed * jnp.mean(upstream * normed, axis=-1, keepdims=True)
    )


def valid_pairs(query_position, key_position, length):
    return (key_position[None, :] <= query_position[:, None]) & (key_position[None, :] < length)


def body(log_rows, send_order, place, hist_len, w_in, w_out, cotangent):
    row_count, model_width = log_rows.shape
    head_dim = model_width // HEADS
    score_scale = 1.0 / math.sqrt(head_dim)
    group = min(16, lax.axis_size("seq"))
    outgoing = jnp.take(log_rows, send_order[0], axis=0)
    arrived = lax.all_to_all(outgoing, ("dp", "seq"), split_axis=0, concat_axis=0, tiled=True)
    history = jnp.take(arrived, place[0], axis=0)
    seq_index = lax.axis_index("seq")
    spot = seq_index % group
    length = jnp.take(hist_len[0], seq_index // group)
    counting = jnp.arange(row_count, dtype=jnp.int32)
    query_position = spot * row_count + counting

    def split_heads(block):
        return block.reshape(block.shape[0], HEADS, head_dim)

    hist_f32 = history.astype(jnp.float32)
    hist_hat, hist_inv = normalize(hist_f32)
    normed = hist_hat.astype(jnp.bfloat16)
    preact = jnp.dot(normed, w_in, preferred_element_type=jnp.float32)
    activated = jax.nn.silu(preact).astype(jnp.bfloat16)
    gate_rows = activated[:, :model_width]
    values_own = activated[:, model_width : 2 * model_width]
    queries = activated[:, 2 * model_width : 3 * model_width]
    keys_own = activated[:, 3 * model_width :]
    query_heads = split_heads(queries)
    empty_heads = jnp.zeros((row_count, HEADS, head_dim), jnp.float32)

    def key_live(offset):
        return (offset <= spot) & ((spot - offset) * row_count < length)

    def attend_block(running, keys_block, values_block, offset):
        key_position = (spot - offset) * row_count + counting

        def attend_compute(total):
            scores = (
                jnp.einsum(
                    "qhd,khd->hqk",
                    query_heads,
                    split_heads(keys_block),
                    preferred_element_type=jnp.float32,
                )
                * score_scale
            )
            allowed = valid_pairs(query_position, key_position, length)[None]
            weights = jnp.where(allowed, jax.nn.silu(scores), 0.0).astype(jnp.bfloat16)
            return total + jnp.einsum(
                "hqk,khd->qhd",
                weights,
                split_heads(values_block),
                preferred_element_type=jnp.float32,
            )

        return lax.cond(key_live(offset), attend_compute, lambda total: total, running)

    key_store = jnp.zeros((group, row_count, model_width), jnp.bfloat16).at[0].set(keys_own)
    value_store = jnp.zeros((group, row_count, model_width), jnp.bfloat16).at[0].set(values_own)
    running = attend_block(empty_heads, keys_own, values_own, 0)

    def pair_turn(offset, carry):
        moving, total, keys_kept, values_kept = carry
        moving = shifted((moving[0], moving[1]), "seq", 1)
        total = attend_block(total, moving[0], moving[1], offset)
        keys_kept = lax.dynamic_update_index_in_dim(keys_kept, moving[0], offset, 0)
        values_kept = lax.dynamic_update_index_in_dim(values_kept, moving[1], offset, 0)
        return (moving, total, keys_kept, values_kept)

    _, running, key_store, value_store = lax.fori_loop(
        1, group, pair_turn, ((keys_own, values_own), running, key_store, value_store)
    )
    attended = running.reshape(row_count, model_width)
    attend_hat, attend_inv = normalize(attended)
    gate_f32 = gate_rows.astype(jnp.float32)
    gated_rows = (attend_hat * gate_f32).astype(jnp.bfloat16)
    mixed_rows = (hist_f32 + jnp.dot(gated_rows, w_out, preferred_element_type=jnp.float32)).astype(
        jnp.bfloat16
    )
    upstream = jnp.dot(cotangent, w_out.T, preferred_element_type=jnp.float32)
    grad_gate = upstream * attend_hat
    grad_attended = norm_back(upstream * gate_f32, attend_hat, attend_inv).astype(jnp.bfloat16)
    grad_heads = split_heads(grad_attended)

    def query_turn(offset, total):
        keys_block = split_heads(key_store[offset])
        values_block = split_heads(value_store[offset])
        key_position = (spot - offset) * row_count + counting

        def query_compute(acc):
            scores = (
                jnp.einsum(
                    "qhd,khd->hqk", query_heads, keys_block, preferred_element_type=jnp.float32
                )
                * score_scale
            )
            allowed = valid_pairs(query_position, key_position, length)[None]
            grad_weights = jnp.einsum(
                "qhd,khd->hqk", grad_heads, values_block, preferred_element_type=jnp.float32
            )
            grad_scores = jnp.where(allowed, grad_weights * silu_grad(scores), 0.0).astype(
                jnp.bfloat16
            )
            return (
                acc
                + jnp.einsum(
                    "hqk,khd->qhd", grad_scores, keys_block, preferred_element_type=jnp.float32
                )
                * score_scale
            )

        return lax.cond(key_live(offset), query_compute, lambda acc: acc, total)

    grad_query = lax.fori_loop(0, group, query_turn, empty_heads).reshape(row_count, model_width)

    def key_terms(
        piece_qheads, piece_gheads, piece_position, keys_block, values_block, key_position
    ):
        key_heads = split_heads(keys_block)
        value_heads = split_heads(values_block)
        scores = (
            jnp.einsum("qhd,khd->hqk", piece_qheads, key_heads, preferred_element_type=jnp.float32)
            * score_scale
        )
        allowed = valid_pairs(piece_position, key_position, length)[None]
        weights = jnp.where(allowed, jax.nn.silu(scores), 0.0).astype(jnp.bfloat16)
        grad_weights = jnp.einsum(
            "qhd,khd->hqk", piece_gheads, value_heads, preferred_element_type=jnp.float32
        )
        grad_scores = jnp.where(allowed, grad_weights * silu_grad(scores), 0.0).astype(jnp.bfloat16)
        key_term = (
            jnp.einsum(
                "hqk,qhd->khd", grad_scores, piece_qheads, preferred_element_type=jnp.float32
            )
            * score_scale
        )
        value_term = jnp.einsum(
            "hqk,qhd->khd", weights, piece_gheads, preferred_element_type=jnp.float32
        )
        return jnp.concatenate(
            [key_term.reshape(row_count, model_width), value_term.reshape(row_count, model_width)],
            axis=1,
        )

    zero_terms = jnp.zeros((row_count, 2 * model_width), jnp.float32)

    def stored_term(offset):
        key_position = (spot - offset) * row_count + counting
        return lax.cond(
            key_live(offset),
            lambda: key_terms(
                query_heads,
                grad_heads,
                query_position,
                key_store[offset],
                value_store[offset],
                key_position,
            ),
            lambda: zero_terms,
        )

    def partial_turn(step, acc):
        offset = group - 1 - step
        return shifted((acc + stored_term(offset)).astype(jnp.bfloat16), "seq", -1).astype(
            jnp.float32
        )

    carried = lax.fori_loop(0, group - 1, partial_turn, zero_terms)
    summed = carried + stored_term(0)
    grad_key = summed[:, :model_width]
    grad_value = summed[:, model_width:]
    grad_act = jnp.concatenate([grad_gate, grad_value, grad_query, grad_key], axis=1)
    grad_pre = (grad_act * silu_grad(preact)).astype(jnp.bfloat16)
    grad_norm = jnp.dot(grad_pre, w_in.T, preferred_element_type=jnp.float32)
    grad_history = norm_back(grad_norm, hist_hat, hist_inv) + cotangent.astype(jnp.float32)
    inverse_slots = jnp.zeros((row_count,), jnp.int32).at[place[0]].set(counting)
    returned = lax.all_to_all(
        jnp.take(grad_history, inverse_slots, axis=0).astype(jnp.bfloat16),
        ("dp", "seq"),
        split_axis=0,
        concat_axis=0,
        tiled=True,
    ).astype(jnp.float32)
    inverse_order = jnp.zeros((row_count,), jnp.int32).at[send_order[0]].set(counting)
    log_grad = jnp.take(returned, inverse_order, axis=0)
    return (mixed_rows, log_grad)


def solution(mesh):
    placed = (
        P(("dp", "seq"), None),
        P(("dp", "seq"), None),
        P(("dp", "seq"), None),
        P("dp", None),
        P(),
        P(),
        P(("dp", "seq"), None),
    )
    return jax.shard_map(
        body,
        mesh=mesh,
        in_specs=placed,
        out_specs=(P(("dp", "seq"), None), P(("dp", "seq"), None)),
        check_vma=False,
    )
```

profile of v0, /device:TPU:1, one launch (start us, length us, event | category | flops | bytes accessed | tf_op | source)
XLA Modules:
  0.0 1195.7 jit_solution(10920157302581172179)
XLA Ops:
  6.0 11.5 all-to-all-start
  33.0 8.0 multiply_convert_fusion
  56.9 307.2 %while.61 = (s32[]{:T(128)}, bf16[256,1024]{1,0:T(8,128)(2,1)}, bf16[256,1024]{1,0:T(8,128)(2,1)}, f32[256,8,128]{2,0,1:T(8,128)}, bf16[16,256,1024]{2,1,0:T(8,1...) while((s32[]{:T(128)}, bf16[256,1024]{1,0:T(8,128)(2,1)}, ...), condition=%wide.region_7.9_spmd.clone, body=%wide.region_4.8_spmd.clone.sunk | while | flops 272499456 | bytes 12197781 | solution.py:112
  97.3 7.9 collective-permute-start
  281.5 7.8 collective-permute-start.1
  325.0 7.7 collective-permute-start.1
  373.4 12.3 %copy.46 = bf16[16,256,1024]{1,2,0:T(8,128)(2,1)} copy(bf16[16,256,1024]{2,1,0:T(8,128)(2,1)} %get-tuple-element.1056) | data formatting | bytes 16777216
  385.7 466.1 %while.63 = (s32[]{:T(128)}, f32[256,2048]{0,1:T(8,128)}, s32[]{:T(128)}, s32[]{:T(128)}, bf16[16,256,1024]{2,1,0:T(8,128)(2,1)}, /*index=5*/bf16[256,8,128]{0,2...) while((s32[]{:T(128)}, f32[256,2048]{0,1:T(8,128)}, ...), condition=%wide.region_15.17_spmd.clone, body=%wide.region_12.16_spmd.clone.sunk | while | flops 549323520 | bytes 42147760 | solution.py:210
  392.0 15.2 %collective-permute-done.2 = bf16[256,2048]{0,1:T(8,128)(2,1)} collective-permute-done((bf16[256,2048]{0,1:T(8,128)(2,1)}, bf16[256,2048]{0,1:T(8,128)(2,1)}, u32[]{:S(2)}, u32[]{:S(2)}) %collective-permute-start.2) | collective-permute-done | bytes 1048608 | tf_op jit(solution)/shard_map/while/body/eval_jaxpr/ppermute | solution.py:17
  416.8 14.5 %collective-permute-done.2 = bf16[256,2048]{0,1:T(8,128)(2,1)} collective-permute-done((bf16[256,2048]{0,1:T(8,128)(2,1)}, bf16[256,2048]{0,1:T(8,128)(2,1)}, u32[]{:S(2)}, u32[]{:S(2)}) %collective-permute-start.2) | collective-permute-done | bytes 1048608 | tf_op jit(solution)/shard_map/while/body/eval_jaxpr/ppermute | solution.py:17
  441.0 14.5 %collective-permute-done.2 = bf16[256,2048]{0,1:T(8,128)(2,1)} collective-permute-done((bf16[256,2048]{0,1:T(8,128)(2,1)}, bf16[256,2048]{0,1:T(8,128)(2,1)}, u32[]{:S(2)}, u32[]{:S(2)}) %collective-permute-start.2) | collective-permute-done | bytes 1048608 | tf_op jit(solution)/shard_map/while/body/eval_jaxpr/ppermute | solution.py:17
  465.1 14.5 %collective-permute-done.2 = bf16[256,2048]{0,1:T(8,128)(2,1)} collective-permute-done((bf16[256,2048]{0,1:T(8,128)(2,1)}, bf16[256,2048]{0,1:T(8,128)(2,1)}, u32[]{:S(2)}, u32[]{:S(2)}) %collective-permute-start.2) | collective-permute-done | bytes 1048608 | tf_op jit(solution)/shard_map/while/body/eval_jaxpr/ppermute | solution.py:17
  489.3 14.5 %collective-permute-done.2 = bf16[256,2048]{0,1:T(8,128)(2,1)} collective-permute-done((bf16[256,2048]{0,1:T(8,128)(2,1)}, bf16[256,2048]{0,1:T(8,128)(2,1)}, u32[]{:S(2)}, u32[]{:S(2)}) %collective-permute-start.2) | collective-permute-done | bytes 1048608 | tf_op jit(solution)/shard_map/while/body/eval_jaxpr/ppermute | solution.py:17
  513.4 14.5 %collective-permute-done.2 = bf16[256,2048]{0,1:T(8,128)(2,1)} collective-permute-done((bf16[256,2048]{0,1:T(8,128)(2,1)}, bf16[256,2048]{0,1:T(8,128)(2,1)}, u32[]{:S(2)}, u32[]{:S(2)}) %collective-permute-start.2) | collective-permute-done | bytes 1048608 | tf_op jit(solution)/shard_map/while/body/eval_jaxpr/ppermute | solution.py:17
  537.6 14.5 %collective-permute-done.2 = bf16[256,2048]{0,1:T(8,128)(2,1)} collective-permute-done((bf16[256,2048]{0,1:T(8,128)(2,1)}, bf16[256,2048]{0,1:T(8,128)(2,1)}, u32[]{:S(2)}, u32[]{:S(2)}) %collective-permute-start.2) | collective-permute-done | bytes 1048608 | tf_op jit(solution)/shard_map/while/body/eval_jaxpr/ppermute | solution.py:17
  561.7 14.5 %collective-permute-done.2 = bf16[256,2048]{0,1:T(8,128)(2,1)} collective-permute-done((bf16[256,2048]{0,1:T(8,128)(2,1)}, bf16[256,2048]{0,1:T(8,128)(2,1)}, u32[]{:S(2)}, u32[]{:S(2)}) %collective-permute-start.2) | collective-permute-done | bytes 1048608 | tf_op jit(solution)/shard_map/while/body/eval_jaxpr/ppermute | solution.py:17
  585.9 14.5 %collective-permute-done.2 = bf16[256,2048]{0,1:T(8,128)(2,1)} collective-permute-done((bf16[256,2048]{0,1:T(8,128)(2,1)}, bf16[256,2048]{0,1:T(8,128)(2,1)}, u32[]{:S(2)}, u32[]{:S(2)}) %collective-permute-start.2) | collective-permute-done | bytes 1048608 | tf_op jit(solution)/shard_map/while/body/eval_jaxpr/ppermute | solution.py:17
  610.1 14.5 %collective-permute-done.2 = bf16[256,2048]{0,1:T(8,128)(2,1)} collective-permute-done((bf16[256,2048]{0,1:T(8,128)(2,1)}, bf16[256,2048]{0,1:T(8,128)(2,1)}, u32[]{:S(2)}, u32[]{:S(2)}) %collective-permute-start.2) | collective-permute-done | bytes 1048608 | tf_op jit(solution)/shard_map/while/body/eval_jaxpr/ppermute | solution.py:17
  634.2 14.5 %collective-permute-done.2 = bf16[256,2048]{0,1:T(8,128)(2,1)} collective-permute-done((bf16[256,2048]{0,1:T(8,128)(2,1)}, bf16[256,2048]{0,1:T(8,128)(2,1)}, u32[]{:S(2)}, u32[]{:S(2)}) %collective-permute-start.2) | collective-permute-done | bytes 1048608 | tf_op jit(solution)/shard_map/while/body/eval_jaxpr/ppermute | solution.py:17
  658.4 14.5 %collective-permute-done.2 = bf16[256,2048]{0,1:T(8,128)(2,1)} collective-permute-done((bf16[256,2048]{0,1:T(8,128)(2,1)}, bf16[256,2048]{0,1:T(8,128)(2,1)}, u32[]{:S(2)}, u32[]{:S(2)}) %collective-permute-start.2) | collective-permute-done | bytes 1048608 | tf_op jit(solution)/shard_map/while/body/eval_jaxpr/ppermute | solution.py:17
  682.5 14.5 %collective-permute-done.2 = bf16[256,2048]{0,1:T(8,128)(2,1)} collective-permute-done((bf16[256,2048]{0,1:T(8,128)(2,1)}, bf16[256,2048]{0,1:T(8,128)(2,1)}, u32[]{:S(2)}, u32[]{:S(2)}) %collective-permute-start.2) | collective-permute-done | bytes 1048608 | tf_op jit(solution)/shard_map/while/body/eval_jaxpr/ppermute | solution.py:17
  706.7 104.8 %collective-permute-done.2 = bf16[256,2048]{0,1:T(8,128)(2,1)} collective-permute-done((bf16[256,2048]{0,1:T(8,128)(2,1)}, bf16[256,2048]{0,1:T(8,128)(2,1)}, u32[]{:S(2)}, u32[]{:S(2)}) %collective-permute-start.2) | collective-permute-done | bytes 1048608 | tf_op jit(solution)/shard_map/while/body/eval_jaxpr/ppermute | solution.py:17
  814.2 12.8 %conditional.15 = (f32[256,2048]{0,1:T(8,128)}) conditional(s32[]{:T(128)} %convert_element_type.206, () %tuple.206, (s32[]{:T(128)}, s32[256]{0:T(256)S(1)}, s32[]{:T(128)}, s32[]{:T(128)}, s32[]{:T(128)}, /*index=5*/bf16[16,256,1024]{2,1,0:T(8,128)(2,1)}, bf16[256,8,128]{0,2,1:T(8,128)(2,1)}, bf16[16,256,1024]{1,2,0:T(8,128)(2,1)}, ...), branch_computations={%region_13.14_spmd, %region_14.15_spmd} | conditional | flops 547226368 | bytes 29563510 | solution.py:191
  832.4 16.6 %collective-permute-done.2 = bf16[256,2048]{0,1:T(8,128)(2,1)} collective-permute-done((bf16[256,2048]{0,1:T(8,128)(2,1)}, bf16[256,2048]{0,1:T(8,128)(2,1)}, u32[]{:S(2)}, u32[]{:S(2)}) %collective-permute-start.2) | collective-permute-done | bytes 1048608 | tf_op jit(solution)/shard_map/while/body/eval_jaxpr/ppermute | solution.py:17
  854.7 30.9 %conditional.6 = (f32[256,2048]{1,0:T(8,128)}) conditional(s32[]{:T(128)} %convert_element_type.106, () %tuple.125, (s32[256]{0:T(256)S(1)}, s32[]{:T(128)}, bf16[16,256,1024]{2,1,0:T(8,128)(2,1)}, bf16[256,8,128]{2,1,0:T(8,128)(2,1)S(1)}, bf16[16,256,1024]{2,1,0:T(8,128)(2,1)}, /*index=5*/bf16[256,8,128]{2,1,0:T(8,128)(2,1)}) %tuple.234), branch_computations={%region_16.18_spmd, %region_17.19_spmd} | conditional | flops 547225856 | bytes 54725216 | solution.py:191
  857.2 12.4 %copy.49 = bf16[16,256,1024]{1,2,0:T(8,128)(2,1)} copy(bf16[16,256,1024]{2,1,0:T(8,128)(2,1)} %get-tuple-element.1048) | data formatting | bytes 16777216 | tf_op jit(solution)/shard_map
  890.7 18.2 %while.62 = (s32[]{:T(128)}, f32[256,8,128]{2,0,1:T(8,128)}, s32[]{:T(128)}, s32[]{:T(128)}, bf16[16,256,1024]{2,1,0:T(8,128)(2,1)}, /*index=5*/bf16[256,8,128]{...) while((s32[]{:T(128)}, f32[256,8,128]{2,0,1:T(8,128)}, ...), condition=%wide.region_21.23_spmd.clone, body=%wide.region_18.22_spmd.clone.sunk | while | flops 409076480 | bytes 11673371 | solution.py:156
  890.7 8.7 conditional.14
  899.4 8.7 conditional.14
  910.6 10.4 fusion.131
  925.8 251.2 %all-to-all-start.1 = ((bf16[128,2,1024]{2,1,0:T(2,128)(2,1)}), bf16[128,2,1024]{2,1,0:T(2,128)(2,1)}, u32[]{:S(2)}, u32[]{:S(2)}) async-start(bf16[128,2,1024]{2,1,0:T(2,128)(2,1)} %all_to_all.17), calls=%async_computation.1 | async-start | bytes 1048576 | tf_op jit(solution)/shard_map/all_to_all | solution.py:219
  1180.0 10.2 all-to-all-done.1
  (426 shorter events, 570.0 us)
Async XLA Ops:
  6.0 25.0 %all-to-all-start = ((bf16[128,2,1024]{2,1,0:T(2,128)(2,1)}), bf16[128,2,1024]{2,1,0:T(2,128)(2,1)S(1)}, u32[]{:S(2)}, u32[]{:S(2)}) async-start(bf16[128,2,1024]{2,1,0:T(2,128)(2,1)} %all_to_all.14), calls=%async_computation | async-start | bytes 1048576 | tf_op jit(solution)/shard_map/all_to_all | solution.py:50
  58.8 12.0 %collective-permute-start.1 = (bf16[256,1024]{1,0:T(8,128)(2,1)}, bf16[256,1024]{1,0:T(8,128)(2,1)S(1)}, u32[]{:S(2)}, u32[]{:S(2)}) collective-permute-start(bf16[256,1024]{1,0:T(8,128)(2,1)} %get-tuple-element.1338), channel_id=1, source_target_pairs={{0,1},{1,2},{2,3},{3,4},{4,5},{5,6},{6,7},{7,8},{8,9},{9,10},{10,1... | collective-permute-start | bytes 1572872 | tf_op jit(solution)/shard_map/while/body/eval_jaxpr/ppermute | solution.py:17
  82.0 12.0 %collective-permute-start.1 = (bf16[256,1024]{1,0:T(8,128)(2,1)}, bf16[256,1024]{1,0:T(8,128)(2,1)S(1)}, u32[]{:S(2)}, u32[]{:S(2)}) collective-permute-start(bf16[256,1024]{1,0:T(8,128)(2,1)} %get-tuple-element.1338), channel_id=1, source_target_pairs={{0,1},{1,2},{2,3},{3,4},{4,5},{5,6},{6,7},{7,8},{8,9},{9,10},{10,1... | collective-permute-start | bytes 1572872 | tf_op jit(solution)/shard_map/while/body/eval_jaxpr/ppermute | solution.py:17
  97.3 14.3 %collective-permute-start = (bf16[256,1024]{1,0:T(8,128)(2,1)}, bf16[256,1024]{1,0:T(8,128)(2,1)S(1)}, u32[]{:S(2)}, u32[]{:S(2)}) collective-permute-start(bf16[256,1024]{1,0:T(8,128)(2,1)} %get-tuple-element.1337), channel_id=1, source_target_pairs={{0,1},{1,2},{2,3},{3,4},{4,5},{5,6},{6,7},{7,8},{8,9},{9,10},{10,1... | collective-permute-start | bytes 1572872 | tf_op jit(solution)/shard_map/while/body/eval_jaxpr/ppermute | solution.py:17
  105.2 12.0 %collective-permute-start.1 = (bf16[256,1024]{1,0:T(8,128)(2,1)}, bf16[256,1024]{1,0:T(8,128)(2,1)S(1)}, u32[]{:S(2)}, u32[]{:S(2)}) collective-permute-start(bf16[256,1024]{1,0:T(8,128)(2,1)} %get-tuple-element.1338), channel_id=1, source_target_pairs={{0,1},{1,2},{2,3},{3,4},{4,5},{5,6},{6,7},{7,8},{8,9},{9,10},{10,1... | collective-permute-start | bytes 1572872 | tf_op jit(solution)/shard_map/while/body/eval_jaxpr/ppermute | solution.py:17
  124.8 12.0 %collective-permute-start.1 = (bf16[256,1024]{1,0:T(8,128)(2,1)}, bf16[256,1024]{1,0:T(8,128)(2,1)S(1)}, u32[]{:S(2)}, u32[]{:S(2)}) collective-permute-start(bf16[256,1024]{1,0:T(8,128)(2,1)} %get-tuple-element.1338), channel_id=1, source_target_pairs={{0,1},{1,2},{2,3},{3,4},{4,5},{5,6},{6,7},{7,8},{8,9},{9,10},{10,1... | collective-permute-start | bytes 1572872 | tf_op jit(solution)/shard_map/while/body/eval_jaxpr/ppermute | solution.py:17
  144.4 12.0 %collective-permute-start.1 = (bf16[256,1024]{1,0:T(8,128)(2,1)}, bf16[256,1024]{1,0:T(8,128)(2,1)S(1)}, u32[]{:S(2)}, u32[]{:S(2)}) collective-permute-start(bf16[256,1024]{1,0:T(8,128)(2,1)} %get-tuple-element.1338), channel_id=1, source_target_pairs={{0,1},{1,2},{2,3},{3,4},{4,5},{5,6},{6,7},{7,8},{8,9},{9,10},{10,1... | collective-permute-start | bytes 1572872 | tf_op jit(solution)/shard_map/while/body/eval_jaxpr/ppermute | solution.py:17
  163.9 12.0 %collective-permute-start.1 = (bf16[256,1024]{1,0:T(8,128)(2,1)}, bf16[256,1024]{1,0:T(8,128)(2,1)S(1)}, u32[]{:S(2)}, u32[]{:S(2)}) collective-permute-start(bf16[256,1024]{1,0:T(8,128)(2,1)} %get-tuple-element.1338), channel_id=1, source_target_pairs={{0,1},{1,2},{2,3},{3,4},{4,5},{5,6},{6,7},{7,8},{8,9},{9,10},{10,1... | collective-permute-start | bytes 1572872 | tf_op jit(solution)/shard_map/while/body/eval_jaxpr/ppermute | solution.py:17
  183.5 12.0 %collective-permute-start.1 = (bf16[256,1024]{1,0:T(8,128)(2,1)}, bf16[256,1024]{1,0:T(8,128)(2,1)S(1)}, u32[]{:S(2)}, u32[]{:S(2)}) collective-permute-start(bf16[256,1024]{1,0:T(8,128)(2,1)} %get-tuple-element.1338), channel_id=1, source_target_pairs={{0,1},{1,2},{2,3},{3,4},{4,5},{5,6},{6,7},{7,8},{8,9},{9,10},{10,1... | collective-permute-start | bytes 1572872 | tf_op jit(solution)/shard_map/while/body/eval_jaxpr/ppermute | solution.py:17
  203.1 12.0 %collective-permute-start.1 = (bf16[256,1024]{1,0:T(8,128)(2,1)}, bf16[256,1024]{1,0:T(8,128)(2,1)S(1)}, u32[]{:S(2)}, u32[]{:S(2)}) collective-permute-start(bf16[256,1024]{1,0:T(8,128)(2,1)} %get-tuple-element.1338), channel_id=1, source_target_pairs={{0,1},{1,2},{2,3},{3,4},{4,5},{5,6},{6,7},{7,8},{8,9},{9,10},{10,1... | collective-permute-start | bytes 1572872 | tf_op jit(solution)/shard_map/while/body/eval_jaxpr/ppermute | solution.py:17
  222.7 12.0 %collective-permute-start.1 = (bf16[256,1024]{1,0:T(8,128)(2,1)}, bf16[256,1024]{1,0:T(8,128)(2,1)S(1)}, u32[]{:S(2)}, u32[]{:S(2)}) collective-permute-start(bf16[256,1024]{1,0:T(8,128)(2,1)} %get-tuple-element.1338), channel_id=1, source_target_pairs={{0,1},{1,2},{2,3},{3,4},{4,5},{5,6},{6,7},{7,8},{8,9},{9,10},{10,1... | collective-permute-start | bytes 1572872 | tf_op jit(solution)/shard_map/while/body/eval_jaxpr/ppermute | solution.py:17
  277.2 12.1 %collective-permute-start = (bf16[256,1024]{1,0:T(8,128)(2,1)}, bf16[256,1024]{1,0:T(8,128)(2,1)S(1)}, u32[]{:S(2)}, u32[]{:S(2)}) collective-permute-start(bf16[256,1024]{1,0:T(8,128)(2,1)} %get-tuple-element.1337), channel_id=1, source_target_pairs={{0,1},{1,2},{2,3},{3,4},{4,5},{5,6},{6,7},{7,8},{8,9},{9,10},{10,1... | collective-permute-start | bytes 1572872 | tf_op jit(solution)/shard_map/while/body/eval_jaxpr/ppermute | solution.py:17
  281.5 14.3 %collective-permute-start.1 = (bf16[256,1024]{1,0:T(8,128)(2,1)}, bf16[256,1024]{1,0:T(8,128)(2,1)S(1)}, u32[]{:S(2)}, u32[]{:S(2)}) collective-permute-start(bf16[256,1024]{1,0:T(8,128)(2,1)} %get-tuple-element.1338), channel_id=1, source_target_pairs={{0,1},{1,2},{2,3},{3,4},{4,5},{5,6},{6,7},{7,8},{8,9},{9,10},{10,1... | collective-permute-start | bytes 1572872 | tf_op jit(solution)/shard_map/while/body/eval_jaxpr/ppermute | solution.py:17
  303.3 14.1 %collective-permute-start.1 = (bf16[256,1024]{1,0:T(8,128)(2,1)}, bf16[256,1024]{1,0:T(8,128)(2,1)S(1)}, u32[]{:S(2)}, u32[]{:S(2)}) collective-permute-start(bf16[256,1024]{1,0:T(8,128)(2,1)} %get-tuple-element.1338), channel_id=1, source_target_pairs={{0,1},{1,2},{2,3},{3,4},{4,5},{5,6},{6,7},{7,8},{8,9},{9,10},{10,1... | collective-permute-start | bytes 1572872 | tf_op jit(solution)/shard_map/while/body/eval_jaxpr/ppermute | solution.py:17
  325.0 14.1 %collective-permute-start.1 = (bf16[256,1024]{1,0:T(8,128)(2,1)}, bf16[256,1024]{1,0:T(8,128)(2,1)S(1)}, u32[]{:S(2)}, u32[]{:S(2)}) collective-permute-start(bf16[256,1024]{1,0:T(8,128)(2,1)} %get-tuple-element.1338), channel_id=1, source_target_pairs={{0,1},{1,2},{2,3},{3,4},{4,5},{5,6},{6,7},{7,8},{8,9},{9,10},{10,1... | collective-permute-start | bytes 1572872 | tf_op jit(solution)/shard_map/while/body/eval_jaxpr/ppermute | solution.py:17
  346.6 14.1 %collective-permute-start.1 = (bf16[256,1024]{1,0:T(8,128)(2,1)}, bf16[256,1024]{1,0:T(8,128)(2,1)S(1)}, u32[]{:S(2)}, u32[]{:S(2)}) collective-permute-start(bf16[256,1024]{1,0:T(8,128)(2,1)} %get-tuple-element.1338), channel_id=1, source_target_pairs={{0,1},{1,2},{2,3},{3,4},{4,5},{5,6},{6,7},{7,8},{8,9},{9,10},{10,1... | collective-permute-start | bytes 1572872 | tf_op jit(solution)/shard_map/while/body/eval_jaxpr/ppermute | solution.py:17
  390.1 17.1 %collective-permute-start.2 = (bf16[256,2048]{0,1:T(8,128)(2,1)}, bf16[256,2048]{0,1:T(8,128)(2,1)}, u32[]{:S(2)}, u32[]{:S(2)}) collective-permute-start(bf16[256,2048]{0,1:T(8,128)(2,1)} %fusion.164), channel_id=1, source_target_pairs={{1,0},{2,1},{3,2},{4,3},{5,4},{6,5},{7,6},{8,7},{9,8},{10,9},{11,1... | collective-permute-start | bytes 3145736 | tf_op jit(solution)/shard_map/while/body/eval_jaxpr/ppermute | solution.py:17
  414.9 16.4 %collective-permute-start.2 = (bf16[256,2048]{0,1:T(8,128)(2,1)}, bf16[256,2048]{0,1:T(8,128)(2,1)}, u32[]{:S(2)}, u32[]{:S(2)}) collective-permute-start(bf16[256,2048]{0,1:T(8,128)(2,1)} %fusion.164), channel_id=1, source_target_pairs={{1,0},{2,1},{3,2},{4,3},{5,4},{6,5},{7,6},{8,7},{9,8},{10,9},{11,1... | collective-permute-start | bytes 3145736 | tf_op jit(solution)/shard_map/while/body/eval_jaxpr/ppermute | solution.py:17
  439.0 16.4 %collective-permute-start.2 = (bf16[256,2048]{0,1:T(8,128)(2,1)}, bf16[256,2048]{0,1:T(8,128)(2,1)}, u32[]{:S(2)}, u32[]{:S(2)}) collective-permute-start(bf16[256,2048]{0,1:T(8,128)(2,1)} %fusion.164), channel_id=1, source_target_pairs={{1,0},{2,1},{3,2},{4,3},{5,4},{6,5},{7,6},{8,7},{9,8},{10,9},{11,1... | collective-permute-start | bytes 3145736 | tf_op jit(solution)/shard_map/while/body/eval_jaxpr/ppermute | solution.py:17
  463.2 16.4 %collective-permute-start.2 = (bf16[256,2048]{0,1:T(8,128)(2,1)}, bf16[256,2048]{0,1:T(8,128)(2,1)}, u32[]{:S(2)}, u32[]{:S(2)}) collective-permute-start(bf16[256,2048]{0,1:T(8,128)(2,1)} %fusion.164), channel_id=1, source_target_pairs={{1,0},{2,1},{3,2},{4,3},{5,4},{6,5},{7,6},{8,7},{9,8},{10,9},{11,1... | collective-permute-start | bytes 3145736 | tf_op jit(solution)/shard_map/while/body/eval_jaxpr/ppermute | solution.py:17
  487.4 16.4 %collective-permute-start.2 = (bf16[256,2048]{0,1:T(8,128)(2,1)}, bf16[256,2048]{0,1:T(8,128)(2,1)}, u32[]{:S(2)}, u32[]{:S(2)}) collective-permute-start(bf16[256,2048]{0,1:T(8,128)(2,1)} %fusion.164), channel_id=1, source_target_pairs={{1,0},{2,1},{3,2},{4,3},{5,4},{6,5},{7,6},{8,7},{9,8},{10,9},{11,1... | collective-permute-start | bytes 3145736 | tf_op jit(solution)/shard_map/while/body/eval_jaxpr/ppermute | solution.py:17
  511.5 16.4 %collective-permute-start.2 = (bf16[256,2048]{0,1:T(8,128)(2,1)}, bf16[256,2048]{0,1:T(8,128)(2,1)}, u32[]{:S(2)}, u32[]{:S(2)}) collective-permute-start(bf16[256,2048]{0,1:T(8,128)(2,1)} %fusion.164), channel_id=1, source_target_pairs={{1,0},{2,1},{3,2},{4,3},{5,4},{6,5},{7,6},{8,7},{9,8},{10,9},{11,1... | collective-permute-start | bytes 3145736 | tf_op jit(solution)/shard_map/while/body/eval_jaxpr/ppermute | solution.py:17
  535.7 16.4 %collective-permute-start.2 = (bf16[256,2048]{0,1:T(8,128)(2,1)}, bf16[256,2048]{0,1:T(8,128)(2,1)}, u32[]{:S(2)}, u32[]{:S(2)}) collective-permute-start(bf16[256,2048]{0,1:T(8,128)(2,1)} %fusion.164), channel_id=1, source_target_pairs={{1,0},{2,1},{3,2},{4,3},{5,4},{6,5},{7,6},{8,7},{9,8},{10,9},{11,1... | collective-permute-start | bytes 3145736 | tf_op jit(solution)/shard_map/while/body/eval_jaxpr/ppermute | solution.py:17
  559.8 16.4 %collective-permute-start.2 = (bf16[256,2048]{0,1:T(8,128)(2,1)}, bf16[256,2048]{0,1:T(8,128)(2,1)}, u32[]{:S(2)}, u32[]{:S(2)}) collective-permute-start(bf16[256,2048]{0,1:T(8,128)(2,1)} %fusion.164), channel_id=1, source_target_pairs={{1,0},{2,1},{3,2},{4,3},{5,4},{6,5},{7,6},{8,7},{9,8},{10,9},{11,1... | collective-permute-start | bytes 3145736 | tf_op jit(solution)/shard_map/while/body/eval_jaxpr/ppermute | solution.py:17
  584.0 16.4 %collective-permute-start.2 = (bf16[256,2048]{0,1:T(8,128)(2,1)}, bf16[256,2048]{0,1:T(8,128)(2,1)}, u32[]{:S(2)}, u32[]{:S(2)}) collective-permute-start(bf16[256,2048]{0,1:T(8,128)(2,1)} %fusion.164), channel_id=1, source_target_pairs={{1,0},{2,1},{3,2},{4,3},{5,4},{6,5},{7,6},{8,7},{9,8},{10,9},{11,1... | collective-permute-start | bytes 3145736 | tf_op jit(solution)/shard_map/while/body/eval_jaxpr/ppermute | solution.py:17
  608.1 16.4 %collective-permute-start.2 = (bf16[256,2048]{0,1:T(8,128)(2,1)}, bf16[256,2048]{0,1:T(8,128)(2,1)}, u32[]{:S(2)}, u32[]{:S(2)}) collective-permute-start(bf16[256,2048]{0,1:T(8,128)(2,1)} %fusion.164), channel_id=1, source_target_pairs={{1,0},{2,1},{3,2},{4,3},{5,4},{6,5},{7,6},{8,7},{9,8},{10,9},{11,1... | collective-permute-start | bytes 3145736 | tf_op jit(solution)/shard_map/while/body/eval_jaxpr/ppermute | solution.py:17
  632.3 16.4 %collective-permute-start.2 = (bf16[256,2048]{0,1:T(8,128)(2,1)}, bf16[256,2048]{0,1:T(8,128)(2,1)}, u32[]{:S(2)}, u32[]{:S(2)}) collective-permute-start(bf16[256,2048]{0,1:T(8,128)(2,1)} %fusion.164), channel_id=1, source_target_pairs={{1,0},{2,1},{3,2},{4,3},{5,4},{6,5},{7,6},{8,7},{9,8},{10,9},{11,1... | collective-permute-start | bytes 3145736 | tf_op jit(solution)/shard_map/while/body/eval_jaxpr/ppermute | solution.py:17
  656.5 16.4 %collective-permute-start.2 = (bf16[256,2048]{0,1:T(8,128)(2,1)}, bf16[256,2048]{0,1:T(8,128)(2,1)}, u32[]{:S(2)}, u32[]{:S(2)}) collective-permute-start(bf16[256,2048]{0,1:T(8,128)(2,1)} %fusion.164), channel_id=1, source_target_pairs={{1,0},{2,1},{3,2},{4,3},{5,4},{6,5},{7,6},{8,7},{9,8},{10,9},{11,1... | collective-permute-start | bytes 3145736 | tf_op jit(solution)/shard_map/while/body/eval_jaxpr/ppermute | solution.py:17
  680.6 16.4 %collective-permute-start.2 = (bf16[256,2048]{0,1:T(8,128)(2,1)}, bf16[256,2048]{0,1:T(8,128)(2,1)}, u32[]{:S(2)}, u32[]{:S(2)}) collective-permute-start(bf16[256,2048]{0,1:T(8,128)(2,1)} %fusion.164), channel_id=1, source_target_pairs={{1,0},{2,1},{3,2},{4,3},{5,4},{6,5},{7,6},{8,7},{9,8},{10,9},{11,1... | collective-permute-start | bytes 3145736 | tf_op jit(solution)/shard_map/while/body/eval_jaxpr/ppermute | solution.py:17
  704.8 106.7 %collective-permute-start.2 = (bf16[256,2048]{0,1:T(8,128)(2,1)}, bf16[256,2048]{0,1:T(8,128)(2,1)}, u32[]{:S(2)}, u32[]{:S(2)}) collective-permute-start(bf16[256,2048]{0,1:T(8,128)(2,1)} %fusion.164), channel_id=1, source_target_pairs={{1,0},{2,1},{3,2},{4,3},{5,4},{6,5},{7,6},{8,7},{9,8},{10,9},{11,1... | collective-permute-start | bytes 3145736 | tf_op jit(solution)/shard_map/while/body/eval_jaxpr/ppermute | solution.py:17
  830.5 18.5 %collective-permute-start.2 = (bf16[256,2048]{0,1:T(8,128)(2,1)}, bf16[256,2048]{0,1:T(8,128)(2,1)}, u32[]{:S(2)}, u32[]{:S(2)}) collective-permute-start(bf16[256,2048]{0,1:T(8,128)(2,1)} %fusion.164), channel_id=1, source_target_pairs={{1,0},{2,1},{3,2},{4,3},{5,4},{6,5},{7,6},{8,7},{9,8},{10,9},{11,1... | collective-permute-start | bytes 3145736 | tf_op jit(solution)/shard_map/while/body/eval_jaxpr/ppermute | solution.py:17
  925.8 264.4 %all-to-all-start.1 = ((bf16[128,2,1024]{2,1,0:T(2,128)(2,1)}), bf16[128,2,1024]{2,1,0:T(2,128)(2,1)}, u32[]{:S(2)}, u32[]{:S(2)}) async-start(bf16[128,2,1024]{2,1,0:T(2,128)(2,1)} %all_to_all.17), calls=%async_computation.1 | async-start | bytes 1048576 | tf_op jit(solution)/shard_map/all_to_all | solution.py:219
  (42 other events, 1195.0 us)
where the time goes:
time: 1200 us
  waiting for transfers between devices  465 us (39%)
  starting transfers between devices  409 us (34%)
  local copies, waits for them, and re-layouts  146 us (12%)
  other arithmetic  116 us (10%)
  matrix products  56 us (5%)
    ppermute x45, waiting for transfers between devices, shifted(): return lax.ppermute(block, axis, route)  447 us
    all_to_all x1, starting transfers between devices, body(): lax.all_to_all(jnp.take(grad_history, inverse_slots, axis=0).astype(jnp.b...  251 us
    ppermute x45, starting transfers between devices, shifted(): return lax.ppermute(block, axis, route)  146 us
    convert_element_type x15, other arithmetic, partial_turn(): (acc + stored_term(offset)).astype(jnp.bfloat16)  51.8 us
    convert_element_type x15, other arithmetic, partial_turn(): shifted((acc + stored_term(offset)).astype(jnp.bfloat16), 'seq', -1)  41.4 us
  transfers between devices with their start and end apart: 47, of which 43 were waited for; matrix products, arithmetic and copies ran while one was open for 1% of the time, Pallas kernels for 0%

commit v1 on v0

v1 whole, which is shorter than its diff:
```python
import functools
import math

import jax
import jax.numpy as jnp
from jax import lax
from jax.experimental import pallas as pl
from jax.experimental.pallas import tpu as pltpu
from jax.sharding import PartitionSpec as P

HEADS = 8
GROUP = 16
EPSILON = 1e-05
HALF = 128
HEAD_DIM = 128
TILE = 2
BF16 = jnp.bfloat16
F32 = jnp.float32
VMEM = pltpu.VMEM
SMEM = pltpu.SMEM


def params(limit=48 * 1024 * 1024, **kw):
    return pltpu.CompilerParams(vmem_limit_bytes=limit, **kw)


def vspec():
    return pl.BlockSpec(memory_space=VMEM)


def sspec():
    return pl.BlockSpec(memory_space=SMEM)


def dot(a, b):
    return jnp.dot(a, b, preferred_element_type=F32)


def dot_nt(a, b):
    return lax.dot_general(a, b, (((1,), (1,)), ((), ())), preferred_element_type=F32)


def dot_tn(a, b):
    return lax.dot_general(a, b, (((0,), (0,)), ((), ())), preferred_element_type=F32)


def onehot(order):
    count = order.shape[1]
    spots = lax.broadcasted_iota(jnp.int32, (count, count), 0)
    return jnp.where(spots == order, 1.0, 0.0).astype(BF16)


def row_mean(x):
    return jnp.mean(x, axis=-1, keepdims=True)


def normalize(inputs):
    centred = inputs - row_mean(inputs)
    inverse = lax.rsqrt(row_mean(centred * centred) + EPSILON)
    return centred * inverse, inverse


def pick_kernel(rows_ref, order_ref, out_ref):
    out_ref[...] = dot_tn(onehot(order_ref[...]), rows_ref[...]).astype(out_ref.dtype)


def pick_rows(rows, order):
    return pl.pallas_call(
        pick_kernel,
        out_shape=jax.ShapeDtypeStruct(rows.shape, rows.dtype),
        in_specs=[vspec(), vspec()],
        out_specs=vspec(),
        compiler_params=params(),
        name="pick_rows",
    )(rows, order)


def unpick_kernel(rows_ref, order_ref, out_ref):
    out_ref[...] = dot(onehot(order_ref[...]), rows_ref[...]).astype(out_ref.dtype)


def unpick_rows(rows, order, dtype):
    return pl.pallas_call(
        unpick_kernel,
        out_shape=jax.ShapeDtypeStruct(rows.shape, dtype),
        in_specs=[vspec(), vspec()],
        out_specs=vspec(),
        compiler_params=params(),
        name="unpick_rows",
    )(rows, order)


def project_kernel(
    info, arrived_ref, place_ref, w_ref, up_ref, hist_ref, gate_ref, slope_ref, buf_ref, normed_ref
):
    step = pl.program_id(0)
    odd = info[1] % 2

    @pl.when(step == 0)
    def _():
        history = dot_tn(onehot(place_ref[...]), arrived_ref[...])
        hist_ref[...] = history.astype(BF16)
        normed_ref[...] = normalize(history)[0].astype(BF16)

    preact = dot(normed_ref[...], w_ref[...])
    sigmoid = jax.nn.sigmoid(preact)
    act = preact * sigmoid
    slope_ref[...] = (sigmoid * (1.0 + preact * (1.0 - sigmoid))).astype(BF16)
    act = act.astype(BF16)

    def lay(part, block):
        for half in range(2):
            for head in range(HEADS):
                buf_ref[2 * head + (half ^ odd), part] = block[
                    half * HALF : (half + 1) * HALF, head * HEAD_DIM : (head + 1) * HEAD_DIM
                ]

    @pl.when(step == 0)
    def _():
        gate_ref[...] = act
        lay(3, (up_ref[...] * act.astype(F32)).astype(BF16))

    @pl.when(step == 1)
    def _():
        lay(1, act)

    @pl.when(step == 2)
    def _():
        lay(2, act)

    @pl.when(step == 3)
    def _():
        lay(0, act)


def project(info, arrived, place, w_in, upstream):
    rows, width = arrived.shape

    def whole(*shape):
        return pl.BlockSpec(shape, lambda j, *_: (0,) * len(shape))

    return pl.pallas_call(
        project_kernel,
        grid_spec=pltpu.PrefetchScalarGridSpec(
            num_scalar_prefetch=1,
            grid=(4,),
            in_specs=[
                whole(rows, width),
                whole(1, rows),
                pl.BlockSpec((width, width), lambda j, *_: (0, j)),
                whole(rows, width),
            ],
            out_specs=[
                whole(rows, width),
                whole(rows, width),
                pl.BlockSpec((rows, width), lambda j, *_: (0, j)),
                whole(GROUP, 4, HALF, HEAD_DIM),
            ],
            scratch_shapes=[VMEM((rows, width), BF16)],
        ),
        out_shape=[
            jax.ShapeDtypeStruct((rows, width), BF16),
            jax.ShapeDtypeStruct((rows, width), BF16),
            jax.ShapeDtypeStruct((rows, 4 * width), BF16),
            jax.ShapeDtypeStruct((GROUP, 4, HALF, HEAD_DIM), BF16),
        ],
        compiler_params=params(),
        name="project",
    )(info, arrived, place, w_in, upstream)


def lay_keys(info, mine_ref, other_ref, part, out_ref):
    length, core = info[0], info[2]
    spots = lax.broadcasted_iota(jnp.int32, (HALF, HEAD_DIM), 0)
    for owner in range(GROUP):
        for source, half in ((mine_ref, core ^ (owner & 1)), (other_ref, 1 - (core ^ (owner & 1)))):
            start = pl.multiple_of(owner * 2 * HALF + half * HALF, HALF)
            rows = source[owner, part].astype(F32)
            rows = jnp.where(spots + start < length, rows, 0.0)
            out_ref[pl.ds(start, HALF), :] = rows.astype(BF16)


def half_position(core, index):
    chunk = index >> 7
    return chunk * 2 * HALF + (core ^ (chunk & 1)) * HALF + (index & (HALF - 1))


def forward_kernel(info, mine_ref, other_ref, att_ref, stats_ref, key_ref, value_ref, sum_ref):
    query_tile, key_tile = TILE * HALF, TILE * 2 * HALF
    tiles = GROUP // TILE
    length, core = info[0], info[2]
    lay_keys(info, mine_ref, other_ref, 0, key_ref)
    lay_keys(info, mine_ref, other_ref, 1, value_ref)
    scale = 0.5 / math.sqrt(HEAD_DIM)
    live = (length + key_tile - 1) // key_tile

    def term(queries, j, masked):
        keys = pl.ds(pl.multiple_of(j * key_tile, key_tile), key_tile)
        half_scores = dot_nt(queries, key_ref[keys, :]) * scale
        weights = half_scores * jnp.tanh(half_scores) + half_scores
        if masked:
            query_spot = half_position(
                core, lax.broadcasted_iota(jnp.int32, (query_tile, key_tile), 0)
            )
            key_spot = lax.broadcasted_iota(jnp.int32, (query_tile, key_tile), 1)
            weights = jnp.where(key_spot <= query_spot, weights, 0.0)
        return dot(weights.astype(BF16), value_ref[keys, :])

    def query_turn(i, carry):
        queries = mine_ref[pl.ds(i * TILE, TILE), 2].reshape(query_tile, HEAD_DIM)
        sum_ref[...] = jnp.zeros_like(sum_ref)

        def key_turn(j, carry):
            sum_ref[...] += term(queries, j, False)
            return carry

        lax.fori_loop(0, jnp.minimum(i, live), key_turn, 0)

        @pl.when(i < live)
        def _():
            sum_ref[...] += term(queries, i, True)

        att = sum_ref[...].T
        up = (
            mine_ref[pl.ds(i * TILE, TILE), 3].reshape(query_tile, HEAD_DIM).astype(F32).T
        )
        where = pl.ds(pl.multiple_of(i * query_tile, query_tile), query_tile)
        att_ref[:, where] = att
        mean = jnp.mean(att, axis=0, keepdims=True)
        centred = att - mean
        stats = jnp.concatenate(
            [
                mean,
                jnp.sum(centred * centred, axis=0, keepdims=True),
                jnp.sum(up, axis=0, keepdims=True),
                jnp.sum(up * centred, axis=0, keepdims=True),
            ],
            axis=0,
        )
        for head in range(HEADS):
            stats_ref[head, :, where] = stats
        return carry

    lax.fori_loop(0, tiles, query_turn, 0)


def forward(info, mine, other):
    half = GROUP * HALF
    return pl.pallas_call(
        forward_kernel,
        out_shape=[
            jax.ShapeDtypeStruct((HEAD_DIM, half), F32),
            jax.ShapeDtypeStruct((HEADS, 4, half), F32),
        ],
        in_specs=[sspec(), vspec(), vspec()],
        out_specs=[vspec(), vspec()],
        scratch_shapes=[
            VMEM((2 * half, HEAD_DIM), BF16),
            VMEM((2 * half, HEAD_DIM), BF16),
            VMEM((TILE * HALF, HEAD_DIM), F32),
        ],
        compiler_params=params(),
        name="forward",
    )(info, mine, other)


def backward_kernel(
    info,
    mine_ref,
    other_ref,
    att_ref,
    stats_ref,
    out_ref,
    own_ref,
    sib_ref,
    key_ref,
    key_t_ref,
    value_ref,
    query_t_ref,
    grad_ref,
    grad_t_ref,
    dq_ref,
    dk_ref,
    dv_ref,
):
    query_tile, key_tile = TILE * HALF, TILE * 2 * HALF
    tiles = GROUP // TILE
    length, core = info[0], info[2]
    width = HEADS * HEAD_DIM
    lay_keys(info, mine_ref, other_ref, 0, key_ref)
    lay_keys(info, mine_ref, other_ref, 1, value_ref)
    scale = 0.5 / math.sqrt(HEAD_DIM)
    live = (length + key_tile - 1) // key_tile

    stat = [[stats_ref[head, s : s + 1, :] for s in range(4)] for head in range(HEADS)]
    mean = sum(row[0] for row in stat) * (1.0 / HEADS)
    square = sum(row[1] + HEAD_DIM * (row[0] - mean) * (row[0] - mean) for row in stat)
    inverse = lax.rsqrt(square * (1.0 / width) + EPSILON)
    up_mean = sum(row[2] for row in stat) * (1.0 / width)
    cross = sum(row[3] + (row[0] - mean) * row[2] for row in stat) * inverse * (1.0 / width)

    for chunk in range(GROUP):
        where = slice(chunk * HALF, (chunk + 1) * HALF)
        up = mine_ref[chunk, 3].astype(F32).T
        hat = (att_ref[:, where] - mean[:, where]) * inverse[:, where]
        out_ref[chunk, 3] = hat.T.astype(BF16)
        grad = inverse[:, where] * (up - up_mean[:, where] - hat * cross[:, where])
        grad_t_ref[:, where] = grad.astype(BF16)
        grad_ref[where, :] = grad.T.astype(BF16)
        query_t_ref[:, where] = mine_ref[chunk, 2].astype(F32).T.astype(BF16)
    for block in range(2 * GROUP):
        where = slice(block * HALF, (block + 1) * HALF)
        key_t_ref[:, where] = key_ref[where, :].astype(F32).T.astype(BF16)

    dq_ref[...] = jnp.zeros_like(dq_ref)
    dk_ref[...] = jnp.zeros_like(dk_ref)
    dv_ref[...] = jnp.zeros_like(dv_ref)

    def term(i, j, masked):
        keys = pl.ds(pl.multiple_of(j * key_tile, key_tile), key_tile)
        rows = pl.ds(pl.multiple_of(i * query_tile, query_tile), query_tile)
        half_scores = dot(key_ref[keys, :], query_t_ref[:, rows]) * scale
        grad_weights = dot(value_ref[keys, :], grad_t_ref[:, rows])
        plus = jnp.tanh(half_scores) + 1.0
        weights = half_scores * plus
        slope = plus * ((half_scores + half_scores + 1.0) - weights)
        grad_scores = grad_weights * slope
        if masked:
            query_spot = half_position(
                core, lax.broadcasted_iota(jnp.int32, (key_tile, query_tile), 1)
            )
            key_spot = lax.broadcasted_iota(jnp.int32, (key_tile, query_tile), 0)
            allowed = key_spot <= query_spot
            weights = jnp.where(allowed, weights, 0.0)
            grad_scores = jnp.where(allowed, grad_scores, 0.0)
        weights = weights.astype(BF16)
        grad_scores = grad_scores.astype(BF16)
        dv_ref[keys, :] += dot(weights, grad_ref[rows, :])
        queries = mine_ref[pl.ds(i * TILE, TILE), 2].reshape(query_tile, HEAD_DIM)
        dk_ref[keys, :] += dot(grad_scores, queries)
        dq_ref[:, rows] += dot(key_t_ref[:, keys], grad_scores)

    def key_turn(j, carry):
        def query_turn(i, carry):
            term(i, j, False)
            return carry

        term(j, j, True)
        lax.fori_loop(j + 1, tiles, query_turn, 0)
        return carry

    lax.fori_loop(0, live, key_turn, 0)

    for owner in range(GROUP):
        where = slice(owner * HALF, (owner + 1) * HALF)
        out_ref[owner, 2] = (dq_ref[:, where].T * scale).astype(BF16)
        half = core ^ (owner & 1)
        kept = pl.ds(pl.multiple_of(owner * 2 * HALF + half * HALF, HALF), HALF)
        sent = pl.ds(pl.multiple_of(owner * 2 * HALF + (1 - half) * HALF, HALF), HALF)
        own_ref[owner, 0] = dk_ref[kept, :] * scale
        own_ref[owner, 1] = dv_ref[kept, :]
        sib_ref[owner, 0] = (dk_ref[sent, :] * scale).astype(BF16)
        sib_ref[owner, 1] = dv_ref[sent, :].astype(BF16)


def backward(info, mine, other, att, stats):
    half = GROUP * HALF
    return pl.pallas_call(
        backward_kernel,
        out_shape=[
            jax.ShapeDtypeStruct((GROUP, 4, HALF, HEAD_DIM), BF16),
            jax.ShapeDtypeStruct((GROUP, 2, HALF, HEAD_DIM), F32),
            jax.ShapeDtypeStruct((GROUP, 2, HALF, HEAD_DIM), BF16),
        ],
        in_specs=[sspec(), vspec(), vspec(), vspec(), vspec()],
        out_specs=[vspec(), vspec(), vspec()],
        scratch_shapes=[
            VMEM((2 * half, HEAD_DIM), BF16),
            VMEM((HEAD_DIM, 2 * half), BF16),
            VMEM((2 * half, HEAD_DIM), BF16),
            VMEM((HEAD_DIM, half), BF16),
            VMEM((half, HEAD_DIM), BF16),
            VMEM((HEAD_DIM, half), BF16),
            VMEM((HEAD_DIM, half), F32),
            VMEM((2 * half, HEAD_DIM), F32),
            VMEM((2 * half, HEAD_DIM), F32),
        ],
        compiler_params=params(),
        name="backward",
    )(info, mine, other, att, stats)


def merge_kernel(out_ref, own_ref, sib_ref, done_ref):
    done_ref[:, 0:2] = (own_ref[...] + sib_ref[...].astype(F32)).astype(BF16)
    done_ref[:, 2:4] = out_ref[:, 2:4]


def merge(out, own, sib):
    block = 4
    return pl.pallas_call(
        merge_kernel,
        grid=(GROUP // block,),
        in_specs=[
            pl.BlockSpec((block, 4, HALF, HEAD_DIM), lambda i: (i, 0, 0, 0)),
            pl.BlockSpec((block, 2, HALF, HEAD_DIM), lambda i: (i, 0, 0, 0)),
            pl.BlockSpec((block, 2, HALF, HEAD_DIM), lambda i: (i, 0, 0, 0)),
        ],
        out_specs=pl.BlockSpec((block, 4, HALF, HEAD_DIM), lambda i: (i, 0, 0, 0)),
        out_shape=jax.ShapeDtypeStruct(out.shape, out.dtype),
        compiler_params=params(),
        name="merge",
    )(out, own, sib)


def finish_kernel(
    info,
    back_ref,
    gate_ref,
    slope_ref,
    hist_ref,
    up_ref,
    cot_ref,
    place_ref,
    w_in_ref,
    w_out_ref,
    mixed_ref,
    rows_ref,
    part_ref,
    total_ref,
):
    step = pl.program_id(0)
    odd = info[1] % 2

    def gather(part):
        for half in range(2):
            for head in range(HEADS):
                part_ref[
                    half * HALF : (half + 1) * HALF, head * HEAD_DIM : (head + 1) * HEAD_DIM
                ] = back_ref[2 * head + (half ^ odd), part]
        return part_ref[...].astype(F32)

    def add(grad):
        pre = (grad * slope_ref[...].astype(F32)).astype(BF16)
        return dot_nt(pre, w_in_ref[...])

    @pl.when(step == 0)
    def _():
        hat = gather(3)
        gated = (hat * gate_ref[...].astype(F32)).astype(BF16)
        mixed_ref[...] = (hist_ref[...].astype(F32) + dot(gated, w_out_ref[...])).astype(BF16)
        total_ref[...] = add(up_ref[...] * hat)

    for s, part in ((1, 1), (2, 2), (3, 0)):

        @pl.when(step == s)
        def _():
            total_ref[...] += add(gather(part))

    @pl.when(step == 3)
    def _():
        hat, inverse = normalize(hist_ref[...].astype(F32))
        grad = total_ref[...]
        grad = inverse * (grad - row_mean(grad) - hat * row_mean(grad * hat))
        grad = (grad + cot_ref[...].astype(F32)).astype(BF16)
        rows_ref[...] = dot(onehot(place_ref[...]), grad).astype(BF16)


def finish(info, back, gate, slope, history, upstream, cotangent, place, w_in, w_out):
    rows, width = history.shape

    def whole(*shape):
        return pl.BlockSpec(shape, lambda j, *_: (0,) * len(shape))

    return pl.pallas_call(
        finish_kernel,
        grid_spec=pltpu.PrefetchScalarGridSpec(
            num_scalar_prefetch=1,
            grid=(4,),
            in_specs=[
                whole(GROUP, 4, HALF, HEAD_DIM),
                whole(rows, width),
                pl.BlockSpec((rows, width), lambda j, *_: (0, j)),
                whole(rows, width),
                whole(rows, width),
                whole(rows, width),
                whole(1, rows),
                pl.BlockSpec((width, width), lambda j, *_: (0, j)),
                whole(width, width),
            ],
            out_specs=[whole(rows, width), whole(rows, width)],
            scratch_shapes=[VMEM((rows, width), BF16), VMEM((rows, width), F32)],
        ),
        out_shape=[
            jax.ShapeDtypeStruct((rows, width), BF16),
            jax.ShapeDtypeStruct((rows, width), BF16),
        ],
        compiler_params=params(),
        name="finish",
    )(info, back, gate, slope, history, upstream, cotangent, place, w_in, w_out)


def body(log_rows, send_order, place, hist_len, w_in, w_out, cotangent):
    rows, width = log_rows.shape
    seq_size = lax.axis_size("seq")
    seq_index = lax.axis_index("seq")
    spot = seq_index % GROUP
    length = jnp.take(hist_len[0], seq_index // GROUP)
    info = jnp.stack([length, spot, spot % 2]).astype(jnp.int32)
    groups = [list(range(g, g + GROUP)) for g in range(0, seq_size, GROUP)]
    same_core = [list(range(g + c, g + GROUP, 2)) for g in range(0, seq_size, GROUP) for c in (0, 1)]
    swap = [(i, i ^ 1) for i in range(seq_size)]

    def to_all(block):
        block = block.reshape(rows // 2, 2, width)
        block = lax.all_to_all(block, ("dp", "seq"), split_axis=0, concat_axis=0, tiled=True)
        return block.reshape(rows, width)

    def to_group(block, members):
        return lax.all_to_all(
            block, "seq", split_axis=0, concat_axis=0, tiled=True, axis_index_groups=members
        )

    upstream = jnp.dot(cotangent, w_out.T, preferred_element_type=F32)
    arrived = to_all(pick_rows(log_rows, send_order))
    history, gate, slope, block = project(info, arrived, place, w_in, upstream)
    mine = to_group(block, groups)
    other = lax.ppermute(mine[:, :2], "seq", swap)
    att, stats = forward(info, mine, other)
    stats = to_group(stats, same_core)
    out, own, sib = backward(info, mine, other, att, stats)
    sib = lax.ppermute(sib, "seq", swap)
    back = to_group(merge(out, own, sib), groups)
    mixed, grads = finish(
        info, back, gate, slope, history, upstream, cotangent, place, w_in, w_out
    )
    log_grad = unpick_rows(to_all(grads), send_order, F32)
    return (mixed, log_grad)


def solution(mesh):
    rows = P(("dp", "seq"), None)
    return jax.shard_map(
        body,
        mesh=mesh,
        in_specs=(rows, rows, rows, P("dp", None), P(), P(), rows),
        out_specs=(rows, rows),
        check_vma=False,
    )
```

time: 1200 us -> 191 us (0.16)
  waiting for transfers between devices: 465 us -> 14.4 us
  starting transfers between devices: 409 us -> 13.4 us
  local copies, waits for them, and re-layouts: 146 us -> 4.1 us
  other arithmetic: 116 us -> 0.08 us
  blocking collectives: 0 us -> 88.8 us
  Pallas kernels: 0 us -> 65.7 us
  matrix products: 56 us -> 2.35 us
    ppermute x45 -> x2, waiting for transfers between devices: 447 us -> 4.57 us  [the longest x1 2.29 us: body(): sib = lax.ppermute(sib, 'seq', swap)]
    all_to_all x2 -> x1, starting transfers between devices: 263 us -> 11.5 us  [to_all(): lax.all_to_all(block, ('dp', 'seq'), split_axis=0, concat_axis=0, tiled=T...]
    ppermute x45 -> x2, starting transfers between devices: 146 us -> 1.95 us  [the longest x1 1.14 us: body(): other = lax.ppermute(mine[:, :2], 'seq', swap)]
    convert_element_type x31 -> x0, other arithmetic: 94.3 us -> none  [the longest x15 51.8 us: partial_turn(): (acc + stored_term(offset)).astype(jnp.bfloat16)]
    all_to_all x0 -> x4, blocking collectives: none -> 88.8 us  [the longest x3 70.9 us: to_group(): lax.all_to_all(block, 'seq', split_axis=0, concat_axis=0, tiled=True, axi...]
    pallas_call x0 -> x7, Pallas kernels: none -> 65.7 us  [the longest x1 26.3 us: backward(): pl.pallas_call(backward_kernel, out_shape=[jax.ShapeDtypeStruct((GROUP, 4...]
    dot_general x16 -> x1, matrix products: 56 us -> 2.35 us  [body(): upstream = jnp.dot(cotangent, w_out.T, preferred_element_type=F32)]
    while x31 -> x0, local copies, waits for them, and re-layouts: 26.7 us -> none
  transfers between devices with their start and end apart: 47 -> 3, of which waited for: 43 -> 3; matrix products, arithmetic and copies ran while one was open for 1% -> 2% of each run, Pallas kernels for 0% -> 0%
where the time goes in v1:
time: 191 us; the launch traced here: 190 us
  blocking collectives  88.8 us (46%)
  Pallas kernels  65.7 us (34%)
  waiting for transfers between devices  14.4 us (8%)
  starting transfers between devices  13.4 us (7%)
  local copies, waits for them, and re-layouts  4.1 us (2%)
  matrix products  2.35 us (1%)
    all_to_all x3, blocking collectives, to_group(): lax.all_to_all(block, 'seq', split_axis=0, concat_axis=0, tiled=True, axi...  70.9 us
    pallas_call x1, Pallas kernels, backward(): pl.pallas_call(backward_kernel, out_shape=[jax.ShapeDtypeStruct((GROUP, 4...  26.3 us
    all_to_all x1, blocking collectives, to_all(): lax.all_to_all(block, ('dp', 'seq'), split_axis=0, concat_axis=0, tiled=T...  17.9 us
    pallas_call x1, Pallas kernels, forward(): pl.pallas_call(forward_kernel, out_shape=[jax.ShapeDtypeStruct((HEAD_DIM,...  17.2 us
    all_to_all x1, starting transfers between devices, to_all(): lax.all_to_all(block, ('dp', 'seq'), split_axis=0, concat_axis=0, tiled=T...  11.5 us
    all_to_all x1, waiting for transfers between devices, to_all(): lax.all_to_all(block, ('dp', 'seq'), split_axis=0, concat_axis=0, tiled=T...  9.78 us
    pallas_call x1, Pallas kernels, finish(): pl.pallas_call(finish_kernel, grid_spec=pltpu.PrefetchScalarGridSpec(num_...  9.45 us
    pallas_call x1, Pallas kernels, project(): pl.pallas_call(project_kernel, grid_spec=pltpu.PrefetchScalarGridSpec(num...  8.78 us
  transfers between devices with their start and end apart: 3, of which 3 were waited for; matrix products, arithmetic and copies ran while one was open for 2% of the time, Pallas kernels for 0%

profile of v1, /device:TPU:1, one launch (start us, length us, event | category | flops | bytes accessed | tf_op | source)
XLA Modules:
  0.0 190.3 jit_solution(12197859742205997206)
XLA Ops:
  0.6 0.0 copy-start
  0.6 0.0 copy-start.3
  0.7 0.0 copy-start.4
  0.7 1.1 copy-done.4
  1.8 0.7 copy-done.5
  2.4 0.3 pick_rows.1
  2.8 1.0 reshape.17
  3.8 11.5 %all-to-all-start = ((bf16[128,2,1024]{2,1,0:T(2,128)(2,1)}), bf16[128,2,1024]{2,1,0:T(2,128)(2,1)S(1)}, u32[]{:S(2)}, u32[]{:S(2)}) async-start(bf16[128,2,1024]{2,1,0:T(2,128)(2,1)} %reshape.17), calls=%async_computation | async-start | bytes 1048576 | tf_op jit(solution)/shard_map/all_to_all | solution.py:515
  15.3 0.0 copy-done
  15.3 0.6 constant_dynamic-slice_fusion
  16.6 0.1 pad_add_fusion.info
  16.6 2.3 %fusion.up_ref = f32[256,1024]{1,0:T(8,128)S(1)} fusion(bf16[256,1024]{1,0:T(8,128)(2,1)S(1)} %copy-done.3, bf16[1024,1024]{1,0:T(8,128)(2,1)} %w_out_ref.1), kind=kOutput, calls=%fused_computation.2 | convolution fusion | flops 536870912 | bytes 3670016 | tf_op jit(solution)/shard_map/dot_general | solution.py:523
  19.0 9.8 %all-to-all-done = bf16[128,2,1024]{2,1,0:T(2,128)(2,1)S(1)} async-done(((bf16[128,2,1024]{2,1,0:T(2,128)(2,1)}), bf16[128,2,1024]{2,1,0:T(2,128)(2,1)S(1)}, u32[]{:S(2)}, u32[]{:S(2)}) %all-to-all-start) | async-done | bytes 524320 | tf_op jit(solution)/shard_map/all_to_all | solution.py:515
  28.8 0.2 reshape.18.arrived_ref
  29.0 8.8 %project.1 = (bf16[256,1024]{1,0:T(8,128)(2,1)S(1)}, bf16[256,1024]{1,0:T(8,128)(2,1)S(1)}, bf16[256,4096]{1,0:T(8,128)(2,1)S(1)}, bf16[16,4,128,128]{3,2,1,0:T(8,128)(2,1)}) custom-call(s32[3]{0:T(128)S(1)} %pad_add_fusion.info, bf16[256,1024]{1,0:T(8,128)(2,1)S(1)} %reshape.18.arrived_ref, s32[1,256]{1,0:T(1,128)S(1)} %copy-done.7, ...), custom_call_target="tpu_custom_call" | custom-call | tf_op jit(solution)/shard_map/project/pallas_call | solution.py:142
  37.8 31.4 %all_to_all.25.mine_ref = bf16[16,4,128,128]{3,2,1,0:T(8,128)(2,1)S(1)} all-to-all(bf16[16,4,128,128]{3,2,1,0:T(8,128)(2,1)} %get-tuple-element.13), channel_id=1, replica_groups={{0,1,2,3,4,5,6,7,8,9,10,11,12,13,14,15},{16,17,18,19,20,21,22,23,24,25,..., dimensions={0} | all-to-all | bytes 4194304 | tf_op jit(solution)/shard_map/all_to_all | solution.py:519
  69.2 0.0 copy-done.2
  69.2 0.1 slice.9
  69.3 1.1 collective-permute-start
  70.5 2.3 %collective-permute-done.other_ref = bf16[16,2,128,128]{3,2,1,0:T(8,128)(2,1)S(1)} collective-permute-done((bf16[16,2,128,128]{3,2,1,0:T(8,128)(2,1)S(1)}, bf16[16,2,128,128]{3,2,1,0:T(8,128)(2,1)S(1)}, u32[]{:S(2)}, u32[]{:S(2)}) %collective-permute-start) | collective-permute-done | bytes 1048608 | tf_op jit(solution)/shard_map/ppermute | solution.py:527
  72.7 17.2 %forward.1 = (f32[128,2048]{1,0:T(8,128)S(1)}, f32[8,4,2048]{2,1,0:T(4,128)S(1)}) custom-call(s32[3]{0:T(128)S(1)} %pad_add_fusion.info, bf16[16,4,128,128]{3,2,1,0:T(8,128)(2,1)S(1)} %all_to_all.25.mine_ref, bf16[16,2,128,128]{3,2,1,0:T(8,128)(2,1)S(1)} %collective-permute-done.other_ref), custom_call_target="tpu_custom_call" | custom-call | tf_op jit(solution)/shard_map/forward/pallas_call | solution.py:249
  90.0 9.8 %all_to_all.26.stats_ref = f32[8,4,2048]{2,1,0:T(4,128)S(1)} all-to-all(f32[8,4,2048]{2,1,0:T(4,128)S(1)} %get-tuple-element.15), channel_id=1, replica_groups={{0,2,4,6,8,10,12,14},{1,3,5,7,9,11,13,15},{16,18,20,22,24,26,28,30},{17..., dimensions={0} | all-to-all | bytes 524288 | tf_op jit(solution)/shard_map/all_to_all | solution.py:519
  99.8 26.3 %backward.1 = (bf16[16,4,128,128]{3,2,1,0:T(8,128)(2,1)S(1)}, f32[16,2,128,128]{3,2,1,0:T(8,128)}, bf16[16,2,128,128]{3,2,1,0:T(8,128)(2,1)S(1)}) custom-call(s32[3]{0:T(128)S(1)} %pad_add_fusion.info, bf16[16,4,128,128]{3,2,1,0:T(8,128)(2,1)} %copy-done.1, bf16[16,2,128,128]{3,2,1,0:T(8,128)(2,1)S(1)} %collective-permute-done.other_ref, ...), custom_call_target="tpu_custom_call" | custom-call | tf_op jit(solution)/shard_map/backward/pallas_call | solution.py:368
  126.1 0.8 collective-permute-start.1
  126.9 2.3 %collective-permute-done.1.sib_ref = bf16[16,2,128,128]{3,2,1,0:T(8,128)(2,1)S(1)} collective-permute-done((bf16[16,2,128,128]{3,2,1,0:T(8,128)(2,1)S(1)}, bf16[16,2,128,128]{3,2,1,0:T(8,128)(2,1)S(1)}, u32[]{:S(2)}, u32[]{:S(2)}) %collective-permute-start.1) | collective-permute-done | bytes 1048608 | tf_op jit(solution)/shard_map/ppermute | solution.py:531
  129.2 2.4 %merge.1 = bf16[16,4,128,128]{3,2,1,0:T(8,128)(2,1)S(1)} custom-call(bf16[16,4,128,128]{3,2,1,0:T(8,128)(2,1)S(1)} %get-tuple-element.16.out_ref, f32[16,2,128,128]{3,2,1,0:T(8,128)} %get-tuple-element.17.own_ref, bf16[16,2,128,128]{3,2,1,0:T(8,128)(2,1)S(1)} %collective-permute-done.1.sib_ref), custom_call_target="tpu_custom_call" | custom-call | tf_op jit(solution)/shard_map/merge/pallas_call | solution.py:400
  131.6 29.6 %all_to_all.27.back_ref = bf16[16,4,128,128]{3,2,1,0:T(8,128)(2,1)S(1)} all-to-all(bf16[16,4,128,128]{3,2,1,0:T(8,128)(2,1)S(1)} %merge.1), channel_id=1, replica_groups={{0,1,2,3,4,5,6,7,8,9,10,11,12,13,14,15},{16,17,18,19,20,21,22,23,24,25,..., dimensions={0} | all-to-all | bytes 4194304 | tf_op jit(solution)/shard_map/all_to_all | solution.py:519
  161.3 9.4 %finish.1 = (bf16[256,1024]{1,0:T(8,128)(2,1)}, bf16[256,1024]{1,0:T(8,128)(2,1)S(1)}) custom-call(s32[3]{0:T(128)S(1)} %pad_add_fusion.info, bf16[16,4,128,128]{3,2,1,0:T(8,128)(2,1)S(1)} %all_to_all.27.back_ref, bf16[256,1024]{1,0:T(8,128)(2,1)S(1)} %get-tuple-element.19.gate_ref, bf16[256,4096]{1,0:T(8,128)(2,1)} %copy-done.2, ...), custom_call_target="tpu_custom_call" | custom-call | tf_op jit(solution)/shard_map/finish/pallas_call | solution.py:474
  170.7 0.2 reshape.19
  170.9 17.9 %all_to_all.28 = bf16[128,2,1024]{2,1,0:T(2,128)(2,1)S(1)} all-to-all(bf16[128,2,1024]{2,1,0:T(2,128)(2,1)S(1)} %reshape.19), channel_id=1, replica_groups=mesh['dp'=4,'seq'=32] {'dp','seq'}, dimensions={0} | all-to-all | bytes 1048576 | tf_op jit(solution)/shard_map/all_to_all | solution.py:515
  188.8 0.2 reshape.20.rows_ref
  189.1 1.3 unpick_rows.1
  (9 shorter events, 0.0 us)
Async XLA Ops:
  0.6 14.7 %copy-start = (s32[1,2]{1,0:T(1,128)S(1)}, s32[1,2]{1,0:T(1,128)}, u32[]{:S(2)}) copy-start(s32[1,2]{1,0:T(1,128)} %param.10) | copy-start | bytes 28
  0.6 16.0 %copy-start.3 = (bf16[256,1024]{1,0:T(8,128)(2,1)S(1)}, bf16[256,1024]{1,0:T(8,128)(2,1)}, u32[]{:S(2)}) copy-start(bf16[256,1024]{1,0:T(8,128)(2,1)} %cot_ref.1) | copy-start | bytes 1572868
  0.7 1.1 copy-start.4
  1.8 0.7 copy-start.5
  3.8 25.0 %all-to-all-start = ((bf16[128,2,1024]{2,1,0:T(2,128)(2,1)}), bf16[128,2,1024]{2,1,0:T(2,128)(2,1)S(1)}, u32[]{:S(2)}, u32[]{:S(2)}) async-start(bf16[128,2,1024]{2,1,0:T(2,128)(2,1)} %reshape.17), calls=%async_computation | async-start | bytes 1048576 | tf_op jit(solution)/shard_map/all_to_all | solution.py:515
  16.6 12.3 %copy-start.7 = (s32[1,256]{1,0:T(1,128)S(1)}, s32[1,256]{1,0:T(1,128)}, u32[]{:S(2)}) copy-start(s32[1,256]{1,0:T(1,128)} %place_ref.3) | copy-start | bytes 3076
  37.8 31.4 %copy-start.2 = (bf16[256,4096]{1,0:T(8,128)(2,1)}, bf16[256,4096]{1,0:T(8,128)(2,1)S(1)}, u32[]{:S(2)}) copy-start(bf16[256,4096]{1,0:T(8,128)(2,1)S(1)} %get-tuple-element.20.slope_ref) | copy-start | bytes 6291460
  69.2 20.8 %copy-start.1 = (bf16[16,4,128,128]{3,2,1,0:T(8,128)(2,1)}, bf16[16,4,128,128]{3,2,1,0:T(8,128)(2,1)S(1)}, u32[]{:S(2)}) copy-start(bf16[16,4,128,128]{3,2,1,0:T(8,128)(2,1)S(1)} %all_to_all.25.mine_ref) | copy-start | bytes 6291460
  69.3 3.4 %collective-permute-start = (bf16[16,2,128,128]{3,2,1,0:T(8,128)(2,1)S(1)}, bf16[16,2,128,128]{3,2,1,0:T(8,128)(2,1)S(1)}, u32[]{:S(2)}, u32[]{:S(2)}) collective-permute-start(bf16[16,2,128,128]{3,2,1,0:T(8,128)(2,1)S(1)} %slice.9), channel_id=1, source_target_pairs={{0,1},{1,0},{2,3},{3,2},{4,5},{5,4},{6,7},{7,6},{8,9},{9,8},{10,11... | collective-permute-start | bytes 3145736 | tf_op jit(solution)/shard_map/ppermute | solution.py:527
  126.1 3.1 %collective-permute-start.1 = (bf16[16,2,128,128]{3,2,1,0:T(8,128)(2,1)S(1)}, bf16[16,2,128,128]{3,2,1,0:T(8,128)(2,1)S(1)}, u32[]{:S(2)}, u32[]{:S(2)}) collective-permute-start(bf16[16,2,128,128]{3,2,1,0:T(8,128)(2,1)S(1)} %get-tuple-element.18), channel_id=1, source_target_pairs={{0,1},{1,0},{2,3},{3,2},{4,5},{5,4},{6,7},{7,6},{8,9},{9,8},{10,11... | collective-permute-start | bytes 3145736 | tf_op jit(solution)/shard_map/ppermute | solution.py:531
  170.7 18.3 %copy-start.6 = (s32[1,256]{1,0:T(1,128)S(1)}, s32[1,256]{1,0:T(1,128)}, u32[]{:S(2)}) copy-start(s32[1,256]{1,0:T(1,128)} %order_ref.3) | copy-start | bytes 3076

commit v2 on v1

v2 whole, which is shorter than its diff:
```python
import functools
import math

import jax
import jax.numpy as jnp
from jax import lax
from jax.experimental import pallas as pl
from jax.experimental.pallas import tpu as pltpu
from jax.sharding import PartitionSpec as P

HEADS = 8
GROUP = 16
EPSILON = 1e-05
CHIPS = 8
ROWS = 256
HEAD_DIM = 128
BF16 = jnp.bfloat16
F32 = jnp.float32
VMEM = pltpu.VMEM
SMEM = pltpu.SMEM


def params(limit=48 * 1024 * 1024, **kw):
    return pltpu.CompilerParams(vmem_limit_bytes=limit, **kw)


def vspec():
    return pl.BlockSpec(memory_space=VMEM)


def sspec():
    return pl.BlockSpec(memory_space=SMEM)


def dot(a, b):
    return jnp.dot(a, b, preferred_element_type=F32)


def dot_nt(a, b):
    return lax.dot_general(a, b, (((1,), (1,)), ((), ())), preferred_element_type=F32)


def dot_tn(a, b):
    return lax.dot_general(a, b, (((0,), (0,)), ((), ())), preferred_element_type=F32)


def onehot(order):
    count = order.shape[1]
    spots = lax.broadcasted_iota(jnp.int32, (count, count), 0)
    return jnp.where(spots == order, 1.0, 0.0).astype(BF16)


def row_mean(x):
    return jnp.mean(x, axis=-1, keepdims=True)


def normalize(inputs):
    centred = inputs - row_mean(inputs)
    inverse = lax.rsqrt(row_mean(centred * centred) + EPSILON)
    return centred * inverse, inverse


def pick_kernel(rows_ref, order_ref, out_ref):
    out_ref[...] = dot_tn(onehot(order_ref[...]), rows_ref[...]).astype(out_ref.dtype)


def pick_rows(rows, order):
    return pl.pallas_call(
        pick_kernel,
        out_shape=jax.ShapeDtypeStruct(rows.shape, rows.dtype),
        in_specs=[vspec(), vspec()],
        out_specs=vspec(),
        compiler_params=params(),
        name="pick_rows",
    )(rows, order)


def unpick_kernel(rows_ref, order_ref, out_ref):
    out_ref[...] = dot(onehot(order_ref[...]), rows_ref[...]).astype(out_ref.dtype)


def unpick_rows(rows, order, dtype):
    return pl.pallas_call(
        unpick_kernel,
        out_shape=jax.ShapeDtypeStruct(rows.shape, dtype),
        in_specs=[vspec(), vspec()],
        out_specs=vspec(),
        compiler_params=params(),
        name="unpick_rows",
    )(rows, order)


def project_kernel(
    arrived_ref, place_ref, w_ref, up_ref, hist_ref, gate_ref, slope_ref, buf_ref, normed_ref
):
    step = pl.program_id(0)

    @pl.when(step == 0)
    def _():
        history = dot_tn(onehot(place_ref[...]), arrived_ref[...])
        hist_ref[...] = history.astype(BF16)
        normed_ref[...] = normalize(history)[0].astype(BF16)

    preact = dot(normed_ref[...], w_ref[...])
    sigmoid = jnp.tanh(preact * 0.5) * 0.5 + 0.5
    act = preact * sigmoid
    slope_ref[...] = (sigmoid + act - act * sigmoid).astype(BF16)
    act = act.astype(BF16)

    def lay(part, block):
        for head in range(HEADS):
            buf_ref[head, part] = block[:, head * HEAD_DIM : (head + 1) * HEAD_DIM]

    @pl.when(step == 0)
    def _():
        gate_ref[...] = act
        lay(3, (up_ref[...] * act.astype(F32)).astype(BF16))

    @pl.when(step == 1)
    def _():
        lay(1, act)

    @pl.when(step == 2)
    def _():
        lay(2, act)

    @pl.when(step == 3)
    def _():
        lay(0, act)


def project(arrived, place, w_in, upstream):
    rows, width = arrived.shape

    def whole(*shape):
        return pl.BlockSpec(shape, lambda j, *_: (0,) * len(shape))

    return pl.pallas_call(
        project_kernel,
        grid_spec=pltpu.PrefetchScalarGridSpec(
            num_scalar_prefetch=0,
            grid=(4,),
            in_specs=[
                whole(rows, width),
                whole(1, rows),
                pl.BlockSpec((width, width), lambda j, *_: (0, j)),
                whole(rows, width),
            ],
            out_specs=[
                whole(rows, width),
                whole(rows, width),
                pl.BlockSpec((rows, width), lambda j, *_: (0, j)),
                whole(CHIPS, 4, ROWS, HEAD_DIM),
            ],
            scratch_shapes=[VMEM((rows, width), BF16)],
        ),
        out_shape=[
            jax.ShapeDtypeStruct((rows, width), BF16),
            jax.ShapeDtypeStruct((rows, width), BF16),
            jax.ShapeDtypeStruct((rows, 4 * width), BF16),
            jax.ShapeDtypeStruct((CHIPS, 4, ROWS, HEAD_DIM), BF16),
        ],
        compiler_params=params(),
        name="project",
    )(arrived, place, w_in, upstream)


def lay_keys(info, mine_ref, other_ref, part, out_ref):
    length, core = info[0], info[2]
    for chip in range(CHIPS):
        for source, side in ((mine_ref, core), (other_ref, 1 - core)):
            start = pl.multiple_of((2 * chip + side) * ROWS, ROWS)
            out_ref[pl.ds(start, ROWS), :] = source[chip, part]

    @pl.when(length < GROUP * ROWS)
    def _():
        def clear(block, carry):
            where = pl.ds(pl.multiple_of(block * ROWS, ROWS), ROWS)
            spots = lax.broadcasted_iota(jnp.int32, (ROWS, HEAD_DIM), 0) + block * ROWS
            rows = jnp.where(spots < length, out_ref[where, :].astype(F32), 0.0)
            out_ref[where, :] = rows.astype(BF16)
            return carry

        lax.fori_loop(length // ROWS, GROUP, clear, 0)


def forward_kernel(info, mine_ref, other_ref, att_ref, stats_ref, key_ref, value_ref, sum_ref):
    many, key_tile = 4, 1024
    query_tile = many * ROWS
    length, core = info[0], info[2]
    lay_keys(info, mine_ref, other_ref, 0, key_ref)
    lay_keys(info, mine_ref, other_ref, 1, value_ref)
    scale = 0.5 / math.sqrt(HEAD_DIM)

    def weigh(queries, keys):
        half_scores = dot_nt(queries, keys) * scale
        return half_scores * jnp.tanh(half_scores) + half_scores

    def whole(queries, start, size):
        keys = pl.ds(pl.multiple_of(start, ROWS), size)
        return dot(weigh(queries, key_ref[keys, :]).astype(BF16), value_ref[keys, :])

    def query_turn(n, carry):
        queries = mine_ref[pl.ds(n * many, many), 2].reshape(query_tile, HEAD_DIM)
        sum_ref[...] = jnp.zeros_like(sum_ref)
        base = n * many * 2 * ROWS

        def key_turn(j, carry):
            sum_ref[...] += whole(queries, j * key_tile, key_tile)
            return carry

        live = (length + key_tile - 1) // key_tile
        lax.fori_loop(0, jnp.minimum(base // key_tile, live), key_turn, 0)

        @pl.when(base < length)
        def _():
            for g in range(many):
                rows = slice(g * ROWS, (g + 1) * ROWS)
                block = mine_ref[n * many + g, 2]
                if g:
                    sum_ref[rows, :] += whole(block, base, 2 * ROWS * g)
                keys = pl.ds(pl.multiple_of(base + 2 * ROWS * g, ROWS), 2 * ROWS)
                query_spot = lax.broadcasted_iota(jnp.int32, (ROWS, 2 * ROWS), 0) + core * ROWS
                key_spot = lax.broadcasted_iota(jnp.int32, (ROWS, 2 * ROWS), 1)
                weights = jnp.where(key_spot <= query_spot, weigh(block, key_ref[keys, :]), 0.0)
                sum_ref[rows, :] += dot(weights.astype(BF16), value_ref[keys, :])

        att = sum_ref[...].T
        up = mine_ref[pl.ds(n * many, many), 3].reshape(query_tile, HEAD_DIM).astype(F32).T
        where = pl.ds(pl.multiple_of(n * query_tile, query_tile), query_tile)
        att_ref[:, where] = att
        mean = jnp.mean(att, axis=0, keepdims=True)
        centred = att - mean
        stats = jnp.concatenate(
            [
                mean,
                jnp.sum(centred * centred, axis=0, keepdims=True),
                jnp.sum(up, axis=0, keepdims=True),
                jnp.sum(up * centred, axis=0, keepdims=True),
            ],
            axis=0,
        )
        for head in range(HEADS):
            stats_ref[head, :, where] = stats
        return carry

    lax.fori_loop(0, CHIPS // many, query_turn, 0)


def forward(info, mine, other):
    half = CHIPS * ROWS
    return pl.pallas_call(
        forward_kernel,
        out_shape=[
            jax.ShapeDtypeStruct((HEAD_DIM, half), F32),
            jax.ShapeDtypeStruct((HEADS, 4, half), F32),
        ],
        in_specs=[sspec(), vspec(), vspec()],
        out_specs=[vspec(), vspec()],
        scratch_shapes=[
            VMEM((2 * half, HEAD_DIM), BF16),
            VMEM((2 * half, HEAD_DIM), BF16),
            VMEM((4 * ROWS, HEAD_DIM), F32),
        ],
        compiler_params=params(),
        name="forward",
    )(info, mine, other)


def backward_kernel(
    info,
    mine_ref,
    other_ref,
    att_ref,
    stats_ref,
    out_ref,
    sib_ref,
    key_ref,
    key_t_ref,
    value_ref,
    query_t_ref,
    grad_ref,
    grad_t_ref,
    dq_ref,
    dk_ref,
    dv_ref,
):
    key_tile = 2 * ROWS
    length, core = info[0], info[2]
    width = HEADS * HEAD_DIM
    lay_keys(info, mine_ref, other_ref, 0, key_ref)
    lay_keys(info, mine_ref, other_ref, 1, value_ref)
    scale = 0.5 / math.sqrt(HEAD_DIM)

    stat = [[stats_ref[head, s : s + 1, :] for s in range(4)] for head in range(HEADS)]
    mean = sum(row[0] for row in stat) * (1.0 / HEADS)
    square = sum(row[1] + HEAD_DIM * (row[0] - mean) * (row[0] - mean) for row in stat)
    inverse = lax.rsqrt(square * (1.0 / width) + EPSILON)
    up_mean = sum(row[2] for row in stat) * (1.0 / width)
    cross = sum(row[3] + (row[0] - mean) * row[2] for row in stat) * inverse * (1.0 / width)

    for chip in range(CHIPS):
        where = slice(chip * ROWS, (chip + 1) * ROWS)
        up = mine_ref[chip, 3].astype(F32).T
        hat = (att_ref[:, where] - mean[:, where]) * inverse[:, where]
        out_ref[chip, 3] = hat.T.astype(BF16)
        grad = inverse[:, where] * (up - up_mean[:, where] - hat * cross[:, where])
        grad_t_ref[:, where] = grad.astype(BF16)
        grad_ref[where, :] = grad.T.astype(BF16)
        query_t_ref[:, where] = mine_ref[chip, 2].T
    for block in range(GROUP):
        where = slice(block * ROWS, (block + 1) * ROWS)
        key_t_ref[:, where] = key_ref[where, :].T

    def pair(j, m):
        keys = slice(key_tile * j, key_tile * (j + 1))
        rows = slice(m * ROWS, (m + 1) * ROWS)
        half_scores = dot(key_ref[keys, :], query_t_ref[:, rows]) * scale
        grad_weights = dot(value_ref[keys, :], grad_t_ref[:, rows])
        plus = jnp.tanh(half_scores) + 1.0
        weights = half_scores * plus
        grad_scores = grad_weights * (plus * ((half_scores + half_scores + 1.0) - weights))
        if m == j:
            query_spot = lax.broadcasted_iota(jnp.int32, (key_tile, ROWS), 1) + core * ROWS
            key_spot = lax.broadcasted_iota(jnp.int32, (key_tile, ROWS), 0)
            allowed = key_spot <= query_spot
            weights = jnp.where(allowed, weights, 0.0)
            grad_scores = jnp.where(allowed, grad_scores, 0.0)
        weights = weights.astype(BF16)
        grad_scores = grad_scores.astype(BF16)
        dv = dot(weights, grad_ref[rows, :])
        dk = dot(grad_scores, mine_ref[m, 2])
        dq = dot(key_t_ref[:, keys], grad_scores)
        if m == j:
            dv_ref[keys, :] = dv
            dk_ref[keys, :] = dk
        else:
            dv_ref[keys, :] += dv
            dk_ref[keys, :] += dk
        if j == 0:
            dq_ref[:, rows] = dq
        else:
            dq_ref[:, rows] += dq

    for j in range(CHIPS):

        @pl.when(key_tile * j < length)
        def _():
            for m in range(j, CHIPS):
                pair(j, m)

        @pl.when(key_tile * j >= length)
        def _():
            keys = slice(key_tile * j, key_tile * (j + 1))
            dv_ref[keys, :] = jnp.zeros((key_tile, HEAD_DIM), F32)
            dk_ref[keys, :] = jnp.zeros((key_tile, HEAD_DIM), F32)

    for chip in range(CHIPS):
        out_ref[chip, 2] = (dq_ref[:, chip * ROWS : (chip + 1) * ROWS].T * scale).astype(BF16)
        kept = pl.ds(pl.multiple_of((2 * chip + core) * ROWS, ROWS), ROWS)
        sent = pl.ds(pl.multiple_of((2 * chip + 1 - core) * ROWS, ROWS), ROWS)
        out_ref[chip, 0] = (dk_ref[kept, :] * scale).astype(BF16)
        out_ref[chip, 1] = dv_ref[kept, :].astype(BF16)
        sib_ref[chip, 0] = (dk_ref[sent, :] * scale).astype(BF16)
        sib_ref[chip, 1] = dv_ref[sent, :].astype(BF16)


def backward(info, mine, other, att, stats):
    half = CHIPS * ROWS
    return pl.pallas_call(
        backward_kernel,
        out_shape=[
            jax.ShapeDtypeStruct((CHIPS, 4, ROWS, HEAD_DIM), BF16),
            jax.ShapeDtypeStruct((CHIPS, 2, ROWS, HEAD_DIM), BF16),
        ],
        in_specs=[sspec(), vspec(), vspec(), vspec(), vspec()],
        out_specs=[vspec(), vspec()],
        scratch_shapes=[
            VMEM((2 * half, HEAD_DIM), BF16),
            VMEM((HEAD_DIM, 2 * half), BF16),
            VMEM((2 * half, HEAD_DIM), BF16),
            VMEM((HEAD_DIM, half), BF16),
            VMEM((half, HEAD_DIM), BF16),
            VMEM((HEAD_DIM, half), BF16),
            VMEM((HEAD_DIM, half), F32),
            VMEM((2 * half, HEAD_DIM), F32),
            VMEM((2 * half, HEAD_DIM), F32),
        ],
        compiler_params=params(),
        name="backward",
    )(info, mine, other, att, stats)


def merge_kernel(out_ref, sib_ref, done_ref):
    done_ref[:, 0:2] = (out_ref[:, 0:2].astype(F32) + sib_ref[...].astype(F32)).astype(BF16)
    done_ref[:, 2:4] = out_ref[:, 2:4]


def merge(out, sib):
    return pl.pallas_call(
        merge_kernel,
        out_shape=jax.ShapeDtypeStruct(out.shape, out.dtype),
        in_specs=[vspec(), vspec()],
        out_specs=vspec(),
        compiler_params=params(16 * 1024 * 1024),
        name="merge",
    )(out, sib)


def finish_kernel(
    back_ref,
    gate_ref,
    slope_ref,
    hist_ref,
    up_ref,
    cot_ref,
    place_ref,
    w_in_ref,
    w_out_ref,
    mixed_ref,
    rows_ref,
    part_ref,
    total_ref,
):
    step = pl.program_id(0)

    def gather(part):
        for head in range(HEADS):
            part_ref[:, head * HEAD_DIM : (head + 1) * HEAD_DIM] = back_ref[head, part]
        return part_ref[...].astype(F32)

    def add(grad):
        pre = (grad * slope_ref[...].astype(F32)).astype(BF16)
        return dot_nt(pre, w_in_ref[...])

    @pl.when(step == 0)
    def _():
        hat = gather(3)
        gated = (hat * gate_ref[...].astype(F32)).astype(BF16)
        mixed_ref[...] = (hist_ref[...].astype(F32) + dot(gated, w_out_ref[...])).astype(BF16)
        total_ref[...] = add(up_ref[...] * hat)

    for s, part in ((1, 1), (2, 2), (3, 0)):

        @pl.when(step == s)
        def _():
            total_ref[...] += add(gather(part))

    @pl.when(step == 3)
    def _():
        hat, inverse = normalize(hist_ref[...].astype(F32))
        grad = total_ref[...]
        grad = inverse * (grad - row_mean(grad) - hat * row_mean(grad * hat))
        grad = (grad + cot_ref[...].astype(F32)).astype(BF16)
        rows_ref[...] = dot(onehot(place_ref[...]), grad).astype(BF16)


def finish(back, gate, slope, history, upstream, cotangent, place, w_in, w_out):
    rows, width = history.shape

    def whole(*shape):
        return pl.BlockSpec(shape, lambda j, *_: (0,) * len(shape))

    return pl.pallas_call(
        finish_kernel,
        grid_spec=pltpu.PrefetchScalarGridSpec(
            num_scalar_prefetch=0,
            grid=(4,),
            in_specs=[
                whole(CHIPS, 4, ROWS, HEAD_DIM),
                whole(rows, width),
                pl.BlockSpec((rows, width), lambda j, *_: (0, j)),
                whole(rows, width),
                whole(rows, width),
                whole(rows, width),
                whole(1, rows),
                pl.BlockSpec((width, width), lambda j, *_: (0, j)),
                whole(width, width),
            ],
            out_specs=[whole(rows, width), whole(rows, width)],
            scratch_shapes=[VMEM((rows, width), BF16), VMEM((rows, width), F32)],
        ),
        out_shape=[
            jax.ShapeDtypeStruct((rows, width), BF16),
            jax.ShapeDtypeStruct((rows, width), BF16),
        ],
        compiler_params=params(),
        name="finish",
    )(back, gate, slope, history, upstream, cotangent, place, w_in, w_out)


def body(log_rows, send_order, place, hist_len, w_in, w_out, cotangent):
    rows, width = log_rows.shape
    seq_size = lax.axis_size("seq")
    seq_index = lax.axis_index("seq")
    spot = seq_index % GROUP
    length = jnp.take(hist_len[0], seq_index // GROUP)
    info = jnp.stack([length, spot, spot % 2]).astype(jnp.int32)
    same_core = [list(range(g + c, g + GROUP, 2)) for g in range(0, seq_size, GROUP) for c in (0, 1)]
    swap = [(i, i ^ 1) for i in range(seq_size)]

    def to_all(block):
        block = block.reshape(rows // 2, 2, width)
        block = lax.all_to_all(block, ("dp", "seq"), split_axis=0, concat_axis=0, tiled=True)
        return block.reshape(rows, width)

    def to_group(block, members):
        return lax.all_to_all(
            block, "seq", split_axis=0, concat_axis=0, tiled=True, axis_index_groups=members
        )

    upstream = jnp.dot(cotangent, w_out.T, preferred_element_type=F32)
    arrived = to_all(pick_rows(log_rows, send_order))
    history, gate, slope, block = project(arrived, place, w_in, upstream)
    mine = to_group(block, same_core)
    other = lax.ppermute(mine[:, :2], "seq", swap)
    att, stats = forward(info, mine, other)
    stats = to_group(stats, same_core)
    out, sib = backward(info, mine, other, att, stats)
    sib = lax.ppermute(sib, "seq", swap)
    back = to_group(merge(out, sib), same_core)
    mixed, grads = finish(
        back, gate, slope, history, upstream, cotangent, place, w_in, w_out
    )
    log_grad = unpick_rows(to_all(grads), send_order, F32)
    return (mixed, log_grad)


def solution(mesh):
    rows = P(("dp", "seq"), None)
    return jax.shard_map(
        body,
        mesh=mesh,
        in_specs=(rows, rows, rows, P("dp", None), P(), P(), rows),
        out_specs=(rows, rows),
        check_vma=False,
    )
```

time: 191 us -> 177 us (0.927)
  Pallas kernels: 65.7 us -> 42.7 us
  local copies, waits for them, and re-layouts: 4.1 us -> 8.27 us
  blocking collectives: 88.8 us -> 91.7 us
    pallas_call x2, Pallas kernels: 28.7 us -> 15.7 us  [the longest x1 15.4 us: backward(): pl.pallas_call(backward_kernel, out_shape=[jax.ShapeDtypeStruct((CHIPS, 4...]
    pallas_call x1, Pallas kernels: 17.2 us -> 8.21 us  [forward(): pl.pallas_call(forward_kernel, out_shape=[jax.ShapeDtypeStruct((HEAD_DIM,...]
    all_to_all x1, blocking collectives: 17.9 us -> 22.8 us  [to_all(): lax.all_to_all(block, ('dp', 'seq'), split_axis=0, concat_axis=0, tiled=T...]
    unnamed x16 -> x28, local copies, waits for them, and re-layouts: 1.8 us -> 4.2 us
    all_to_all x3, blocking collectives: 70.9 us -> 68.9 us  [to_group(): lax.all_to_all(block, 'seq', split_axis=0, concat_axis=0, tiled=True, axi...]
where the time goes in v2:
time: 177 us; the launch traced here: 176 us
  blocking collectives  91.7 us (52%)
  Pallas kernels  42.7 us (24%)
  waiting for transfers between devices  14.8 us (8%)
  starting transfers between devices  14.4 us (8%)
  local copies, waits for them, and re-layouts  8.27 us (5%)
  matrix products  2.39 us (1%)
    all_to_all x3, blocking collectives, to_group(): lax.all_to_all(block, 'seq', split_axis=0, concat_axis=0, tiled=True, axi...  68.9 us
    all_to_all x1, blocking collectives, to_all(): lax.all_to_all(block, ('dp', 'seq'), split_axis=0, concat_axis=0, tiled=T...  22.8 us
    pallas_call x1, Pallas kernels, backward(): pl.pallas_call(backward_kernel, out_shape=[jax.ShapeDtypeStruct((CHIPS, 4...  15.4 us
    all_to_all x1, starting transfers between devices, to_all(): lax.all_to_all(block, ('dp', 'seq'), split_axis=0, concat_axis=0, tiled=T...  11.5 us
    all_to_all x1, waiting for transfers between devices, to_all(): lax.all_to_all(block, ('dp', 'seq'), split_axis=0, concat_axis=0, tiled=T...  11.1 us
    pallas_call x1, Pallas kernels, finish(): pl.pallas_call(finish_kernel, grid_spec=pltpu.PrefetchScalarGridSpec(num_...  8.87 us
    pallas_call x1, Pallas kernels, project(): pl.pallas_call(project_kernel, grid_spec=pltpu.PrefetchScalarGridSpec(num...  8.36 us
    pallas_call x1, Pallas kernels, forward(): pl.pallas_call(forward_kernel, out_shape=[jax.ShapeDtypeStruct((HEAD_DIM,...  8.21 us
  transfers between devices with their start and end apart: 3, of which 3 were waited for; matrix products, arithmetic and copies ran while one was open for 2% of the time, Pallas kernels for 0%

profile of v2, /device:TPU:1, one launch (start us, length us, event | category | flops | bytes accessed | tf_op | source)
XLA Modules:
  0.0 175.6 jit_solution(14021118807683820174)
XLA Ops:
  0.6 0.0 copy-start
  0.6 0.0 copy-start.3
  0.7 1.1 copy-done.10
  1.8 0.7 copy-done.12
  2.4 0.3 pick_rows.1
  2.8 1.0 reshape.17
  3.8 11.5 %all-to-all-start = ((bf16[128,2,1024]{2,1,0:T(2,128)(2,1)}), bf16[128,2,1024]{2,1,0:T(2,128)(2,1)S(1)}, u32[]{:S(2)}, u32[]{:S(2)}) async-start(bf16[128,2,1024]{2,1,0:T(2,128)(2,1)} %reshape.17), calls=%async_computation | async-start | bytes 1048576 | tf_op jit(solution)/shard_map/all_to_all | solution.py:504
  15.3 0.0 copy-start.11
  15.3 2.4 %fusion.up_ref = f32[256,1024]{1,0:T(8,128)S(1)} fusion(bf16[256,1024]{1,0:T(8,128)(2,1)S(1)} %copy-done.3, bf16[1024,1024]{1,0:T(8,128)(2,1)} %w_out_ref.1), kind=kOutput, calls=%fused_computation.2 | convolution fusion | flops 536870912 | bytes 3670016 | tf_op jit(solution)/shard_map/dot_general | solution.py:512
  17.7 11.1 %all-to-all-done = bf16[128,2,1024]{2,1,0:T(2,128)(2,1)S(1)} async-done(((bf16[128,2,1024]{2,1,0:T(2,128)(2,1)}), bf16[128,2,1024]{2,1,0:T(2,128)(2,1)S(1)}, u32[]{:S(2)}, u32[]{:S(2)}) %all-to-all-start) | async-done | bytes 524320 | tf_op jit(solution)/shard_map/all_to_all | solution.py:504
  28.8 1.0 reshape.18.arrived_ref
  29.8 1.0 copy-done.5
  30.8 8.4 %project.1 = (bf16[256,1024]{1,0:T(8,128)(2,1)S(1)}, bf16[256,1024]{1,0:T(8,128)(2,1)S(1)}, bf16[256,4096]{1,0:T(8,128)(2,1)S(1)}, bf16[8,4,256,128]{3,2,1,0:T(8,128)(2,1)}) custom-call(bf16[256,1024]{1,0:T(8,128)(2,1)S(1)} %copy-done.5, s32[1,256]{1,0:T(1,128)S(1)} %copy-done.11, bf16[1024,4096]{1,0:T(8,128)(2,1)} %w_in_ref.1, f32[256,1024]{1,0:T(8,128)S(1)} %fusion.up_ref), custom_call_target="tpu_custom_call" | custom-call | tf_op jit(solution)/shard_map/project/pallas_call | solution.py:138
  39.2 1.3 copy-done.2
  40.5 29.4 %all_to_all.25.mine_ref = bf16[8,4,256,128]{3,2,1,0:T(8,128)(2,1)S(1)} all-to-all(bf16[8,4,256,128]{3,2,1,0:T(8,128)(2,1)} %get-tuple-element.12), channel_id=1, replica_groups={{0,2,4,6,8,10,12,14},{1,3,5,7,9,11,13,15},{16,18,20,22,24,26,28,30},{17..., dimensions={0} | all-to-all | bytes 4194304 | tf_op jit(solution)/shard_map/all_to_all | solution.py:508
  69.9 1.1 slice.9
  71.0 2.0 %collective-permute-start = (bf16[8,2,256,128]{3,2,1,0:T(8,128)(2,1)}, bf16[8,2,256,128]{3,2,1,0:T(8,128)(2,1)}, u32[]{:S(2)}, u32[]{:S(2)}) collective-permute-start(bf16[8,2,256,128]{3,2,1,0:T(8,128)(2,1)} %slice.9), channel_id=1, source_target_pairs={{0,1},{1,0},{2,3},{3,2},{4,5},{5,4},{6,7},{7,6},{8,9},{9,8},{10,11... | collective-permute-start | bytes 3145736 | tf_op jit(solution)/shard_map/ppermute | solution.py:516
  73.0 0.6 constant_dynamic-slice_fusion
  74.2 0.1 pad_add_fusion.info
  74.3 1.4 collective-permute-done.other_ref
  75.7 8.2 %forward.1 = (f32[128,2048]{1,0:T(8,128)S(1)}, f32[8,4,2048]{2,1,0:T(4,128)S(1)}) custom-call(s32[3]{0:T(128)S(1)} %pad_add_fusion.info, bf16[8,4,256,128]{3,2,1,0:T(8,128)(2,1)S(1)} %all_to_all.25.mine_ref, bf16[8,2,256,128]{3,2,1,0:T(8,128)(2,1)} %collective-permute-done.other_ref), custom_call_target="tpu_custom_call" | custom-call | tf_op jit(solution)/shard_map/forward/pallas_call | solution.py:252
  83.9 9.8 %all_to_all.26.stats_ref = f32[8,4,2048]{2,1,0:T(4,128)S(1)} all-to-all(f32[8,4,2048]{2,1,0:T(4,128)S(1)} %get-tuple-element.14), channel_id=1, replica_groups={{0,2,4,6,8,10,12,14},{1,3,5,7,9,11,13,15},{16,18,20,22,24,26,28,30},{17..., dimensions={0} | all-to-all | bytes 524288 | tf_op jit(solution)/shard_map/all_to_all | solution.py:508
  93.7 15.4 %backward.1 = (bf16[8,4,256,128]{3,2,1,0:T(8,128)(2,1)S(1)}, bf16[8,2,256,128]{3,2,1,0:T(8,128)(2,1)S(1)}) custom-call(s32[3]{0:T(128)S(1)} %pad_add_fusion.info, bf16[8,4,256,128]{3,2,1,0:T(8,128)(2,1)} %copy-done.1, bf16[8,2,256,128]{3,2,1,0:T(8,128)(2,1)} %collective-permute-done.other_ref, f32[128,2048]{1,0:T(8,128)S(1)} %get-tuple-element.13.att_ref, ...), custom_call_target="tpu_custom_call" | custom-call | tf_op jit(solution)/shard_map/backward/pallas_call | solution.py:370
  109.1 0.9 collective-permute-start.1
  110.0 2.3 %collective-permute-done.1.sib_ref = bf16[8,2,256,128]{3,2,1,0:T(8,128)(2,1)S(1)} collective-permute-done((bf16[8,2,256,128]{3,2,1,0:T(8,128)(2,1)S(1)}, bf16[8,2,256,128]{3,2,1,0:T(8,128)(2,1)S(1)}, u32[]{:S(2)}, u32[]{:S(2)}) %collective-permute-start.1) | collective-permute-done | bytes 1048608 | tf_op jit(solution)/shard_map/ppermute | solution.py:520
  112.3 0.3 merge.1
  112.6 29.7 %all_to_all.27.back_ref = bf16[8,4,256,128]{3,2,1,0:T(8,128)(2,1)S(1)} all-to-all(bf16[8,4,256,128]{3,2,1,0:T(8,128)(2,1)S(1)} %merge.1), channel_id=1, replica_groups={{0,2,4,6,8,10,12,14},{1,3,5,7,9,11,13,15},{16,18,20,22,24,26,28,30},{17..., dimensions={0} | all-to-all | bytes 4194304 | tf_op jit(solution)/shard_map/all_to_all | solution.py:508
  142.3 8.9 %finish.1 = (bf16[256,1024]{1,0:T(8,128)(2,1)}, bf16[256,1024]{1,0:T(8,128)(2,1)S(1)}) custom-call(bf16[8,4,256,128]{3,2,1,0:T(8,128)(2,1)S(1)} %all_to_all.27.back_ref, bf16[256,1024]{1,0:T(8,128)(2,1)S(1)} %copy-done.9, bf16[256,4096]{1,0:T(8,128)(2,1)} %copy-done.2, bf16[256,1024]{1,0:T(8,128)(2,1)S(1)} %copy-done.7, f32[256,1024]{1,0:T(8,128)S(1)} %fusion.up_ref, ...), custom_call_target="tpu_custom_call" | custom-call | tf_op jit(solution)/shard_map/finish/pallas_call | solution.py:464
  151.2 0.2 reshape.19
  151.4 22.8 %all_to_all.28 = bf16[128,2,1024]{2,1,0:T(2,128)(2,1)S(1)} all-to-all(bf16[128,2,1024]{2,1,0:T(2,128)(2,1)S(1)} %reshape.19), channel_id=1, replica_groups=mesh['dp'=4,'seq'=32] {'dp','seq'}, dimensions={0} | all-to-all | bytes 1048576 | tf_op jit(solution)/shard_map/all_to_all | solution.py:504
  174.2 0.2 reshape.20.rows_ref
  174.4 1.3 unpick_rows.1
  (21 shorter events, 0.0 us)
Async XLA Ops:
  0.6 72.4 %copy-start = (s32[1,2]{1,0:T(1,128)S(1)}, s32[1,2]{1,0:T(1,128)}, u32[]{:S(2)}) copy-start(s32[1,2]{1,0:T(1,128)} %param.10) | copy-start | bytes 28
  0.6 14.6 %copy-start.3 = (bf16[256,1024]{1,0:T(8,128)(2,1)S(1)}, bf16[256,1024]{1,0:T(8,128)(2,1)}, u32[]{:S(2)}) copy-start(bf16[256,1024]{1,0:T(8,128)(2,1)} %cot_ref.1) | copy-start | bytes 1572868
  0.7 1.1 copy-start.10
  1.8 0.7 copy-start.12
  3.8 25.0 %all-to-all-start = ((bf16[128,2,1024]{2,1,0:T(2,128)(2,1)}), bf16[128,2,1024]{2,1,0:T(2,128)(2,1)S(1)}, u32[]{:S(2)}, u32[]{:S(2)}) async-start(bf16[128,2,1024]{2,1,0:T(2,128)(2,1)} %reshape.17), calls=%async_computation | async-start | bytes 1048576 | tf_op jit(solution)/shard_map/all_to_all | solution.py:504
  15.3 14.5 %copy-start.11 = (s32[1,256]{1,0:T(1,128)S(1)}, s32[1,256]{1,0:T(1,128)}, u32[]{:S(2)}) copy-start(s32[1,256]{1,0:T(1,128)} %place_ref.3) | copy-start | bytes 3076
  29.8 1.0 copy-start.5
  39.2 1.3 copy-start.2
  40.5 29.4 %copy-start.6 = (bf16[256,1024]{1,0:T(8,128)(2,1)}, bf16[256,1024]{1,0:T(8,128)(2,1)S(1)}, u32[]{:S(2)}) copy-start(bf16[256,1024]{1,0:T(8,128)(2,1)S(1)} %get-tuple-element.19.hist_ref) | copy-start | bytes 1572868
  40.5 29.4 %copy-start.8 = (bf16[256,1024]{1,0:T(8,128)(2,1)}, bf16[256,1024]{1,0:T(8,128)(2,1)S(1)}, u32[]{:S(2)}) copy-start(bf16[256,1024]{1,0:T(8,128)(2,1)S(1)} %get-tuple-element.17.gate_ref) | copy-start | bytes 1572868
  69.9 14.0 %copy-start.1 = (bf16[8,4,256,128]{3,2,1,0:T(8,128)(2,1)}, bf16[8,4,256,128]{3,2,1,0:T(8,128)(2,1)S(1)}, u32[]{:S(2)}) copy-start(bf16[8,4,256,128]{3,2,1,0:T(8,128)(2,1)S(1)} %all_to_all.25.mine_ref) | copy-start | bytes 6291460
  71.0 4.6 %collective-permute-start = (bf16[8,2,256,128]{3,2,1,0:T(8,128)(2,1)}, bf16[8,2,256,128]{3,2,1,0:T(8,128)(2,1)}, u32[]{:S(2)}, u32[]{:S(2)}) collective-permute-start(bf16[8,2,256,128]{3,2,1,0:T(8,128)(2,1)} %slice.9), channel_id=1, source_target_pairs={{0,1},{1,0},{2,3},{3,2},{4,5},{5,4},{6,7},{7,6},{8,9},{9,8},{10,11... | collective-permute-start | bytes 3145736 | tf_op jit(solution)/shard_map/ppermute | solution.py:516
  109.1 3.2 %collective-permute-start.1 = (bf16[8,2,256,128]{3,2,1,0:T(8,128)(2,1)S(1)}, bf16[8,2,256,128]{3,2,1,0:T(8,128)(2,1)S(1)}, u32[]{:S(2)}, u32[]{:S(2)}) collective-permute-start(bf16[8,2,256,128]{3,2,1,0:T(8,128)(2,1)S(1)} %get-tuple-element.16), channel_id=1, source_target_pairs={{0,1},{1,0},{2,3},{3,2},{4,5},{5,4},{6,7},{7,6},{8,9},{9,8},{10,11... | collective-permute-start | bytes 3145736 | tf_op jit(solution)/shard_map/ppermute | solution.py:520
  112.6 29.7 %copy-start.4 = (bf16[256,1024]{1,0:T(8,128)(2,1)S(1)}, bf16[256,1024]{1,0:T(8,128)(2,1)}, u32[]{:S(2)}) copy-start(bf16[256,1024]{1,0:T(8,128)(2,1)} %cot_ref.1) | copy-start | bytes 1572868
  112.6 29.7 %copy-start.7 = (bf16[256,1024]{1,0:T(8,128)(2,1)S(1)}, bf16[256,1024]{1,0:T(8,128)(2,1)}, u32[]{:S(2)}) copy-start(bf16[256,1024]{1,0:T(8,128)(2,1)} %copy-done.6) | copy-start | bytes 1572868
  112.6 29.7 %copy-start.9 = (bf16[256,1024]{1,0:T(8,128)(2,1)S(1)}, bf16[256,1024]{1,0:T(8,128)(2,1)}, u32[]{:S(2)}) copy-start(bf16[256,1024]{1,0:T(8,128)(2,1)} %copy-done.8) | copy-start | bytes 1572868
  151.2 23.2 %copy-start.13 = (s32[1,256]{1,0:T(1,128)S(1)}, s32[1,256]{1,0:T(1,128)}, u32[]{:S(2)}) copy-start(s32[1,256]{1,0:T(1,128)} %order_ref.3) | copy-start | bytes 3076

commit v3 on v2

v3 whole, which is shorter than its diff:
```python
import functools
import math

import jax
import jax.numpy as jnp
from jax import lax
from jax.experimental import pallas as pl
from jax.experimental.pallas import tpu as pltpu
from jax.sharding import PartitionSpec as P

HEADS = 8
GROUP = 16
EPSILON = 1e-05
CHIPS = 8
ROWS = 256
HEAD_DIM = 128
MIB = 1024 * 1024
DENSE = 56
SMALL = 48
ATTN = 48
BF16 = jnp.bfloat16
F32 = jnp.float32
VMEM = pltpu.VMEM
SMEM = pltpu.SMEM


def params(mib):
    return pltpu.CompilerParams(vmem_limit_bytes=mib * MIB)


def vspec():
    return pl.BlockSpec(memory_space=VMEM)


def aspec():
    return pl.BlockSpec(memory_space=pl.ANY)


def hspec():
    return pl.BlockSpec(memory_space=pltpu.HBM)


def sspec():
    return pl.BlockSpec(memory_space=SMEM)


def dot(a, b):
    return jnp.dot(a, b, preferred_element_type=F32)


def dot_nt(a, b):
    return lax.dot_general(a, b, (((1,), (1,)), ((), ())), preferred_element_type=F32)


def dot_tn(a, b):
    return lax.dot_general(a, b, (((0,), (0,)), ((), ())), preferred_element_type=F32)


def onehot(order):
    count = order.shape[1]
    spots = lax.broadcasted_iota(jnp.int32, (count, count), 0)
    return jnp.where(spots == order, 1.0, 0.0).astype(BF16)


def row_mean(x):
    return jnp.mean(x, axis=-1, keepdims=True)


def normalize(inputs):
    centred = inputs - row_mean(inputs)
    inverse = lax.rsqrt(row_mean(centred * centred) + EPSILON)
    return centred * inverse, inverse


def pick_kernel(rows_ref, order_ref, out_ref):
    rows = dot_tn(onehot(order_ref[...]), rows_ref[...]).astype(out_ref.dtype)
    out_ref[...] = rows.reshape(out_ref.shape)


def pick_rows(rows, order):
    return pl.pallas_call(
        pick_kernel,
        out_shape=jax.ShapeDtypeStruct((rows.shape[0] // 2, 2, rows.shape[1]), rows.dtype),
        in_specs=[vspec(), vspec()],
        out_specs=vspec(),
        compiler_params=params(SMALL),
        name="pick_rows",
    )(rows, order)


def unpick_kernel(rows_ref, order_ref, out_ref):
    out_ref[...] = dot(onehot(order_ref[...]), rows_ref[...].reshape(out_ref.shape)).astype(
        out_ref.dtype
    )


def unpick_rows(rows, order, dtype):
    return pl.pallas_call(
        unpick_kernel,
        out_shape=jax.ShapeDtypeStruct((2 * rows.shape[0], rows.shape[2]), dtype),
        in_specs=[vspec(), vspec()],
        out_specs=vspec(),
        compiler_params=params(SMALL),
        name="unpick_rows",
    )(rows, order)


CHUNK = 512


def start_weights(w_hbm, w_ref, sems, blocks):
    width = w_hbm.shape[0]
    per = width // CHUNK

    def copy(slot, chunk):
        return pltpu.make_async_copy(
            w_hbm.at[:, pl.ds(blocks[slot] * width + chunk * CHUNK, CHUNK)],
            w_ref.at[slot * per + chunk],
            sems.at[slot * per + chunk],
        )

    for slot in range(len(blocks)):
        for chunk in range(per):
            copy(slot, chunk).start()
    return lambda slot, chunk: copy(slot, chunk).wait()


def chunks(width):
    return [(c, slice(c * CHUNK, (c + 1) * CHUNK)) for c in range(width // CHUNK)]


def activate(preact):
    sigmoid = jnp.tanh(preact * 0.5) * 0.5 + 0.5
    act = preact * sigmoid
    return act.astype(BF16), (sigmoid + act - act * sigmoid).astype(BF16)


def lay(buf_ref, part, chunk, block):
    heads = CHUNK // HEAD_DIM
    for head in range(heads):
        buf_ref[chunk * heads + head, part] = block[:, head * HEAD_DIM : (head + 1) * HEAD_DIM]


def project_kq_kernel(
    info,
    arrived_ref,
    place_ref,
    w_hbm,
    _,
    hist_ref,
    normed_ref,
    slope_ref,
    buf_ref,
    w_ref,
    sems,
):
    rows, width = hist_ref.shape
    arrive = start_weights(w_hbm, w_ref, sems, (3, 2))
    history = dot_tn(onehot(place_ref[...]), arrived_ref[...].reshape(rows, width))
    hist_ref[...] = history.astype(BF16)
    normed = normalize(history)[0].astype(BF16)
    normed_ref[...] = normed
    for part in range(2):
        for chunk, columns in chunks(width):
            arrive(part, chunk)
            act, slope = activate(dot(normed, w_ref[part * (width // CHUNK) + chunk]))
            slope_ref[part, :, columns] = slope
            lay(buf_ref, part, chunk, act)


def project_vu_kernel(
    normed_ref, w_hbm, up_ref, gate_ref, slope_ref, buf_ref, token_ref, w_ref, sems
):
    width = normed_ref.shape[1]
    arrive = start_weights(w_hbm, w_ref, sems, (1, 0))
    normed = normed_ref[...]
    for part in range(2):
        for chunk, columns in chunks(width):
            arrive(part, chunk)
            act, slope = activate(dot(normed, w_ref[part * (width // CHUNK) + chunk]))
            slope_ref[part, :, columns] = slope
            if part:
                gate_ref[:, columns] = act
                act = (up_ref[:, columns] * act.astype(F32)).astype(BF16)
            lay(buf_ref, part, chunk, act)
    token_ref[...] = jnp.zeros_like(token_ref)


def weight_scratch(width):
    count = 2 * (width // CHUNK)
    return [VMEM((count, width, CHUNK), BF16), pltpu.SemaphoreType.DMA((count,))]


def dense_cost(rows, width, blocks):
    return pl.CostEstimate(
        flops=2 * rows * width * width * blocks,
        bytes_accessed=2 * width * width * blocks + 8 * rows * width * blocks,
        transcendentals=rows * width * blocks,
    )


def project_kq(info, arrived, place, w_in, upstream):
    rows, width = upstream.shape
    return pl.pallas_call(
        project_kq_kernel,
        in_specs=[sspec(), vspec(), vspec(), hspec(), aspec()],
        out_specs=[vspec()] * 4,
        out_shape=[
            jax.ShapeDtypeStruct((rows, width), BF16),
            jax.ShapeDtypeStruct((rows, width), BF16),
            jax.ShapeDtypeStruct((2, rows, width), BF16),
            jax.ShapeDtypeStruct((CHIPS, 2, ROWS, HEAD_DIM), BF16),
        ],
        scratch_shapes=weight_scratch(width),
        compiler_params=params(DENSE),
        cost_estimate=dense_cost(rows, width, 2),
        name="project_kq",
    )(info, arrived, place, w_in, upstream)


def project_vu(normed, w_in, upstream):
    rows, width = normed.shape
    return pl.pallas_call(
        project_vu_kernel,
        in_specs=[vspec(), hspec(), vspec()],
        out_specs=[vspec()] * 4,
        out_shape=[
            jax.ShapeDtypeStruct((rows, width), BF16),
            jax.ShapeDtypeStruct((2, rows, width), BF16),
            jax.ShapeDtypeStruct((CHIPS, 2, ROWS, HEAD_DIM), BF16),
            jax.ShapeDtypeStruct((8, HEAD_DIM), F32),
        ],
        scratch_shapes=weight_scratch(width),
        compiler_params=params(DENSE),
        cost_estimate=dense_cost(rows, width, 2),
        name="project_vu",
    )(normed, w_in, upstream)


def part_kernel(pair_ref, _, out_ref):
    out_ref[...] = pair_ref[:, 0]


def first_part(pair, after):
    chips, _, rows, width = pair.shape
    return pl.pallas_call(
        part_kernel,
        out_shape=jax.ShapeDtypeStruct((chips, rows, width), pair.dtype),
        in_specs=[vspec(), aspec()],
        out_specs=vspec(),
        compiler_params=params(SMALL),
        name="first_part",
    )(pair, after)


TILES = CHIPS * (CHIPS + 1) // 2
KEY_TILE = 2 * ROWS
SCALE = 0.5 / math.sqrt(HEAD_DIM)


def tile_of(j, m):
    return j * CHIPS - j * (j - 1) // 2 + m - j


def lay_rows(info, own_ref, other_ref, out_ref):
    length, core = info[0], info[1]
    for chip in range(CHIPS):
        for source, side in ((own_ref.at[chip, 0], core), (other_ref.at[chip], 1 - core)):
            start = pl.multiple_of((2 * chip + side) * ROWS, ROWS)
            out_ref[pl.ds(start, ROWS), :] = source[...]

    @pl.when(length < GROUP * ROWS)
    def _():
        def clear(block, carry):
            where = pl.ds(pl.multiple_of(block * ROWS, ROWS), ROWS)
            spots = lax.broadcasted_iota(jnp.int32, (ROWS, HEAD_DIM), 0) + block * ROWS
            rows = jnp.where(spots < length, out_ref[where, :].astype(F32), 0.0)
            out_ref[where, :] = rows.astype(BF16)
            return carry

        lax.fori_loop(length // ROWS, GROUP, clear, 0)


def each_tile(length, work, dead=None, order=range(CHIPS)[::-1]):
    for j in order:
        if j == 0:
            work(0)
            continue
        pl.when(KEY_TILE * j < length)(functools.partial(work, j))
        if dead is not None:
            pl.when(KEY_TILE * j >= length)(functools.partial(dead, j))


def tiles_of(j):
    return pl.ds(tile_of(j, j), CHIPS - j)


def fetch_tiles(length, kept_ref, here_ref, sems):
    def copy(j):
        return pltpu.make_async_copy(kept_ref.at[tiles_of(j)], here_ref.at[tiles_of(j)], sems.at[j])

    each_tile(length, lambda j: copy(j).start())
    return lambda j: copy(j).wait()


def keys_of(j):
    return slice(KEY_TILE * j, KEY_TILE * (j + 1))


def rows_of(m):
    return slice(ROWS * m, ROWS * (m + 1))


def weigh_kernel(
    info,
    kq_ref,
    other_ref,
    _,
    weight_out,
    slope_out,
    token_ref,
    key_ref,
    query_t_ref,
    weight_ref,
    slope_ref,
    weight_sems,
    slope_sems,
):
    length, core = info[0], info[1]

    def copies(j):
        where = tiles_of(j)
        return (
            pltpu.make_async_copy(weight_ref.at[where], weight_out.at[where], weight_sems.at[j]),
            pltpu.make_async_copy(slope_ref.at[where], slope_out.at[where], slope_sems.at[j]),
        )

    lay_rows(info, kq_ref, other_ref, key_ref)
    for m in range(CHIPS):
        query_t_ref[:, rows_of(m)] = (kq_ref[m, 1].astype(F32) * SCALE).T.astype(BF16)

    def work(j):
        for m in range(j, CHIPS):
            half = dot(key_ref[keys_of(j), :], query_t_ref[:, rows_of(m)])
            tanh = jnp.tanh(half)
            weights = half * (1.0 + tanh)
            slope = (1.0 + tanh) + weights * (1.0 - tanh)
            if m == j:
                query_spot = lax.broadcasted_iota(jnp.int32, (KEY_TILE, ROWS), 1) + core * ROWS
                key_spot = lax.broadcasted_iota(jnp.int32, (KEY_TILE, ROWS), 0)
                allowed = key_spot <= query_spot
                weights = jnp.where(allowed, weights, 0.0)
                slope = jnp.where(allowed, slope, 0.0)
            weight_ref[tile_of(j, m)] = weights.astype(BF16)
            slope_ref[tile_of(j, m)] = slope.astype(BF16)
        for copy in copies(j):
            copy.start()

    def drain(j):
        for copy in copies(j):
            copy.wait()

    each_tile(length, work, order=range(CHIPS))
    token_ref[...] = jnp.zeros_like(token_ref)
    each_tile(length, drain)


def attention_cost(matmuls, exps):
    area = TILES * KEY_TILE * ROWS
    return pl.CostEstimate(
        flops=4 * matmuls * area * HEAD_DIM, bytes_accessed=4 * area, transcendentals=exps * area
    )


def weigh(info, kq, other, after):
    half = CHIPS * ROWS
    return pl.pallas_call(
        weigh_kernel,
        out_shape=[
            jax.ShapeDtypeStruct((TILES, KEY_TILE, ROWS), BF16),
            jax.ShapeDtypeStruct((TILES, KEY_TILE, ROWS), BF16),
            jax.ShapeDtypeStruct((8, HEAD_DIM), F32),
        ],
        in_specs=[sspec(), vspec(), vspec(), aspec()],
        out_specs=[hspec(), hspec(), vspec()],
        scratch_shapes=[
            VMEM((2 * half, HEAD_DIM), BF16),
            VMEM((HEAD_DIM, half), BF16),
            VMEM((TILES, KEY_TILE, ROWS), BF16),
            VMEM((TILES, KEY_TILE, ROWS), BF16),
            pltpu.SemaphoreType.DMA((CHIPS,)),
            pltpu.SemaphoreType.DMA((CHIPS,)),
        ],
        compiler_params=params(ATTN),
        cost_estimate=attention_cost(1, 1),
        name="weigh",
    )(info, kq, other, after)


def attend_kernel(
    info,
    vu_ref,
    other_ref,
    weight_hbm,
    att_ref,
    stats_ref,
    value_ref,
    value_t_ref,
    weight_ref,
    sems,
):
    length = info[0]
    arrive = fetch_tiles(length, weight_hbm, weight_ref, sems)
    lay_rows(info, vu_ref, other_ref, value_ref)
    att_ref[...] = jnp.zeros_like(att_ref)

    def work(j):
        arrive(j)
        for block in (2 * j, 2 * j + 1):
            value_t_ref[:, rows_of(block)] = value_ref[rows_of(block), :].T
        for m in range(j, CHIPS):
            att_ref[:, rows_of(m)] += dot(value_t_ref[:, keys_of(j)], weight_ref[tile_of(j, m)])

    each_tile(length, work)
    for m in range(CHIPS):
        att = att_ref[:, rows_of(m)]
        up = vu_ref[m, 1].astype(F32).T
        mean = jnp.mean(att, axis=0, keepdims=True)
        centred = att - mean
        stats = jnp.concatenate(
            [
                mean,
                jnp.sum(centred * centred, axis=0, keepdims=True),
                jnp.sum(up, axis=0, keepdims=True),
                jnp.sum(up * centred, axis=0, keepdims=True),
            ],
            axis=0,
        )
        for head in range(HEADS):
            stats_ref[head, :, rows_of(m)] = stats


def attend(info, vu, other, weights):
    half = CHIPS * ROWS
    return pl.pallas_call(
        attend_kernel,
        out_shape=[
            jax.ShapeDtypeStruct((HEAD_DIM, half), F32),
            jax.ShapeDtypeStruct((HEADS, 4, half), F32),
        ],
        in_specs=[sspec(), vspec(), vspec(), hspec()],
        out_specs=[vspec(), vspec()],
        scratch_shapes=[
            VMEM((2 * half, HEAD_DIM), BF16),
            VMEM((HEAD_DIM, 2 * half), BF16),
            VMEM((TILES, KEY_TILE, ROWS), BF16),
            pltpu.SemaphoreType.DMA((CHIPS,)),
        ],
        compiler_params=params(ATTN),
        cost_estimate=attention_cost(1, 0),
        name="attend",
    )(info, vu, other, weights)


def back_v_kernel(
    info,
    vu_ref,
    att_ref,
    stats_ref,
    weight_hbm,
    out_ref,
    sib_ref,
    grad_t_ref,
    grad_ref,
    dv_ref,
    weight_ref,
    sems,
):
    length, core = info[0], info[1]
    arrive = fetch_tiles(length, weight_hbm, weight_ref, sems)
    width = HEADS * HEAD_DIM
    stat = [[stats_ref[head, s : s + 1, :] for s in range(4)] for head in range(HEADS)]
    mean = sum(row[0] for row in stat) * (1.0 / HEADS)
    square = sum(row[1] + HEAD_DIM * (row[0] - mean) * (row[0] - mean) for row in stat)
    inverse = lax.rsqrt(square * (1.0 / width) + EPSILON)
    up_mean = sum(row[2] for row in stat) * (1.0 / width)
    cross = sum(row[3] + (row[0] - mean) * row[2] for row in stat) * inverse * (1.0 / width)
    for m in range(CHIPS):
        where = rows_of(m)
        up = vu_ref[m, 1].astype(F32).T
        hat = (att_ref[:, where] - mean[:, where]) * inverse[:, where]
        out_ref[m, 1] = hat.T.astype(BF16)
        grad = inverse[:, where] * (up - up_mean[:, where] - hat * cross[:, where])
        grad_t_ref[:, where] = grad.astype(BF16)
        grad_ref[where, :] = grad.T.astype(BF16)

    def work(j):
        arrive(j)
        for m in range(j, CHIPS):
            term = dot(weight_ref[tile_of(j, m)], grad_ref[rows_of(m), :])
            if m == j:
                dv_ref[keys_of(j), :] = term
            else:
                dv_ref[keys_of(j), :] += term

    def dead(j):
        dv_ref[keys_of(j), :] = jnp.zeros((KEY_TILE, HEAD_DIM), F32)

    each_tile(length, work, dead)
    share(core, dv_ref, 1.0, out_ref, sib_ref)


def share(core, sum_ref, scale, out_ref, sib_ref):
    for chip in range(CHIPS):
        kept = pl.ds(pl.multiple_of((2 * chip + core) * ROWS, ROWS), ROWS)
        sent = pl.ds(pl.multiple_of((2 * chip + 1 - core) * ROWS, ROWS), ROWS)
        out_ref[chip, 0] = (sum_ref[kept, :] * scale).astype(BF16)
        sib_ref[chip] = (sum_ref[sent, :] * scale).astype(BF16)


def back_v(info, vu, att, stats, weights):
    half = CHIPS * ROWS
    return pl.pallas_call(
        back_v_kernel,
        out_shape=[
            jax.ShapeDtypeStruct((CHIPS, 2, ROWS, HEAD_DIM), BF16),
            jax.ShapeDtypeStruct((CHIPS, ROWS, HEAD_DIM), BF16),
            jax.ShapeDtypeStruct((HEAD_DIM, half), BF16),
        ],
        in_specs=[sspec(), vspec(), vspec(), vspec(), hspec()],
        out_specs=[vspec(), vspec(), vspec()],
        scratch_shapes=[
            VMEM((half, HEAD_DIM), BF16),
            VMEM((2 * half, HEAD_DIM), F32),
            VMEM((TILES, KEY_TILE, ROWS), BF16),
            pltpu.SemaphoreType.DMA((CHIPS,)),
        ],
        compiler_params=params(ATTN),
        cost_estimate=attention_cost(1, 0),
        name="back_v",
    )(info, vu, att, stats, weights)


def back_kq_kernel(
    info,
    kq_ref,
    vu_ref,
    other_ref,
    other_key_ref,
    slope_hbm,
    grad_t_ref,
    out_ref,
    sib_ref,
    value_ref,
    key_t_ref,
    dq_ref,
    dk_ref,
    slope_ref,
    sems,
):
    length, core = info[0], info[1]
    arrive = fetch_tiles(length, slope_hbm, slope_ref, sems)
    lay_rows(info, vu_ref, other_ref, value_ref)
    dq_ref[...] = jnp.zeros_like(dq_ref)
    for chip in range(CHIPS):
        for rows, side in ((kq_ref[chip, 0], core), (other_key_ref[chip], 1 - core)):
            start = pl.multiple_of((2 * chip + side) * ROWS, ROWS)
            key_t_ref[:, pl.ds(start, ROWS)] = rows.T

    def work(j):
        arrive(j)
        for m in range(j, CHIPS):
            grad = dot(value_ref[keys_of(j), :], grad_t_ref[:, rows_of(m)])
            grad = (grad * slope_ref[tile_of(j, m)].astype(F32)).astype(BF16)
            dk = dot(grad, kq_ref[m, 1])
            dq = dot(key_t_ref[:, keys_of(j)], grad)
            if m == j:
                dk_ref[keys_of(j), :] = dk
            else:
                dk_ref[keys_of(j), :] += dk
            dq_ref[:, rows_of(m)] += dq

    def dead(j):
        dk_ref[keys_of(j), :] = jnp.zeros((KEY_TILE, HEAD_DIM), F32)

    each_tile(length, work, dead)
    for m in range(CHIPS):
        out_ref[m, 1] = (dq_ref[:, rows_of(m)].T * SCALE).astype(BF16)
    share(core, dk_ref, SCALE, out_ref, sib_ref)


def back_kq(info, kq, vu, other, other_keys, slope, grad_t):
    half = CHIPS * ROWS
    return pl.pallas_call(
        back_kq_kernel,
        out_shape=[
            jax.ShapeDtypeStruct((CHIPS, 2, ROWS, HEAD_DIM), BF16),
            jax.ShapeDtypeStruct((CHIPS, ROWS, HEAD_DIM), BF16),
        ],
        in_specs=[sspec()] + [vspec()] * 4 + [hspec(), vspec()],
        out_specs=[vspec(), vspec()],
        scratch_shapes=[
            VMEM((2 * half, HEAD_DIM), BF16),
            VMEM((HEAD_DIM, 2 * half), BF16),
            VMEM((HEAD_DIM, half), F32),
            VMEM((2 * half, HEAD_DIM), F32),
            VMEM((TILES, KEY_TILE, ROWS), BF16),
            pltpu.SemaphoreType.DMA((CHIPS,)),
        ],
        compiler_params=params(ATTN),
        cost_estimate=attention_cost(3, 0),
        name="back_kq",
    )(info, kq, vu, other, other_keys, slope, grad_t)


def merge_kernel(out_ref, sib_ref, done_ref):
    done_ref[:, 0] = (out_ref[:, 0].astype(F32) + sib_ref[...].astype(F32)).astype(BF16)
    done_ref[:, 1] = out_ref[:, 1]


def merge(out, sib):
    return pl.pallas_call(
        merge_kernel,
        out_shape=jax.ShapeDtypeStruct(out.shape, out.dtype),
        in_specs=[vspec(), vspec()],
        out_specs=vspec(),
        compiler_params=params(SMALL),
        name="merge",
    )(out, sib)


def gather(back_ref, part, chunk):
    heads = CHUNK // HEAD_DIM
    blocks = [back_ref[chunk * heads + head, part].astype(F32) for head in range(heads)]
    return jnp.concatenate(blocks, axis=1)


def finish_vg_kernel(
    back_ref,
    gate_ref,
    slope_ref,
    hist_ref,
    up_ref,
    w_hbm,
    w_out_ref,
    mixed_ref,
    sum_ref,
    w_ref,
    sems,
):
    width = hist_ref.shape[1]
    arrive = start_weights(w_hbm, w_ref, sems, (1, 0))
    mixed = hist_ref[...].astype(F32)
    total = jnp.zeros(hist_ref.shape, F32)
    for part in range(2):
        for chunk, columns in chunks(width):
            grad = gather(back_ref, part, chunk)
            if part:
                gated = (grad * gate_ref[:, columns].astype(F32)).astype(BF16)
                mixed = mixed + dot(gated, w_out_ref[columns, :])
                grad = grad * up_ref[:, columns]
            pre = (grad * slope_ref[part, :, columns].astype(F32)).astype(BF16)
            arrive(part, chunk)
            total = total + dot_nt(pre, w_ref[part * (width // CHUNK) + chunk])
    mixed_ref[...] = mixed.astype(BF16)
    sum_ref[...] = total


def finish_vg(back, gate, slope, history, upstream, w_in, w_out):
    rows, width = history.shape
    return pl.pallas_call(
        finish_vg_kernel,
        in_specs=[vspec()] * 5 + [hspec(), vspec()],
        out_specs=[vspec(), vspec()],
        scratch_shapes=weight_scratch(width),
        out_shape=[
            jax.ShapeDtypeStruct((rows, width), BF16),
            jax.ShapeDtypeStruct((rows, width), F32),
        ],
        compiler_params=params(DENSE),
        cost_estimate=dense_cost(rows, width, 3),
        name="finish_vg",
    )(back, gate, slope, history, upstream, w_in, w_out)


def finish_kq_kernel(
    back_ref, slope_ref, hist_ref, start_ref, cot_ref, place_ref, w_hbm, rows_ref, w_ref, sems
):
    width = hist_ref.shape[1]
    arrive = start_weights(w_hbm, w_ref, sems, (3, 2))
    hat, inverse = normalize(hist_ref[...].astype(F32))
    grad = start_ref[...]
    for part in range(2):
        for chunk, columns in chunks(width):
            pre = gather(back_ref, part, chunk) * slope_ref[part, :, columns].astype(F32)
            arrive(part, chunk)
            grad = grad + dot_nt(pre.astype(BF16), w_ref[part * (width // CHUNK) + chunk])
    grad = inverse * (grad - row_mean(grad) - hat * row_mean(grad * hat))
    grad = (grad + cot_ref[...].astype(F32)).astype(BF16)
    rows_ref[...] = dot(onehot(place_ref[...]), grad).astype(BF16).reshape(rows_ref.shape)


def finish_kq(back, slope, history, start, cotangent, place, w_in):
    rows, width = history.shape
    return pl.pallas_call(
        finish_kq_kernel,
        in_specs=[vspec()] * 6 + [hspec()],
        out_specs=vspec(),
        scratch_shapes=weight_scratch(width),
        out_shape=jax.ShapeDtypeStruct((rows // 2, 2, width), BF16),
        compiler_params=params(DENSE),
        cost_estimate=dense_cost(rows, width, 2),
        name="finish_kq",
    )(back, slope, history, start, cotangent, place, w_in)


def body(log_rows, send_order, place, hist_len, w_in, w_out, cotangent):
    seq_size = lax.axis_size("seq")
    seq_index = lax.axis_index("seq")
    spot = seq_index % GROUP
    length = jnp.take(hist_len[0], seq_index // GROUP)
    info = jnp.stack([length, spot % 2]).astype(jnp.int32)
    same_core = [list(range(g + c, g + GROUP, 2)) for g in range(0, seq_size, GROUP) for c in (0, 1)]
    swap = [(i, i ^ 1) for i in range(seq_size)]

    def to_all(block):
        return lax.all_to_all(block, ("dp", "seq"), split_axis=0, concat_axis=0, tiled=True)

    def to_group(block, members):
        return lax.all_to_all(
            block, "seq", split_axis=0, concat_axis=0, tiled=True, axis_index_groups=members
        )

    upstream = jnp.dot(cotangent, w_out.T, preferred_element_type=F32)
    arrived = to_all(pick_rows(log_rows, send_order))
    history, normed, slope_kq, kq = project_kq(info, arrived, place, w_in, upstream)
    kq = to_group(kq, same_core)
    gate, slope_vg, vu, token = project_vu(normed, w_in, upstream)
    other_keys = lax.ppermute(first_part(kq, token), "seq", swap)
    weights, slopes, token = weigh(info, kq, other_keys, token)
    vu = to_group(vu, same_core)
    other_values = lax.ppermute(first_part(vu, token), "seq", swap)
    att, stats = attend(info, vu, other_values, weights)
    stats = to_group(stats, same_core)
    out, sib, grad_t = back_v(info, vu, att, stats, weights)
    back_vh = merge(out, lax.ppermute(sib, "seq", swap))
    out, sib = back_kq(info, kq, vu, other_values, other_keys, slopes, grad_t)
    back_vh = to_group(back_vh, same_core)
    back_kq_rows = merge(out, lax.ppermute(sib, "seq", swap))
    mixed, start = finish_vg(back_vh, gate, slope_vg, history, upstream, w_in, w_out)
    back_kq_rows = to_group(back_kq_rows, same_core)
    grads = finish_kq(back_kq_rows, slope_kq, history, start, cotangent, place, w_in)
    log_grad = unpick_rows(to_all(grads), send_order, F32)
    return (mixed, log_grad)


def solution(mesh):
    rows = P(("dp", "seq"), None)
    return jax.shard_map(
        body,
        mesh=mesh,
        in_specs=(rows, rows, rows, P("dp", None), P(), P(), rows),
        out_specs=(rows, rows),
        check_vma=False,
    )
```

time: 177 us -> 172 us (0.972)
  blocking collectives: 91.7 us -> 27.9 us
  waiting for transfers between devices: 14.8 us -> 36.9 us
  Pallas kernels: 42.7 us -> 64.4 us
  starting transfers between devices: 14.4 us -> 31.3 us
  local copies, waits for them, and re-layouts: 8.27 us -> 5.91 us
    all_to_all x3 -> x1, blocking collectives: 68.9 us -> 9.84 us  [to_group(): lax.all_to_all(block, 'seq', split_axis=0, concat_axis=0, tiled=True, axi...]
    all_to_all x0 -> x4, waiting for transfers between devices: none -> 21.8 us  [to_group(): lax.all_to_all(block, 'seq', split_axis=0, concat_axis=0, tiled=True, axi...]
    pallas_call x6 -> x12, Pallas kernels: 42.4 us -> 62.1 us  [the longest x1 13.4 us: back_kq(): pl.pallas_call(back_kq_kernel, out_shape=[jax.ShapeDtypeStruct((CHIPS, 2,...]
    all_to_all x0 -> x4, starting transfers between devices: none -> 16.7 us  [to_group(): lax.all_to_all(block, 'seq', split_axis=0, concat_axis=0, tiled=True, axi...]
    all_to_all x1, blocking collectives: 22.8 us -> 18.1 us  [to_all(): lax.all_to_all(block, ('dp', 'seq'), split_axis=0, concat_axis=0, tiled=T...]
    ppermute x2 -> x4, waiting for transfers between devices: 3.7 us -> 6.15 us  [the longest x1 1.54 us: body(): other_keys = lax.ppermute(first_part(kq, token), 'seq', swap)]
    reshape x4 -> x0, local copies, waits for them, and re-layouts: 2.38 us -> none  [the longest x2 1.19 us: to_all(): block = block.reshape(rows // 2, 2, width)]
    all_to_all x1, waiting for transfers between devices: 11.1 us -> 8.95 us  [to_all(): lax.all_to_all(block, ('dp', 'seq'), split_axis=0, concat_axis=0, tiled=T...]
  transfers between devices with their start and end apart: 3 -> 9, of which waited for: 3 -> 8; matrix products, arithmetic and copies ran while one was open for 2% -> 2% of each run, Pallas kernels for 0% -> 22%
where the time goes in v3:
time: 172 us; the launch traced here: 171 us
  Pallas kernels  64.4 us (37%)
  waiting for transfers between devices  36.9 us (21%)
  starting transfers between devices  31.3 us (18%)
  blocking collectives  27.9 us (16%)
  local copies, waits for them, and re-layouts  5.91 us (3%)
  matrix products  2.77 us (2%)
    all_to_all x4, waiting for transfers between devices, to_group(): lax.all_to_all(block, 'seq', split_axis=0, concat_axis=0, tiled=True, axi...  21.8 us
    all_to_all x1, blocking collectives, to_all(): lax.all_to_all(block, ('dp', 'seq'), split_axis=0, concat_axis=0, tiled=T...  18.1 us
    all_to_all x4, starting transfers between devices, to_group(): lax.all_to_all(block, 'seq', split_axis=0, concat_axis=0, tiled=True, axi...  16.7 us
    pallas_call x1, Pallas kernels, back_kq(): pl.pallas_call(back_kq_kernel, out_shape=[jax.ShapeDtypeStruct((CHIPS, 2,...  13.4 us
    all_to_all x1, starting transfers between devices, to_all(): lax.all_to_all(block, ('dp', 'seq'), split_axis=0, concat_axis=0, tiled=T...  11.5 us
    all_to_all x1, blocking collectives, to_group(): lax.all_to_all(block, 'seq', split_axis=0, concat_axis=0, tiled=True, axi...  9.84 us
    all_to_all x1, waiting for transfers between devices, to_all(): lax.all_to_all(block, ('dp', 'seq'), split_axis=0, concat_axis=0, tiled=T...  8.95 us
    pallas_call x1, Pallas kernels, weigh(): pl.pallas_call(weigh_kernel, out_shape=[jax.ShapeDtypeStruct((TILES, KEY_...  8.8 us
  transfers between devices with their start and end apart: 9, of which 8 were waited for; matrix products, arithmetic and copies ran while one was open for 2% of the time, Pallas kernels for 22%

profile of v3, /device:TPU:1, one launch (start us, length us, event | category | flops | bytes accessed | tf_op | source)
XLA Modules:
  0.0 171.2 jit_solution(11833635736218777821)
XLA Ops:
  0.7 1.0 copy-done.1
  2.4 1.1 pick_rows.1
  3.5 11.5 %all-to-all-start = ((bf16[128,2,1024]{2,1,0:T(2,128)(2,1)}), bf16[128,2,1024]{2,1,0:T(2,128)(2,1)S(1)}, u32[]{:S(2)}, u32[]{:S(2)}) async-start(bf16[128,2,1024]{2,1,0:T(2,128)(2,1)} %pick_rows.1), calls=%async_computation | async-start | bytes 1048576 | tf_op jit(solution)/shard_map/all_to_all | solution.py:727
  16.8 2.8 %fusion._.up_ref = f32[256,1024]{1,0:T(8,128)} fusion(bf16[256,1024]{1,0:T(8,128)(2,1)} %cot_ref.1, bf16[1024,1024]{1,0:T(8,128)(2,1)S(1)} %copy-done.8), kind=kOutput, calls=%fused_computation.2 | convolution fusion | flops 536870912 | bytes 3670016 | tf_op jit(solution)/shard_map/dot_general | solution.py:734
  19.6 9.0 %all-to-all-done.arrived_ref = bf16[128,2,1024]{2,1,0:T(2,128)(2,1)S(1)} async-done(((bf16[128,2,1024]{2,1,0:T(2,128)(2,1)}), bf16[128,2,1024]{2,1,0:T(2,128)(2,1)S(1)}, u32[]{:S(2)}, u32[]{:S(2)}) %all-to-all-start) | async-done | bytes 524320 | tf_op jit(solution)/shard_map/all_to_all | solution.py:727
  29.3 5.8 %project_kq.1 = (bf16[256,1024]{1,0:T(8,128)(2,1)}, bf16[256,1024]{1,0:T(8,128)(2,1)}, bf16[2,256,1024]{2,1,0:T(8,128)(2,1)}, bf16[8,2,256,128]{3,2,1,0:T(8,128)(2,1)}) custom-call(s32[2]{0:T(128)} %pad_add_fusion.info, bf16[128,2,1024]{2,1,0:T(2,128)(2,1)} %copy-done.10, s32[1,256]{1,0:T(1,128)} %place_ref.3, bf16[1024,4096]{1,0:T(8,128)(2,1)} %w_hbm.7, ...), custom_call_target="tpu_custom_call" | custom-call | flops 1073741824 | bytes 8388608 | tf_op jit(solution)/shard_map/project_kq/pallas_call | solution.py:204
  35.2 3.6 %all-to-all-start.2 = ((bf16[8,2,256,128]{3,2,1,0:T(8,128)(2,1)}), bf16[8,2,256,128]{3,2,1,0:T(8,128)(2,1)S(1)}, u32[]{:S(2)}, u32[]{:S(2)}) async-start(bf16[8,2,256,128]{3,2,1,0:T(8,128)(2,1)} %get-tuple-element.24), calls=%async_computation.2 | async-start | bytes 2097152 | tf_op jit(solution)/shard_map/all_to_all | solution.py:730
  38.7 6.5 %project_vu.1 = (bf16[256,1024]{1,0:T(8,128)(2,1)}, bf16[2,256,1024]{2,1,0:T(8,128)(2,1)}, bf16[8,2,256,128]{3,2,1,0:T(8,128)(2,1)}, f32[8,128]{1,0:T(8,128)}) custom-call(bf16[256,1024]{1,0:T(8,128)(2,1)} %get-tuple-element.22.normed_ref, bf16[1024,4096]{1,0:T(8,128)(2,1)} %w_hbm.7, f32[256,1024]{1,0:T(8,128)} %fusion._.up_ref), custom_call_target="tpu_custom_call" | custom-call | flops 1073741824 | bytes 8388608 | tf_op jit(solution)/shard_map/project_vu/pallas_call | solution.py:223
  45.2 9.2 %all-to-all-done.2.pair_ref.kq_ref = bf16[8,2,256,128]{3,2,1,0:T(8,128)(2,1)S(1)} async-done(((bf16[8,2,256,128]{3,2,1,0:T(8,128)(2,1)}), bf16[8,2,256,128]{3,2,1,0:T(8,128)(2,1)S(1)}, u32[]{:S(2)}, u32[]{:S(2)}) %all-to-all-start.2) | async-done | bytes 1048608 | tf_op jit(solution)/shard_map/all_to_all | solution.py:730
  54.5 3.6 %all-to-all-start.1 = ((bf16[8,2,256,128]{3,2,1,0:T(8,128)(2,1)}), bf16[8,2,256,128]{3,2,1,0:T(8,128)(2,1)S(1)}, u32[]{:S(2)}, u32[]{:S(2)}) async-start(bf16[8,2,256,128]{3,2,1,0:T(8,128)(2,1)} %get-tuple-element.23), calls=%async_computation.1 | async-start | bytes 2097152 | tf_op jit(solution)/shard_map/all_to_all | solution.py:730
  58.1 0.9 collective-permute-start
  59.0 1.5 collective-permute-done.other_ref.other_key_ref
  60.6 8.8 %weigh.1 = (bf16[36,512,256]{2,1,0:T(8,128)(2,1)}, bf16[36,512,256]{2,1,0:T(8,128)(2,1)}, f32[8,128]{1,0:T(8,128)S(1)}) custom-call(s32[2]{0:T(128)S(1)} %copy-done.2, bf16[8,2,256,128]{3,2,1,0:T(8,128)(2,1)S(1)} %all-to-all-done.2.pair_ref.kq_ref, bf16[8,256,128]{2,1,0:T(8,128)(2,1)S(1)} %collective-permute-done.other_ref.other_key_ref, f32[8,128]{1,0:T(8,128)S(1)} %copy-done.3), custom_call_target="tpu_custom_call" | custom-call | flops 2415919104 | bytes 18874368 | tf_op jit(solution)/shard_map/weigh/pallas_call | solution.py:377
  69.4 4.4 %all-to-all-done.1.pair_ref.vu_ref = bf16[8,2,256,128]{3,2,1,0:T(8,128)(2,1)S(1)} async-done(((bf16[8,2,256,128]{3,2,1,0:T(8,128)(2,1)}), bf16[8,2,256,128]{3,2,1,0:T(8,128)(2,1)S(1)}, u32[]{:S(2)}, u32[]{:S(2)}) %all-to-all-start.1) | async-done | bytes 1048608 | tf_op jit(solution)/shard_map/all_to_all | solution.py:730
  74.8 1.5 collective-permute-done.1.other_ref
  76.3 5.3 %attend.1 = (f32[128,2048]{1,0:T(8,128)S(1)}, f32[8,4,2048]{2,1,0:T(4,128)S(1)}) custom-call(s32[2]{0:T(128)S(1)} %copy-done.2, bf16[8,2,256,128]{3,2,1,0:T(8,128)(2,1)S(1)} %all-to-all-done.1.pair_ref.vu_ref, bf16[8,256,128]{2,1,0:T(8,128)(2,1)S(1)} %collective-permute-done.1.other_ref, bf16[36,512,256]{2,1,0:T(8,128)(2,1)} %get-tuple-element.27.weight_hbm), custom_call_target="tpu_custom_call" | custom-call | flops 2415919104 | bytes 18874368 | tf_op jit(solution)/shard_map/attend/pallas_call | solution.py:445
  81.6 9.8 %all_to_all.35.stats_ref = f32[8,4,2048]{2,1,0:T(4,128)S(1)} all-to-all(f32[8,4,2048]{2,1,0:T(4,128)S(1)} %get-tuple-element.29), channel_id=1, replica_groups={{0,2,4,6,8,10,12,14},{1,3,5,7,9,11,13,15},{16,18,20,22,24,26,28,30},{17..., dimensions={0} | all-to-all | bytes 524288 | tf_op jit(solution)/shard_map/all_to_all | solution.py:730
  91.4 5.7 %back_v.1 = (bf16[8,2,256,128]{3,2,1,0:T(8,128)(2,1)S(1)}, bf16[8,256,128]{2,1,0:T(8,128)(2,1)S(1)}, bf16[128,2048]{1,0:T(8,128)(2,1)S(1)}) custom-call(s32[2]{0:T(128)S(1)} %copy-done.2, bf16[8,2,256,128]{3,2,1,0:T(8,128)(2,1)S(1)} %all-to-all-done.1.pair_ref.vu_ref, f32[128,2048]{1,0:T(8,128)S(1)} %get-tuple-element.28.att_ref, ...), custom_call_target="tpu_custom_call" | custom-call | flops 2415919104 | bytes 18874368 | tf_op jit(solution)/shard_map/back_v/pallas_call | solution.py:523
  98.7 1.5 collective-permute-done.2.sib_ref
  100.3 1.1 merge.2
  101.4 4.2 %all-to-all-start.4 = ((bf16[8,2,256,128]{3,2,1,0:T(8,128)(2,1)}), bf16[8,2,256,128]{3,2,1,0:T(8,128)(2,1)}, u32[]{:S(2)}, u32[]{:S(2)}) async-start(bf16[8,2,256,128]{3,2,1,0:T(8,128)(2,1)} %merge.2), calls=%async_computation.4 | async-start | bytes 2097152 | tf_op jit(solution)/shard_map/all_to_all | solution.py:730
  105.6 1.0 copy-done.7
  106.7 13.4 %back_kq.1 = (bf16[8,2,256,128]{3,2,1,0:T(8,128)(2,1)S(1)}, bf16[8,256,128]{2,1,0:T(8,128)(2,1)S(1)}) custom-call(s32[2]{0:T(128)S(1)} %copy-done.2, bf16[8,2,256,128]{3,2,1,0:T(8,128)(2,1)S(1)} %all-to-all-done.2.pair_ref.kq_ref, bf16[8,2,256,128]{3,2,1,0:T(8,128)(2,1)S(1)} %all-to-all-done.1.pair_ref.vu_ref, ...), custom_call_target="tpu_custom_call" | custom-call | flops 7247757312 | bytes 18874368 | tf_op jit(solution)/shard_map/back_kq/pallas_call | solution.py:594
  120.5 1.5 collective-permute-done.3.sib_ref
  122.1 1.1 merge.3
  123.2 5.3 %all-to-all-start.5 = ((bf16[8,2,256,128]{3,2,1,0:T(8,128)(2,1)}), bf16[8,2,256,128]{3,2,1,0:T(8,128)(2,1)S(1)}, u32[]{:S(2)}, u32[]{:S(2)}) async-start(bf16[8,2,256,128]{3,2,1,0:T(8,128)(2,1)} %merge.3), calls=%async_computation.5 | async-start | bytes 2097152 | tf_op jit(solution)/shard_map/all_to_all | solution.py:730
  128.5 7.7 %finish_vg.1 = (bf16[256,1024]{1,0:T(8,128)(2,1)}, f32[256,1024]{1,0:T(8,128)}) custom-call(bf16[8,2,256,128]{3,2,1,0:T(8,128)(2,1)} %all-to-all-done.4.back_ref, bf16[256,1024]{1,0:T(8,128)(2,1)} %get-tuple-element.32.gate_ref, bf16[2,256,1024]{2,1,0:T(8,128)(2,1)} %get-tuple-element.33.slope_ref, bf16[256,1024]{1,0:T(8,128)(2,1)} %get-tuple-element.34.hist_ref, ...), custom_call_target="tpu_custom_call" | custom-call | flops 1610612736 | bytes 12582912 | tf_op jit(solution)/shard_map/finish_vg/pallas_call | solution.py:671
  136.2 8.2 %all-to-all-done.5.back_ref = bf16[8,2,256,128]{3,2,1,0:T(8,128)(2,1)S(1)} async-done(((bf16[8,2,256,128]{3,2,1,0:T(8,128)(2,1)}), bf16[8,2,256,128]{3,2,1,0:T(8,128)(2,1)S(1)}, u32[]{:S(2)}, u32[]{:S(2)}) %all-to-all-start.5) | async-done | bytes 1048608 | tf_op jit(solution)/shard_map/all_to_all | solution.py:730
  144.3 1.0 copy-done.9
  145.3 6.5 %finish_kq.1 = bf16[128,2,1024]{2,1,0:T(2,128)(2,1)} custom-call(bf16[8,2,256,128]{3,2,1,0:T(8,128)(2,1)} %copy-done.9, bf16[2,256,1024]{2,1,0:T(8,128)(2,1)} %get-tuple-element.40.slope_ref, bf16[256,1024]{1,0:T(8,128)(2,1)} %get-tuple-element.34.hist_ref, f32[256,1024]{1,0:T(8,128)} %get-tuple-element.41.start_ref, bf16[256,1024]{1,0:T(8,128)(2,1)} %cot_ref.1, ...), custom_call_target="tpu_custom_call" | custom-call | flops 1073741824 | bytes 8388608 | tf_op jit(solution)/shard_map/finish_kq/pallas_call | solution.py:705
  151.8 18.1 %all_to_all.36.rows_ref = bf16[128,2,1024]{2,1,0:T(2,128)(2,1)S(1)} all-to-all(bf16[128,2,1024]{2,1,0:T(2,128)(2,1)} %finish_kq.1), channel_id=1, replica_groups=mesh['dp'=4,'seq'=32] {'dp','seq'}, dimensions={0} | all-to-all | bytes 1048576 | tf_op jit(solution)/shard_map/all_to_all | solution.py:727
  169.9 1.3 unpick_rows.1
  (27 shorter events, 5.7 us)
Async XLA Ops:
  0.6 14.4 %copy-start = (s32[1,2]{1,0:T(1,128)S(1)}, s32[1,2]{1,0:T(1,128)}, u32[]{:S(2)}) copy-start(s32[1,2]{1,0:T(1,128)} %param.10) | copy-start | bytes 28
  0.6 1.0 copy-start.1
  1.7 0.7 copy-start.4
  2.4 14.4 %copy-start.8 = (bf16[1024,1024]{1,0:T(8,128)(2,1)S(1)}, bf16[1024,1024]{1,0:T(8,128)(2,1)}, u32[]{:S(2)}) copy-start(bf16[1024,1024]{1,0:T(8,128)(2,1)} %w_out_ref.1) | copy-start | bytes 6291460
  3.5 25.0 %all-to-all-start = ((bf16[128,2,1024]{2,1,0:T(2,128)(2,1)}), bf16[128,2,1024]{2,1,0:T(2,128)(2,1)S(1)}, u32[]{:S(2)}, u32[]{:S(2)}) async-start(bf16[128,2,1024]{2,1,0:T(2,128)(2,1)} %pick_rows.1), calls=%async_computation | async-start | bytes 1048576 | tf_op jit(solution)/shard_map/all_to_all | solution.py:727
  28.5 0.8 copy-start.10
  35.2 19.3 %all-to-all-start.2 = ((bf16[8,2,256,128]{3,2,1,0:T(8,128)(2,1)}), bf16[8,2,256,128]{3,2,1,0:T(8,128)(2,1)S(1)}, u32[]{:S(2)}, u32[]{:S(2)}) async-start(bf16[8,2,256,128]{3,2,1,0:T(8,128)(2,1)} %get-tuple-element.24), calls=%async_computation.2 | async-start | bytes 2097152 | tf_op jit(solution)/shard_map/all_to_all | solution.py:730
  45.2 12.8 %copy-start.3 = (f32[8,128]{1,0:T(8,128)S(1)}, f32[8,128]{1,0:T(8,128)}, u32[]{:S(2)}) copy-start(f32[8,128]{1,0:T(8,128)} %get-tuple-element.25._) | copy-start | bytes 12292
  45.2 15.3 %copy-start.2 = (s32[2]{0:T(128)S(1)}, s32[2]{0:T(128)}, u32[]{:S(2)}) copy-start(s32[2]{0:T(128)} %pad_add_fusion.info) | copy-start | bytes 28
  54.5 19.3 %all-to-all-start.1 = ((bf16[8,2,256,128]{3,2,1,0:T(8,128)(2,1)}), bf16[8,2,256,128]{3,2,1,0:T(8,128)(2,1)S(1)}, u32[]{:S(2)}, u32[]{:S(2)}) async-start(bf16[8,2,256,128]{3,2,1,0:T(8,128)(2,1)} %get-tuple-element.23), calls=%async_computation.1 | async-start | bytes 2097152 | tf_op jit(solution)/shard_map/all_to_all | solution.py:730
  58.1 2.5 %collective-permute-start = (bf16[8,256,128]{2,1,0:T(8,128)(2,1)S(1)}, bf16[8,256,128]{2,1,0:T(8,128)(2,1)S(1)}, u32[]{:S(2)}, u32[]{:S(2)}) collective-permute-start(bf16[8,256,128]{2,1,0:T(8,128)(2,1)S(1)} %first_part.2), channel_id=1, source_target_pairs={{0,1},{1,0},{2,3},{3,2},{4,5},{5,4},{6,7},{7,6},{8,9},{9,8},{10,11... | collective-permute-start | bytes 1572872 | tf_op jit(solution)/shard_map/ppermute | solution.py:739
  73.9 2.4 %collective-permute-start.1 = (bf16[8,256,128]{2,1,0:T(8,128)(2,1)S(1)}, bf16[8,256,128]{2,1,0:T(8,128)(2,1)S(1)}, u32[]{:S(2)}, u32[]{:S(2)}) collective-permute-start(bf16[8,256,128]{2,1,0:T(8,128)(2,1)S(1)} %first_part.3), channel_id=1, source_target_pairs={{0,1},{1,0},{2,3},{3,2},{4,5},{5,4},{6,7},{7,6},{8,9},{9,8},{10,11... | collective-permute-start | bytes 1572872 | tf_op jit(solution)/shard_map/ppermute | solution.py:742
  97.1 0.8 copy-start.6
  97.9 2.3 %collective-permute-start.2 = (bf16[8,256,128]{2,1,0:T(8,128)(2,1)S(1)}, bf16[8,256,128]{2,1,0:T(8,128)(2,1)S(1)}, u32[]{:S(2)}, u32[]{:S(2)}) collective-permute-start(bf16[8,256,128]{2,1,0:T(8,128)(2,1)S(1)} %get-tuple-element.31), channel_id=1, source_target_pairs={{0,1},{1,0},{2,3},{3,2},{4,5},{5,4},{6,7},{7,6},{8,9},{9,8},{10,11... | collective-permute-start | bytes 1572872 | tf_op jit(solution)/shard_map/ppermute | solution.py:746
  101.4 21.8 %all-to-all-start.4 = ((bf16[8,2,256,128]{3,2,1,0:T(8,128)(2,1)}), bf16[8,2,256,128]{3,2,1,0:T(8,128)(2,1)}, u32[]{:S(2)}, u32[]{:S(2)}) async-start(bf16[8,2,256,128]{3,2,1,0:T(8,128)(2,1)} %merge.2), calls=%async_computation.4 | async-start | bytes 2097152 | tf_op jit(solution)/shard_map/all_to_all | solution.py:730
  105.6 1.0 copy-start.7
  120.1 2.0 %collective-permute-start.3 = (bf16[8,256,128]{2,1,0:T(8,128)(2,1)S(1)}, bf16[8,256,128]{2,1,0:T(8,128)(2,1)S(1)}, u32[]{:S(2)}, u32[]{:S(2)}) collective-permute-start(bf16[8,256,128]{2,1,0:T(8,128)(2,1)S(1)} %get-tuple-element.39), channel_id=1, source_target_pairs={{0,1},{1,0},{2,3},{3,2},{4,5},{5,4},{6,7},{7,6},{8,9},{9,8},{10,11... | collective-permute-start | bytes 1572872 | tf_op jit(solution)/shard_map/ppermute | solution.py:749
  123.2 21.2 %all-to-all-start.5 = ((bf16[8,2,256,128]{3,2,1,0:T(8,128)(2,1)}), bf16[8,2,256,128]{3,2,1,0:T(8,128)(2,1)S(1)}, u32[]{:S(2)}, u32[]{:S(2)}) async-start(bf16[8,2,256,128]{3,2,1,0:T(8,128)(2,1)} %merge.3), calls=%async_computation.5 | async-start | bytes 2097152 | tf_op jit(solution)/shard_map/all_to_all | solution.py:730
  144.3 1.0 copy-start.9
  145.3 24.6 %copy-start.5 = (s32[1,256]{1,0:T(1,128)S(1)}, s32[1,256]{1,0:T(1,128)}, u32[]{:S(2)}) copy-start(s32[1,256]{1,0:T(1,128)} %order_ref.3) | copy-start | bytes 3076

commit v4 on v3

--- a/solution.py
+++ b/solution.py
@@ -83,7 +83,7 @@
         out_shape=jax.ShapeDtypeStruct((rows.shape[0] // 2, 2, rows.shape[1]), rows.dtype),
         in_specs=[vspec(), vspec()],
         out_specs=vspec(),
-        compiler_params=params(SMALL),
+        compiler_params=params(DENSE),
         name="pick_rows",
     )(rows, order)
 
@@ -191,14 +191,6 @@
     return [VMEM((count, width, CHUNK), BF16), pltpu.SemaphoreType.DMA((count,))]
 
 
-def dense_cost(rows, width, blocks):
-    return pl.CostEstimate(
-        flops=2 * rows * width * width * blocks,
-        bytes_accessed=2 * width * width * blocks + 8 * rows * width * blocks,
-        transcendentals=rows * width * blocks,
-    )
-
-
 def project_kq(info, arrived, place, w_in, upstream):
     rows, width = upstream.shape
     return pl.pallas_call(
@@ -213,7 +205,6 @@
         ],
         scratch_shapes=weight_scratch(width),
         compiler_params=params(DENSE),
-        cost_estimate=dense_cost(rows, width, 2),
         name="project_kq",
     )(info, arrived, place, w_in, upstream)
 
@@ -232,7 +223,6 @@
         ],
         scratch_shapes=weight_scratch(width),
         compiler_params=params(DENSE),
-        cost_estimate=dense_cost(rows, width, 2),
         name="project_vu",
     )(normed, w_in, upstream)
 
@@ -571,7 +561,10 @@
         arrive(j)
         for m in range(j, CHIPS):
             grad = dot(value_ref[keys_of(j), :], grad_t_ref[:, rows_of(m)])
-            grad = (grad * slope_ref[tile_of(j, m)].astype(F32)).astype(BF16)
+            slope = slope_ref[tile_of(j, m)].astype(F32)
+            slope_ref[tile_of(j, m)] = (grad * slope).astype(BF16)
+        for m in range(j, CHIPS):
+            grad = slope_ref[tile_of(j, m)]
             dk = dot(grad, kq_ref[m, 1])
             dq = dot(key_t_ref[:, keys_of(j)], grad)
             if m == j:
@@ -613,20 +606,21 @@
     )(info, kq, vu, other, other_keys, slope, grad_t)
 
 
-def merge_kernel(out_ref, sib_ref, done_ref):
+def merge_kernel(out_ref, sib_ref, *refs):
+    done_ref = refs[-1]
     done_ref[:, 0] = (out_ref[:, 0].astype(F32) + sib_ref[...].astype(F32)).astype(BF16)
     done_ref[:, 1] = out_ref[:, 1]
 
 
-def merge(out, sib):
+def merge(out, sib, *kept):
     return pl.pallas_call(
         merge_kernel,
         out_shape=jax.ShapeDtypeStruct(out.shape, out.dtype),
-        in_specs=[vspec(), vspec()],
+        in_specs=[vspec(), vspec()] + [vspec() for _ in kept],
         out_specs=vspec(),
         compiler_params=params(SMALL),
         name="merge",
-    )(out, sib)
+    )(out, sib, *kept)
 
 
 def gather(back_ref, part, chunk):
@@ -678,24 +672,56 @@
             jax.ShapeDtypeStruct((rows, width), F32),
         ],
         compiler_params=params(DENSE),
-        cost_estimate=dense_cost(rows, width, 3),
         name="finish_vg",
     )(back, gate, slope, history, upstream, w_in, w_out)
 
 
 def finish_kq_kernel(
-    back_ref, slope_ref, hist_ref, start_ref, cot_ref, place_ref, w_hbm, rows_ref, w_ref, sems
+    back_in,
+    slope_in,
+    hist_in,
+    start_in,
+    cot_in,
+    place_ref,
+    w_hbm,
+    rows_ref,
+    w_ref,
+    sems,
+    back_ref,
+    slope_ref,
+    hist_ref,
+    start_ref,
+    cot_ref,
+    in_sems,
 ):
     width = hist_ref.shape[1]
+    pairs = [
+        (hist_in, hist_ref),
+        (back_in, back_ref),
+        (slope_in, slope_ref),
+        (start_in, start_ref),
+        (cot_in, cot_ref),
+    ]
+    copies = [pltpu.make_async_copy(a, b, in_sems.at[i]) for i, (a, b) in enumerate(pairs)]
+    for copy in copies[:3]:
+        copy.start()
     arrive = start_weights(w_hbm, w_ref, sems, (3, 2))
+    for copy in copies[3:]:
+        copy.start()
+    copies[0].wait()
     hat, inverse = normalize(hist_ref[...].astype(F32))
-    grad = start_ref[...]
+    copies[1].wait()
+    copies[2].wait()
+    grad = jnp.zeros(hist_ref.shape, F32)
     for part in range(2):
         for chunk, columns in chunks(width):
             pre = gather(back_ref, part, chunk) * slope_ref[part, :, columns].astype(F32)
             arrive(part, chunk)
             grad = grad + dot_nt(pre.astype(BF16), w_ref[part * (width // CHUNK) + chunk])
+    copies[3].wait()
+    grad = grad + start_ref[...]
     grad = inverse * (grad - row_mean(grad) - hat * row_mean(grad * hat))
+    copies[4].wait()
     grad = (grad + cot_ref[...].astype(F32)).astype(BF16)
     rows_ref[...] = dot(onehot(place_ref[...]), grad).astype(BF16).reshape(rows_ref.shape)
 
@@ -704,12 +730,19 @@
     rows, width = history.shape
     return pl.pallas_call(
         finish_kq_kernel,
-        in_specs=[vspec()] * 6 + [hspec()],
+        in_specs=[hspec()] * 5 + [vspec(), hspec()],
         out_specs=vspec(),
-        scratch_shapes=weight_scratch(width),
+        scratch_shapes=weight_scratch(width)
+        + [
+            VMEM((CHIPS, 2, ROWS, HEAD_DIM), BF16),
+            VMEM((2, rows, width), BF16),
+            VMEM((rows, width), BF16),
+            VMEM((rows, width), F32),
+            VMEM((rows, width), BF16),
+            pltpu.SemaphoreType.DMA((5,)),
+        ],
         out_shape=jax.ShapeDtypeStruct((rows // 2, 2, width), BF16),
         compiler_params=params(DENSE),
-        cost_estimate=dense_cost(rows, width, 2),
         name="finish_kq",
     )(back, slope, history, start, cotangent, place, w_in)
 
@@ -743,7 +776,7 @@
     att, stats = attend(info, vu, other_values, weights)
     stats = to_group(stats, same_core)
     out, sib, grad_t = back_v(info, vu, att, stats, weights)
-    back_vh = merge(out, lax.ppermute(sib, "seq", swap))
+    back_vh = merge(out, lax.ppermute(sib, "seq", swap), grad_t)
     out, sib = back_kq(info, kq, vu, other_values, other_keys, slopes, grad_t)
     back_vh = to_group(back_vh, same_core)
     back_kq_rows = merge(out, lax.ppermute(sib, "seq", swap))

time: 172 us -> 167 us (0.971)
  Pallas kernels: 64.4 us -> 60.1 us
  waiting for transfers between devices: 36.9 us -> 39.2 us
    pallas_call x1, Pallas kernels: 13.4 us -> 8.88 us  [back_kq(): pl.pallas_call(back_kq_kernel, out_shape=[jax.ShapeDtypeStruct((CHIPS, 2,...]
    all_to_all x4, waiting for transfers between devices: 21.8 us -> 24.3 us  [to_group(): lax.all_to_all(block, 'seq', split_axis=0, concat_axis=0, tiled=True, axi...]
    all_to_all x4, starting transfers between devices: 16.7 us -> 14.9 us  [to_group(): lax.all_to_all(block, 'seq', split_axis=0, concat_axis=0, tiled=True, axi...]
    unnamed x22 -> x18, local copies, waits for them, and re-layouts: 5.33 us -> 3.62 us
  transfers between devices with their start and end apart: 9 -> 9, of which waited for: 8 -> 9; matrix products, arithmetic and copies ran while one was open for 2% -> 2% of each run, Pallas kernels for 22% -> 20%
where the time goes in v4:
time: 167 us; the launch traced here: 166 us
  Pallas kernels  60.1 us (36%)
  waiting for transfers between devices  39.2 us (23%)
  starting transfers between devices  29.6 us (18%)
  blocking collectives  28 us (17%)
  local copies, waits for them, and re-layouts  4.24 us (3%)
  matrix products  2.77 us (2%)
    all_to_all x4, waiting for transfers between devices, to_group(): lax.all_to_all(block, 'seq', split_axis=0, concat_axis=0, tiled=True, axi...  24.3 us
    all_to_all x1, blocking collectives, to_all(): lax.all_to_all(block, ('dp', 'seq'), split_axis=0, concat_axis=0, tiled=T...  18.1 us
    all_to_all x4, starting transfers between devices, to_group(): lax.all_to_all(block, 'seq', split_axis=0, concat_axis=0, tiled=True, axi...  14.9 us
    all_to_all x1, starting transfers between devices, to_all(): lax.all_to_all(block, ('dp', 'seq'), split_axis=0, concat_axis=0, tiled=T...  11.5 us
    all_to_all x1, blocking collectives, to_group(): lax.all_to_all(block, 'seq', split_axis=0, concat_axis=0, tiled=True, axi...  9.84 us
    pallas_call x1, Pallas kernels, back_kq(): pl.pallas_call(back_kq_kernel, out_shape=[jax.ShapeDtypeStruct((CHIPS, 2,...  8.88 us
    all_to_all x1, waiting for transfers between devices, to_all(): lax.all_to_all(block, ('dp', 'seq'), split_axis=0, concat_axis=0, tiled=T...  8.8 us
    pallas_call x1, Pallas kernels, weigh(): pl.pallas_call(weigh_kernel, out_shape=[jax.ShapeDtypeStruct((TILES, KEY_...  8.39 us
  transfers between devices with their start and end apart: 9, of which 9 were waited for; matrix products, arithmetic and copies ran while one was open for 2% of the time, Pallas kernels for 20%

profile of v4, /device:TPU:1, one launch (start us, length us, event | category | flops | bytes accessed | tf_op | source)
XLA Modules:
  0.0 166.0 jit_solution(1780535758456382764)
XLA Ops:
  0.7 2.3 %pick_rows.1 = bf16[128,2,1024]{2,1,0:T(2,128)(2,1)} custom-call(bf16[256,1024]{1,0:T(8,128)(2,1)} %rows_ref.1, s32[1,256]{1,0:T(1,128)} %order_ref.3), custom_call_target="tpu_custom_call" | custom-call | tf_op jit(solution)/shard_map/pick_rows/pallas_call | solution.py:81
  3.0 11.5 %all-to-all-start = ((bf16[128,2,1024]{2,1,0:T(2,128)(2,1)}), bf16[128,2,1024]{2,1,0:T(2,128)(2,1)S(1)}, u32[]{:S(2)}, u32[]{:S(2)}) async-start(bf16[128,2,1024]{2,1,0:T(2,128)(2,1)} %pick_rows.1), calls=%async_computation | async-start | bytes 1048576 | tf_op jit(solution)/shard_map/all_to_all | solution.py:760
  16.4 2.8 %fusion._.up_ref = f32[256,1024]{1,0:T(8,128)} fusion(bf16[256,1024]{1,0:T(8,128)(2,1)} %cot_in.1, bf16[1024,1024]{1,0:T(8,128)(2,1)S(1)} %copy-done.6), kind=kOutput, calls=%fused_computation.2 | convolution fusion | flops 536870912 | bytes 3670016 | tf_op jit(solution)/shard_map/dot_general | solution.py:767
  19.2 8.8 %all-to-all-done.arrived_ref = bf16[128,2,1024]{2,1,0:T(2,128)(2,1)S(1)} async-done(((bf16[128,2,1024]{2,1,0:T(2,128)(2,1)}), bf16[128,2,1024]{2,1,0:T(2,128)(2,1)S(1)}, u32[]{:S(2)}, u32[]{:S(2)}) %all-to-all-start) | async-done | bytes 524320 | tf_op jit(solution)/shard_map/all_to_all | solution.py:760
  28.8 5.8 %project_kq.1 = (bf16[256,1024]{1,0:T(8,128)(2,1)}, bf16[256,1024]{1,0:T(8,128)(2,1)}, bf16[2,256,1024]{2,1,0:T(8,128)(2,1)}, bf16[8,2,256,128]{3,2,1,0:T(8,128)(2,1)}) custom-call(s32[2]{0:T(128)} %pad_add_fusion.info, bf16[128,2,1024]{2,1,0:T(2,128)(2,1)} %copy-done.8, s32[1,256]{1,0:T(1,128)} %place_ref.3, bf16[1024,4096]{1,0:T(8,128)(2,1)} %w_hbm.7, ...), custom_call_target="tpu_custom_call" | custom-call | tf_op jit(solution)/shard_map/project_kq/pallas_call | solution.py:196
  34.6 3.6 %all-to-all-start.2 = ((bf16[8,2,256,128]{3,2,1,0:T(8,128)(2,1)}), bf16[8,2,256,128]{3,2,1,0:T(8,128)(2,1)S(1)}, u32[]{:S(2)}, u32[]{:S(2)}) async-start(bf16[8,2,256,128]{3,2,1,0:T(8,128)(2,1)} %get-tuple-element.24), calls=%async_computation.2 | async-start | bytes 2097152 | tf_op jit(solution)/shard_map/all_to_all | solution.py:763
  38.2 6.5 %project_vu.1 = (bf16[256,1024]{1,0:T(8,128)(2,1)}, bf16[2,256,1024]{2,1,0:T(8,128)(2,1)}, bf16[8,2,256,128]{3,2,1,0:T(8,128)(2,1)}, f32[8,128]{1,0:T(8,128)}) custom-call(bf16[256,1024]{1,0:T(8,128)(2,1)} %get-tuple-element.22.normed_ref, bf16[1024,4096]{1,0:T(8,128)(2,1)} %w_hbm.7, f32[256,1024]{1,0:T(8,128)} %fusion._.up_ref), custom_call_target="tpu_custom_call" | custom-call | tf_op jit(solution)/shard_map/project_vu/pallas_call | solution.py:214
  44.7 9.2 %all-to-all-done.2.pair_ref.kq_ref = bf16[8,2,256,128]{3,2,1,0:T(8,128)(2,1)S(1)} async-done(((bf16[8,2,256,128]{3,2,1,0:T(8,128)(2,1)}), bf16[8,2,256,128]{3,2,1,0:T(8,128)(2,1)S(1)}, u32[]{:S(2)}, u32[]{:S(2)}) %all-to-all-start.2) | async-done | bytes 1048608 | tf_op jit(solution)/shard_map/all_to_all | solution.py:763
  54.0 3.6 %all-to-all-start.1 = ((bf16[8,2,256,128]{3,2,1,0:T(8,128)(2,1)}), bf16[8,2,256,128]{3,2,1,0:T(8,128)(2,1)S(1)}, u32[]{:S(2)}, u32[]{:S(2)}) async-start(bf16[8,2,256,128]{3,2,1,0:T(8,128)(2,1)} %get-tuple-element.23), calls=%async_computation.1 | async-start | bytes 2097152 | tf_op jit(solution)/shard_map/all_to_all | solution.py:763
  57.6 0.9 collective-permute-start
  58.5 1.5 collective-permute-done.other_ref.other_key_ref
  60.0 8.4 %weigh.1 = (bf16[36,512,256]{2,1,0:T(8,128)(2,1)}, bf16[36,512,256]{2,1,0:T(8,128)(2,1)}, f32[8,128]{1,0:T(8,128)S(1)}) custom-call(s32[2]{0:T(128)S(1)} %copy-done.1, bf16[8,2,256,128]{3,2,1,0:T(8,128)(2,1)S(1)} %all-to-all-done.2.pair_ref.kq_ref, bf16[8,256,128]{2,1,0:T(8,128)(2,1)S(1)} %collective-permute-done.other_ref.other_key_ref, f32[8,128]{1,0:T(8,128)S(1)} %copy-done.2), custom_call_target="tpu_custom_call" | custom-call | flops 2415919104 | bytes 18874368 | tf_op jit(solution)/shard_map/weigh/pallas_call | solution.py:367
  69.2 4.1 %all-to-all-done.1.pair_ref.vu_ref = bf16[8,2,256,128]{3,2,1,0:T(8,128)(2,1)S(1)} async-done(((bf16[8,2,256,128]{3,2,1,0:T(8,128)(2,1)}), bf16[8,2,256,128]{3,2,1,0:T(8,128)(2,1)S(1)}, u32[]{:S(2)}, u32[]{:S(2)}) %all-to-all-start.1) | async-done | bytes 1048608 | tf_op jit(solution)/shard_map/all_to_all | solution.py:763
  74.2 1.5 collective-permute-done.1.other_ref
  75.8 5.0 %attend.1 = (f32[128,2048]{1,0:T(8,128)S(1)}, f32[8,4,2048]{2,1,0:T(4,128)S(1)}) custom-call(s32[2]{0:T(128)S(1)} %copy-done.1, bf16[8,2,256,128]{3,2,1,0:T(8,128)(2,1)S(1)} %all-to-all-done.1.pair_ref.vu_ref, bf16[8,256,128]{2,1,0:T(8,128)(2,1)S(1)} %collective-permute-done.1.other_ref, bf16[36,512,256]{2,1,0:T(8,128)(2,1)} %get-tuple-element.27.weight_hbm), custom_call_target="tpu_custom_call" | custom-call | flops 2415919104 | bytes 18874368 | tf_op jit(solution)/shard_map/attend/pallas_call | solution.py:435
  80.8 9.8 %all_to_all.35.stats_ref = f32[8,4,2048]{2,1,0:T(4,128)S(1)} all-to-all(f32[8,4,2048]{2,1,0:T(4,128)S(1)} %get-tuple-element.29), channel_id=1, replica_groups={{0,2,4,6,8,10,12,14},{1,3,5,7,9,11,13,15},{16,18,20,22,24,26,28,30},{17..., dimensions={0} | all-to-all | bytes 524288 | tf_op jit(solution)/shard_map/all_to_all | solution.py:763
  90.7 5.7 %back_v.1 = (bf16[8,2,256,128]{3,2,1,0:T(8,128)(2,1)S(1)}, bf16[8,256,128]{2,1,0:T(8,128)(2,1)S(1)}, bf16[128,2048]{1,0:T(8,128)(2,1)S(1)}) custom-call(s32[2]{0:T(128)S(1)} %copy-done.1, bf16[8,2,256,128]{3,2,1,0:T(8,128)(2,1)S(1)} %all-to-all-done.1.pair_ref.vu_ref, f32[128,2048]{1,0:T(8,128)S(1)} %get-tuple-element.28.att_ref, ...), custom_call_target="tpu_custom_call" | custom-call | flops 2415919104 | bytes 18874368 | tf_op jit(solution)/shard_map/back_v/pallas_call | solution.py:513
  97.2 1.5 collective-permute-done.2.sib_ref
  98.8 1.1 merge.2
  99.9 4.2 %all-to-all-start.4 = ((bf16[8,2,256,128]{3,2,1,0:T(8,128)(2,1)}), bf16[8,2,256,128]{3,2,1,0:T(8,128)(2,1)}, u32[]{:S(2)}, u32[]{:S(2)}) async-start(bf16[8,2,256,128]{3,2,1,0:T(8,128)(2,1)} %merge.2), calls=%async_computation.4 | async-start | bytes 2097152 | tf_op jit(solution)/shard_map/all_to_all | solution.py:763
  104.1 1.0 copy-done.5
  105.2 8.9 %back_kq.1 = (bf16[8,2,256,128]{3,2,1,0:T(8,128)(2,1)S(1)}, bf16[8,256,128]{2,1,0:T(8,128)(2,1)S(1)}) custom-call(s32[2]{0:T(128)S(1)} %copy-done.1, bf16[8,2,256,128]{3,2,1,0:T(8,128)(2,1)S(1)} %all-to-all-done.2.pair_ref.kq_ref, bf16[8,2,256,128]{3,2,1,0:T(8,128)(2,1)S(1)} %all-to-all-done.1.pair_ref.vu_ref, ...), custom_call_target="tpu_custom_call" | custom-call | flops 7247757312 | bytes 18874368 | tf_op jit(solution)/shard_map/back_kq/pallas_call | solution.py:587
  114.5 1.5 collective-permute-done.3.sib_ref
  116.0 1.1 merge.3
  117.1 2.9 %all-to-all-done.4.back_ref = bf16[8,2,256,128]{3,2,1,0:T(8,128)(2,1)} async-done(((bf16[8,2,256,128]{3,2,1,0:T(8,128)(2,1)}), bf16[8,2,256,128]{3,2,1,0:T(8,128)(2,1)}, u32[]{:S(2)}, u32[]{:S(2)}) %all-to-all-start.4) | async-done | bytes 1048608 | tf_op jit(solution)/shard_map/all_to_all | solution.py:763
  120.0 3.6 %all-to-all-start.5 = ((bf16[8,2,256,128]{3,2,1,0:T(8,128)(2,1)}), bf16[8,2,256,128]{3,2,1,0:T(8,128)(2,1)S(1)}, u32[]{:S(2)}, u32[]{:S(2)}) async-start(bf16[8,2,256,128]{3,2,1,0:T(8,128)(2,1)} %merge.3), calls=%async_computation.5 | async-start | bytes 2097152 | tf_op jit(solution)/shard_map/all_to_all | solution.py:763
  123.6 7.7 %finish_vg.1 = (bf16[256,1024]{1,0:T(8,128)(2,1)}, f32[256,1024]{1,0:T(8,128)}) custom-call(bf16[8,2,256,128]{3,2,1,0:T(8,128)(2,1)} %all-to-all-done.4.back_ref, bf16[256,1024]{1,0:T(8,128)(2,1)} %get-tuple-element.33.gate_ref, bf16[2,256,1024]{2,1,0:T(8,128)(2,1)} %get-tuple-element.34.slope_ref, bf16[256,1024]{1,0:T(8,128)(2,1)} %get-tuple-element.35.hist_ref.hist_in, ...), custom_call_target="tpu_custom_call" | custom-call | tf_op jit(solution)/shard_map/finish_vg/pallas_call | solution.py:665
  131.3 8.1 %all-to-all-done.5.back_in = bf16[8,2,256,128]{3,2,1,0:T(8,128)(2,1)S(1)} async-done(((bf16[8,2,256,128]{3,2,1,0:T(8,128)(2,1)}), bf16[8,2,256,128]{3,2,1,0:T(8,128)(2,1)S(1)}, u32[]{:S(2)}, u32[]{:S(2)}) %all-to-all-start.5) | async-done | bytes 1048608 | tf_op jit(solution)/shard_map/all_to_all | solution.py:763
  139.4 1.0 copy-done.7
  140.3 6.2 %finish_kq.1 = bf16[128,2,1024]{2,1,0:T(2,128)(2,1)} custom-call(bf16[8,2,256,128]{3,2,1,0:T(8,128)(2,1)} %copy-done.7, bf16[2,256,1024]{2,1,0:T(8,128)(2,1)} %get-tuple-element.40.slope_in, bf16[256,1024]{1,0:T(8,128)(2,1)} %get-tuple-element.35.hist_ref.hist_in, f32[256,1024]{1,0:T(8,128)} %get-tuple-element.41.start_in, bf16[256,1024]{1,0:T(8,128)(2,1)} %cot_in.1, ...), custom_call_target="tpu_custom_call" | custom-call | tf_op jit(solution)/shard_map/finish_kq/pallas_call | solution.py:731
  146.6 18.1 %all_to_all.36.rows_ref = bf16[128,2,1024]{2,1,0:T(2,128)(2,1)S(1)} all-to-all(bf16[128,2,1024]{2,1,0:T(2,128)(2,1)} %finish_kq.1), channel_id=1, replica_groups=mesh['dp'=4,'seq'=32] {'dp','seq'}, dimensions={0} | all-to-all | bytes 1048576 | tf_op jit(solution)/shard_map/all_to_all | solution.py:760
  164.7 1.3 unpick_rows.1
  (23 shorter events, 5.2 us)
Async XLA Ops:
  0.6 13.9 %copy-start = (s32[1,2]{1,0:T(1,128)S(1)}, s32[1,2]{1,0:T(1,128)}, u32[]{:S(2)}) copy-start(s32[1,2]{1,0:T(1,128)} %param.10) | copy-start | bytes 28
  0.6 15.8 %copy-start.6 = (bf16[1024,1024]{1,0:T(8,128)(2,1)S(1)}, bf16[1024,1024]{1,0:T(8,128)(2,1)}, u32[]{:S(2)}) copy-start(bf16[1024,1024]{1,0:T(8,128)(2,1)} %w_out_ref.1) | copy-start | bytes 6291460
  3.0 25.0 %all-to-all-start = ((bf16[128,2,1024]{2,1,0:T(2,128)(2,1)}), bf16[128,2,1024]{2,1,0:T(2,128)(2,1)S(1)}, u32[]{:S(2)}, u32[]{:S(2)}) async-start(bf16[128,2,1024]{2,1,0:T(2,128)(2,1)} %pick_rows.1), calls=%async_computation | async-start | bytes 1048576 | tf_op jit(solution)/shard_map/all_to_all | solution.py:760
  28.0 0.8 copy-start.8
  34.6 19.3 %all-to-all-start.2 = ((bf16[8,2,256,128]{3,2,1,0:T(8,128)(2,1)}), bf16[8,2,256,128]{3,2,1,0:T(8,128)(2,1)S(1)}, u32[]{:S(2)}, u32[]{:S(2)}) async-start(bf16[8,2,256,128]{3,2,1,0:T(8,128)(2,1)} %get-tuple-element.24), calls=%async_computation.2 | async-start | bytes 2097152 | tf_op jit(solution)/shard_map/all_to_all | solution.py:763
  44.7 12.8 %copy-start.2 = (f32[8,128]{1,0:T(8,128)S(1)}, f32[8,128]{1,0:T(8,128)}, u32[]{:S(2)}) copy-start(f32[8,128]{1,0:T(8,128)} %get-tuple-element.25._) | copy-start | bytes 12292
  44.7 15.3 %copy-start.1 = (s32[2]{0:T(128)S(1)}, s32[2]{0:T(128)}, u32[]{:S(2)}) copy-start(s32[2]{0:T(128)} %pad_add_fusion.info) | copy-start | bytes 28
  54.0 19.3 %all-to-all-start.1 = ((bf16[8,2,256,128]{3,2,1,0:T(8,128)(2,1)}), bf16[8,2,256,128]{3,2,1,0:T(8,128)(2,1)S(1)}, u32[]{:S(2)}, u32[]{:S(2)}) async-start(bf16[8,2,256,128]{3,2,1,0:T(8,128)(2,1)} %get-tuple-element.23), calls=%async_computation.1 | async-start | bytes 2097152 | tf_op jit(solution)/shard_map/all_to_all | solution.py:763
  57.6 2.5 %collective-permute-start = (bf16[8,256,128]{2,1,0:T(8,128)(2,1)S(1)}, bf16[8,256,128]{2,1,0:T(8,128)(2,1)S(1)}, u32[]{:S(2)}, u32[]{:S(2)}) collective-permute-start(bf16[8,256,128]{2,1,0:T(8,128)(2,1)S(1)} %first_part.2), channel_id=1, source_target_pairs={{0,1},{1,0},{2,3},{3,2},{4,5},{5,4},{6,7},{7,6},{8,9},{9,8},{10,11... | collective-permute-start | bytes 1572872 | tf_op jit(solution)/shard_map/ppermute | solution.py:772
  68.4 0.8 copy-start.4
  73.3 2.4 %collective-permute-start.1 = (bf16[8,256,128]{2,1,0:T(8,128)(2,1)S(1)}, bf16[8,256,128]{2,1,0:T(8,128)(2,1)S(1)}, u32[]{:S(2)}, u32[]{:S(2)}) collective-permute-start(bf16[8,256,128]{2,1,0:T(8,128)(2,1)S(1)} %first_part.3), channel_id=1, source_target_pairs={{0,1},{1,0},{2,3},{3,2},{4,5},{5,4},{6,7},{7,6},{8,9},{9,8},{10,11... | collective-permute-start | bytes 1572872 | tf_op jit(solution)/shard_map/ppermute | solution.py:775
  96.3 2.4 %collective-permute-start.2 = (bf16[8,256,128]{2,1,0:T(8,128)(2,1)S(1)}, bf16[8,256,128]{2,1,0:T(8,128)(2,1)S(1)}, u32[]{:S(2)}, u32[]{:S(2)}) collective-permute-start(bf16[8,256,128]{2,1,0:T(8,128)(2,1)S(1)} %get-tuple-element.31), channel_id=1, source_target_pairs={{0,1},{1,0},{2,3},{3,2},{4,5},{5,4},{6,7},{7,6},{8,9},{9,8},{10,11... | collective-permute-start | bytes 1572872 | tf_op jit(solution)/shard_map/ppermute | solution.py:779
  99.9 20.2 %all-to-all-start.4 = ((bf16[8,2,256,128]{3,2,1,0:T(8,128)(2,1)}), bf16[8,2,256,128]{3,2,1,0:T(8,128)(2,1)}, u32[]{:S(2)}, u32[]{:S(2)}) async-start(bf16[8,2,256,128]{3,2,1,0:T(8,128)(2,1)} %merge.2), calls=%async_computation.4 | async-start | bytes 2097152 | tf_op jit(solution)/shard_map/all_to_all | solution.py:763
  104.1 1.0 copy-start.5
  114.0 2.0 %collective-permute-start.3 = (bf16[8,256,128]{2,1,0:T(8,128)(2,1)S(1)}, bf16[8,256,128]{2,1,0:T(8,128)(2,1)S(1)}, u32[]{:S(2)}, u32[]{:S(2)}) collective-permute-start(bf16[8,256,128]{2,1,0:T(8,128)(2,1)S(1)} %get-tuple-element.39), channel_id=1, source_target_pairs={{0,1},{1,0},{2,3},{3,2},{4,5},{5,4},{6,7},{7,6},{8,9},{9,8},{10,11... | collective-permute-start | bytes 1572872 | tf_op jit(solution)/shard_map/ppermute | solution.py:782
  120.0 19.3 %all-to-all-start.5 = ((bf16[8,2,256,128]{3,2,1,0:T(8,128)(2,1)}), bf16[8,2,256,128]{3,2,1,0:T(8,128)(2,1)S(1)}, u32[]{:S(2)}, u32[]{:S(2)}) async-start(bf16[8,2,256,128]{3,2,1,0:T(8,128)(2,1)} %merge.3), calls=%async_computation.5 | async-start | bytes 2097152 | tf_op jit(solution)/shard_map/all_to_all | solution.py:763
  139.4 1.0 copy-start.7
  140.3 24.4 %copy-start.3 = (s32[1,256]{1,0:T(1,128)S(1)}, s32[1,256]{1,0:T(1,128)}, u32[]{:S(2)}) copy-start(s32[1,256]{1,0:T(1,128)} %order_ref.3) | copy-start | bytes 3076

commit v5 on v4

--- a/solution.py
+++ b/solution.py
@@ -327,7 +327,7 @@
 
     lay_rows(info, kq_ref, other_ref, key_ref)
     for m in range(CHIPS):
-        query_t_ref[:, rows_of(m)] = (kq_ref[m, 1].astype(F32) * SCALE).T.astype(BF16)
+        query_t_ref[:, rows_of(m)] = (kq_ref[m, 1].astype(F32) * SCALE).astype(BF16).T
 
     def work(j):
         for m in range(j, CHIPS):
@@ -414,7 +414,7 @@
     each_tile(length, work)
     for m in range(CHIPS):
         att = att_ref[:, rows_of(m)]
-        up = vu_ref[m, 1].astype(F32).T
+        up = vu_ref[m, 1].T.astype(F32)
         mean = jnp.mean(att, axis=0, keepdims=True)
         centred = att - mean
         stats = jnp.concatenate(
@@ -477,12 +477,13 @@
     cross = sum(row[3] + (row[0] - mean) * row[2] for row in stat) * inverse * (1.0 / width)
     for m in range(CHIPS):
         where = rows_of(m)
-        up = vu_ref[m, 1].astype(F32).T
+        up = vu_ref[m, 1].T.astype(F32)
         hat = (att_ref[:, where] - mean[:, where]) * inverse[:, where]
-        out_ref[m, 1] = hat.T.astype(BF16)
+        out_ref[m, 1] = hat.astype(BF16).T
         grad = inverse[:, where] * (up - up_mean[:, where] - hat * cross[:, where])
-        grad_t_ref[:, where] = grad.astype(BF16)
-        grad_ref[where, :] = grad.T.astype(BF16)
+        grad = grad.astype(BF16)
+        grad_t_ref[:, where] = grad
+        grad_ref[where, :] = grad.T
 
     def work(j):
         arrive(j)
@@ -578,7 +579,7 @@
 
     each_tile(length, work, dead)
     for m in range(CHIPS):
-        out_ref[m, 1] = (dq_ref[:, rows_of(m)].T * SCALE).astype(BF16)
+        out_ref[m, 1] = (dq_ref[:, rows_of(m)] * SCALE).astype(BF16).T
     share(core, dk_ref, SCALE, out_ref, sib_ref)
 
 

time: 167 us -> 166 us (level)
  no operation moved by 1% of the time
where the time goes in v5:
time: 166 us
  Pallas kernels  59.7 us (36%)
  waiting for transfers between devices  39.3 us (24%)
  starting transfers between devices  29.6 us (18%)
  blocking collectives  28 us (17%)
  local copies, waits for them, and re-layouts  4.24 us (3%)
  matrix products  2.77 us (2%)
    all_to_all x4, waiting for transfers between devices, to_group(): lax.all_to_all(block, 'seq', split_axis=0, concat_axis=0, tiled=True, axi...  24.4 us
    all_to_all x1, blocking collectives, to_all(): lax.all_to_all(block, ('dp', 'seq'), split_axis=0, concat_axis=0, tiled=T...  18.1 us
    all_to_all x4, starting transfers between devices, to_group(): lax.all_to_all(block, 'seq', split_axis=0, concat_axis=0, tiled=True, axi...  14.9 us
    all_to_all x1, starting transfers between devices, to_all(): lax.all_to_all(block, ('dp', 'seq'), split_axis=0, concat_axis=0, tiled=T...  11.5 us
    all_to_all x1, blocking collectives, to_group(): lax.all_to_all(block, 'seq', split_axis=0, concat_axis=0, tiled=True, axi...  9.84 us
    pallas_call x1, Pallas kernels, back_kq(): pl.pallas_call(back_kq_kernel, out_shape=[jax.ShapeDtypeStruct((CHIPS, 2,...  8.88 us
    all_to_all x1, waiting for transfers between devices, to_all(): lax.all_to_all(block, ('dp', 'seq'), split_axis=0, concat_axis=0, tiled=T...  8.8 us
    pallas_call x1, Pallas kernels, weigh(): pl.pallas_call(weigh_kernel, out_shape=[jax.ShapeDtypeStruct((TILES, KEY_...  8.3 us
  transfers between devices with their start and end apart: 9, of which 9 were waited for; matrix products, arithmetic and copies ran while one was open for 2% of the time, Pallas kernels for 20%

profile of v5, /device:TPU:1, one launch (start us, length us, event | category | flops | bytes accessed | tf_op | source)
XLA Modules:
  0.0 165.7 jit_solution(3389436893597384890)
XLA Ops:
  0.7 2.3 %pick_rows.1 = bf16[128,2,1024]{2,1,0:T(2,128)(2,1)} custom-call(bf16[256,1024]{1,0:T(8,128)(2,1)} %rows_ref.1, s32[1,256]{1,0:T(1,128)} %order_ref.3), custom_call_target="tpu_custom_call" | custom-call | tf_op jit(solution)/shard_map/pick_rows/pallas_call | solution.py:81
  3.0 11.5 %all-to-all-start = ((bf16[128,2,1024]{2,1,0:T(2,128)(2,1)}), bf16[128,2,1024]{2,1,0:T(2,128)(2,1)S(1)}, u32[]{:S(2)}, u32[]{:S(2)}) async-start(bf16[128,2,1024]{2,1,0:T(2,128)(2,1)} %pick_rows.1), calls=%async_computation | async-start | bytes 1048576 | tf_op jit(solution)/shard_map/all_to_all | solution.py:761
  16.4 2.8 %fusion._.up_ref = f32[256,1024]{1,0:T(8,128)} fusion(bf16[256,1024]{1,0:T(8,128)(2,1)} %cot_in.1, bf16[1024,1024]{1,0:T(8,128)(2,1)S(1)} %copy-done.6), kind=kOutput, calls=%fused_computation.2 | convolution fusion | flops 536870912 | bytes 3670016 | tf_op jit(solution)/shard_map/dot_general | solution.py:768
  19.2 8.8 %all-to-all-done.arrived_ref = bf16[128,2,1024]{2,1,0:T(2,128)(2,1)S(1)} async-done(((bf16[128,2,1024]{2,1,0:T(2,128)(2,1)}), bf16[128,2,1024]{2,1,0:T(2,128)(2,1)S(1)}, u32[]{:S(2)}, u32[]{:S(2)}) %all-to-all-start) | async-done | bytes 524320 | tf_op jit(solution)/shard_map/all_to_all | solution.py:761
  28.8 5.8 %project_kq.1 = (bf16[256,1024]{1,0:T(8,128)(2,1)}, bf16[256,1024]{1,0:T(8,128)(2,1)}, bf16[2,256,1024]{2,1,0:T(8,128)(2,1)}, bf16[8,2,256,128]{3,2,1,0:T(8,128)(2,1)}) custom-call(s32[2]{0:T(128)} %pad_add_fusion.info, bf16[128,2,1024]{2,1,0:T(2,128)(2,1)} %copy-done.8, s32[1,256]{1,0:T(1,128)} %place_ref.3, bf16[1024,4096]{1,0:T(8,128)(2,1)} %w_hbm.7, ...), custom_call_target="tpu_custom_call" | custom-call | tf_op jit(solution)/shard_map/project_kq/pallas_call | solution.py:196
  34.6 3.6 %all-to-all-start.2 = ((bf16[8,2,256,128]{3,2,1,0:T(8,128)(2,1)}), bf16[8,2,256,128]{3,2,1,0:T(8,128)(2,1)S(1)}, u32[]{:S(2)}, u32[]{:S(2)}) async-start(bf16[8,2,256,128]{3,2,1,0:T(8,128)(2,1)} %get-tuple-element.24), calls=%async_computation.2 | async-start | bytes 2097152 | tf_op jit(solution)/shard_map/all_to_all | solution.py:764
  38.2 6.5 %project_vu.1 = (bf16[256,1024]{1,0:T(8,128)(2,1)}, bf16[2,256,1024]{2,1,0:T(8,128)(2,1)}, bf16[8,2,256,128]{3,2,1,0:T(8,128)(2,1)}, f32[8,128]{1,0:T(8,128)}) custom-call(bf16[256,1024]{1,0:T(8,128)(2,1)} %get-tuple-element.22.normed_ref, bf16[1024,4096]{1,0:T(8,128)(2,1)} %w_hbm.7, f32[256,1024]{1,0:T(8,128)} %fusion._.up_ref), custom_call_target="tpu_custom_call" | custom-call | tf_op jit(solution)/shard_map/project_vu/pallas_call | solution.py:214
  44.7 9.2 %all-to-all-done.2.pair_ref.kq_ref = bf16[8,2,256,128]{3,2,1,0:T(8,128)(2,1)S(1)} async-done(((bf16[8,2,256,128]{3,2,1,0:T(8,128)(2,1)}), bf16[8,2,256,128]{3,2,1,0:T(8,128)(2,1)S(1)}, u32[]{:S(2)}, u32[]{:S(2)}) %all-to-all-start.2) | async-done | bytes 1048608 | tf_op jit(solution)/shard_map/all_to_all | solution.py:764
  54.0 3.6 %all-to-all-start.1 = ((bf16[8,2,256,128]{3,2,1,0:T(8,128)(2,1)}), bf16[8,2,256,128]{3,2,1,0:T(8,128)(2,1)S(1)}, u32[]{:S(2)}, u32[]{:S(2)}) async-start(bf16[8,2,256,128]{3,2,1,0:T(8,128)(2,1)} %get-tuple-element.23), calls=%async_computation.1 | async-start | bytes 2097152 | tf_op jit(solution)/shard_map/all_to_all | solution.py:764
  57.6 0.9 collective-permute-start
  58.5 1.5 collective-permute-done.other_ref.other_key_ref
  60.0 8.3 %weigh.1 = (bf16[36,512,256]{2,1,0:T(8,128)(2,1)}, bf16[36,512,256]{2,1,0:T(8,128)(2,1)}, f32[8,128]{1,0:T(8,128)S(1)}) custom-call(s32[2]{0:T(128)S(1)} %copy-done.1, bf16[8,2,256,128]{3,2,1,0:T(8,128)(2,1)S(1)} %all-to-all-done.2.pair_ref.kq_ref, bf16[8,256,128]{2,1,0:T(8,128)(2,1)S(1)} %collective-permute-done.other_ref.other_key_ref, f32[8,128]{1,0:T(8,128)S(1)} %copy-done.2), custom_call_target="tpu_custom_call" | custom-call | flops 2415919104 | bytes 18874368 | tf_op jit(solution)/shard_map/weigh/pallas_call | solution.py:367
  69.2 4.1 %all-to-all-done.1.pair_ref.vu_ref = bf16[8,2,256,128]{3,2,1,0:T(8,128)(2,1)S(1)} async-done(((bf16[8,2,256,128]{3,2,1,0:T(8,128)(2,1)}), bf16[8,2,256,128]{3,2,1,0:T(8,128)(2,1)S(1)}, u32[]{:S(2)}, u32[]{:S(2)}) %all-to-all-start.1) | async-done | bytes 1048608 | tf_op jit(solution)/shard_map/all_to_all | solution.py:764
  74.2 1.5 collective-permute-done.1.other_ref
  75.8 5.0 %attend.1 = (f32[128,2048]{1,0:T(8,128)S(1)}, f32[8,4,2048]{2,1,0:T(4,128)S(1)}) custom-call(s32[2]{0:T(128)S(1)} %copy-done.1, bf16[8,2,256,128]{3,2,1,0:T(8,128)(2,1)S(1)} %all-to-all-done.1.pair_ref.vu_ref, bf16[8,256,128]{2,1,0:T(8,128)(2,1)S(1)} %collective-permute-done.1.other_ref, bf16[36,512,256]{2,1,0:T(8,128)(2,1)} %get-tuple-element.27.weight_hbm), custom_call_target="tpu_custom_call" | custom-call | flops 2415919104 | bytes 18874368 | tf_op jit(solution)/shard_map/attend/pallas_call | solution.py:435
  80.8 9.8 %all_to_all.35.stats_ref = f32[8,4,2048]{2,1,0:T(4,128)S(1)} all-to-all(f32[8,4,2048]{2,1,0:T(4,128)S(1)} %get-tuple-element.29), channel_id=1, replica_groups={{0,2,4,6,8,10,12,14},{1,3,5,7,9,11,13,15},{16,18,20,22,24,26,28,30},{17..., dimensions={0} | all-to-all | bytes 524288 | tf_op jit(solution)/shard_map/all_to_all | solution.py:764
  90.6 5.4 %back_v.1 = (bf16[8,2,256,128]{3,2,1,0:T(8,128)(2,1)S(1)}, bf16[8,256,128]{2,1,0:T(8,128)(2,1)S(1)}, bf16[128,2048]{1,0:T(8,128)(2,1)S(1)}) custom-call(s32[2]{0:T(128)S(1)} %copy-done.1, bf16[8,2,256,128]{3,2,1,0:T(8,128)(2,1)S(1)} %all-to-all-done.1.pair_ref.vu_ref, f32[128,2048]{1,0:T(8,128)S(1)} %get-tuple-element.28.att_ref, ...), custom_call_target="tpu_custom_call" | custom-call | flops 2415919104 | bytes 18874368 | tf_op jit(solution)/shard_map/back_v/pallas_call | solution.py:514
  96.9 1.5 collective-permute-done.2.sib_ref
  98.4 1.1 merge.2
  99.5 4.2 %all-to-all-start.4 = ((bf16[8,2,256,128]{3,2,1,0:T(8,128)(2,1)}), bf16[8,2,256,128]{3,2,1,0:T(8,128)(2,1)}, u32[]{:S(2)}, u32[]{:S(2)}) async-start(bf16[8,2,256,128]{3,2,1,0:T(8,128)(2,1)} %merge.2), calls=%async_computation.4 | async-start | bytes 2097152 | tf_op jit(solution)/shard_map/all_to_all | solution.py:764
  103.8 1.0 copy-done.5
  104.8 8.9 %back_kq.1 = (bf16[8,2,256,128]{3,2,1,0:T(8,128)(2,1)S(1)}, bf16[8,256,128]{2,1,0:T(8,128)(2,1)S(1)}) custom-call(s32[2]{0:T(128)S(1)} %copy-done.1, bf16[8,2,256,128]{3,2,1,0:T(8,128)(2,1)S(1)} %all-to-all-done.2.pair_ref.kq_ref, bf16[8,2,256,128]{3,2,1,0:T(8,128)(2,1)S(1)} %all-to-all-done.1.pair_ref.vu_ref, ...), custom_call_target="tpu_custom_call" | custom-call | flops 7247757312 | bytes 18874368 | tf_op jit(solution)/shard_map/back_kq/pallas_call | solution.py:588
  114.2 1.5 collective-permute-done.3.sib_ref
  115.7 1.1 merge.3
  116.8 2.9 %all-to-all-done.4.back_ref = bf16[8,2,256,128]{3,2,1,0:T(8,128)(2,1)} async-done(((bf16[8,2,256,128]{3,2,1,0:T(8,128)(2,1)}), bf16[8,2,256,128]{3,2,1,0:T(8,128)(2,1)}, u32[]{:S(2)}, u32[]{:S(2)}) %all-to-all-start.4) | async-done | bytes 1048608 | tf_op jit(solution)/shard_map/all_to_all | solution.py:764
  119.7 3.6 %all-to-all-start.5 = ((bf16[8,2,256,128]{3,2,1,0:T(8,128)(2,1)}), bf16[8,2,256,128]{3,2,1,0:T(8,128)(2,1)S(1)}, u32[]{:S(2)}, u32[]{:S(2)}) async-start(bf16[8,2,256,128]{3,2,1,0:T(8,128)(2,1)} %merge.3), calls=%async_computation.5 | async-start | bytes 2097152 | tf_op jit(solution)/shard_map/all_to_all | solution.py:764
  123.3 7.7 %finish_vg.1 = (bf16[256,1024]{1,0:T(8,128)(2,1)}, f32[256,1024]{1,0:T(8,128)}) custom-call(bf16[8,2,256,128]{3,2,1,0:T(8,128)(2,1)} %all-to-all-done.4.back_ref, bf16[256,1024]{1,0:T(8,128)(2,1)} %get-tuple-element.33.gate_ref, bf16[2,256,1024]{2,1,0:T(8,128)(2,1)} %get-tuple-element.34.slope_ref, bf16[256,1024]{1,0:T(8,128)(2,1)} %get-tuple-element.35.hist_ref.hist_in, ...), custom_call_target="tpu_custom_call" | custom-call | tf_op jit(solution)/shard_map/finish_vg/pallas_call | solution.py:666
  131.0 8.1 %all-to-all-done.5.back_in = bf16[8,2,256,128]{3,2,1,0:T(8,128)(2,1)S(1)} async-done(((bf16[8,2,256,128]{3,2,1,0:T(8,128)(2,1)}), bf16[8,2,256,128]{3,2,1,0:T(8,128)(2,1)S(1)}, u32[]{:S(2)}, u32[]{:S(2)}) %all-to-all-start.5) | async-done | bytes 1048608 | tf_op jit(solution)/shard_map/all_to_all | solution.py:764
  139.0 1.0 copy-done.7
  140.0 6.2 %finish_kq.1 = bf16[128,2,1024]{2,1,0:T(2,128)(2,1)} custom-call(bf16[8,2,256,128]{3,2,1,0:T(8,128)(2,1)} %copy-done.7, bf16[2,256,1024]{2,1,0:T(8,128)(2,1)} %get-tuple-element.40.slope_in, bf16[256,1024]{1,0:T(8,128)(2,1)} %get-tuple-element.35.hist_ref.hist_in, f32[256,1024]{1,0:T(8,128)} %get-tuple-element.41.start_in, bf16[256,1024]{1,0:T(8,128)(2,1)} %cot_in.1, ...), custom_call_target="tpu_custom_call" | custom-call | tf_op jit(solution)/shard_map/finish_kq/pallas_call | solution.py:732
  146.3 18.1 %all_to_all.36.rows_ref = bf16[128,2,1024]{2,1,0:T(2,128)(2,1)S(1)} all-to-all(bf16[128,2,1024]{2,1,0:T(2,128)(2,1)} %finish_kq.1), channel_id=1, replica_groups=mesh['dp'=4,'seq'=32] {'dp','seq'}, dimensions={0} | all-to-all | bytes 1048576 | tf_op jit(solution)/shard_map/all_to_all | solution.py:761
  164.4 1.3 unpick_rows.1
  (23 shorter events, 5.2 us)
Async XLA Ops:
  0.6 13.9 %copy-start = (s32[1,2]{1,0:T(1,128)S(1)}, s32[1,2]{1,0:T(1,128)}, u32[]{:S(2)}) copy-start(s32[1,2]{1,0:T(1,128)} %param.10) | copy-start | bytes 28
  0.6 15.8 %copy-start.6 = (bf16[1024,1024]{1,0:T(8,128)(2,1)S(1)}, bf16[1024,1024]{1,0:T(8,128)(2,1)}, u32[]{:S(2)}) copy-start(bf16[1024,1024]{1,0:T(8,128)(2,1)} %w_out_ref.1) | copy-start | bytes 6291460
  3.0 25.0 %all-to-all-start = ((bf16[128,2,1024]{2,1,0:T(2,128)(2,1)}), bf16[128,2,1024]{2,1,0:T(2,128)(2,1)S(1)}, u32[]{:S(2)}, u32[]{:S(2)}) async-start(bf16[128,2,1024]{2,1,0:T(2,128)(2,1)} %pick_rows.1), calls=%async_computation | async-start | bytes 1048576 | tf_op jit(solution)/shard_map/all_to_all | solution.py:761
  28.0 0.8 copy-start.8
  34.6 19.3 %all-to-all-start.2 = ((bf16[8,2,256,128]{3,2,1,0:T(8,128)(2,1)}), bf16[8,2,256,128]{3,2,1,0:T(8,128)(2,1)S(1)}, u32[]{:S(2)}, u32[]{:S(2)}) async-start(bf16[8,2,256,128]{3,2,1,0:T(8,128)(2,1)} %get-tuple-element.24), calls=%async_computation.2 | async-start | bytes 2097152 | tf_op jit(solution)/shard_map/all_to_all | solution.py:764
  44.7 12.8 %copy-start.2 = (f32[8,128]{1,0:T(8,128)S(1)}, f32[8,128]{1,0:T(8,128)}, u32[]{:S(2)}) copy-start(f32[8,128]{1,0:T(8,128)} %get-tuple-element.25._) | copy-start | bytes 12292
  44.7 15.3 %copy-start.1 = (s32[2]{0:T(128)S(1)}, s32[2]{0:T(128)}, u32[]{:S(2)}) copy-start(s32[2]{0:T(128)} %pad_add_fusion.info) | copy-start | bytes 28
  54.0 19.3 %all-to-all-start.1 = ((bf16[8,2,256,128]{3,2,1,0:T(8,128)(2,1)}), bf16[8,2,256,128]{3,2,1,0:T(8,128)(2,1)S(1)}, u32[]{:S(2)}, u32[]{:S(2)}) async-start(bf16[8,2,256,128]{3,2,1,0:T(8,128)(2,1)} %get-tuple-element.23), calls=%async_computation.1 | async-start | bytes 2097152 | tf_op jit(solution)/shard_map/all_to_all | solution.py:764
  57.6 2.5 %collective-permute-start = (bf16[8,256,128]{2,1,0:T(8,128)(2,1)S(1)}, bf16[8,256,128]{2,1,0:T(8,128)(2,1)S(1)}, u32[]{:S(2)}, u32[]{:S(2)}) collective-permute-start(bf16[8,256,128]{2,1,0:T(8,128)(2,1)S(1)} %first_part.2), channel_id=1, source_target_pairs={{0,1},{1,0},{2,3},{3,2},{4,5},{5,4},{6,7},{7,6},{8,9},{9,8},{10,11... | collective-permute-start | bytes 1572872 | tf_op jit(solution)/shard_map/ppermute | solution.py:773
  68.4 0.8 copy-start.4
  73.3 2.4 %collective-permute-start.1 = (bf16[8,256,128]{2,1,0:T(8,128)(2,1)S(1)}, bf16[8,256,128]{2,1,0:T(8,128)(2,1)S(1)}, u32[]{:S(2)}, u32[]{:S(2)}) collective-permute-start(bf16[8,256,128]{2,1,0:T(8,128)(2,1)S(1)} %first_part.3), channel_id=1, source_target_pairs={{0,1},{1,0},{2,3},{3,2},{4,5},{5,4},{6,7},{7,6},{8,9},{9,8},{10,11... | collective-permute-start | bytes 1572872 | tf_op jit(solution)/shard_map/ppermute | solution.py:776
  96.0 2.4 %collective-permute-start.2 = (bf16[8,256,128]{2,1,0:T(8,128)(2,1)S(1)}, bf16[8,256,128]{2,1,0:T(8,128)(2,1)S(1)}, u32[]{:S(2)}, u32[]{:S(2)}) collective-permute-start(bf16[8,256,128]{2,1,0:T(8,128)(2,1)S(1)} %get-tuple-element.31), channel_id=1, source_target_pairs={{0,1},{1,0},{2,3},{3,2},{4,5},{5,4},{6,7},{7,6},{8,9},{9,8},{10,11... | collective-permute-start | bytes 1572872 | tf_op jit(solution)/shard_map/ppermute | solution.py:780
  99.5 20.2 %all-to-all-start.4 = ((bf16[8,2,256,128]{3,2,1,0:T(8,128)(2,1)}), bf16[8,2,256,128]{3,2,1,0:T(8,128)(2,1)}, u32[]{:S(2)}, u32[]{:S(2)}) async-start(bf16[8,2,256,128]{3,2,1,0:T(8,128)(2,1)} %merge.2), calls=%async_computation.4 | async-start | bytes 2097152 | tf_op jit(solution)/shard_map/all_to_all | solution.py:764
  103.8 1.0 copy-start.5
  113.7 2.0 %collective-permute-start.3 = (bf16[8,256,128]{2,1,0:T(8,128)(2,1)S(1)}, bf16[8,256,128]{2,1,0:T(8,128)(2,1)S(1)}, u32[]{:S(2)}, u32[]{:S(2)}) collective-permute-start(bf16[8,256,128]{2,1,0:T(8,128)(2,1)S(1)} %get-tuple-element.39), channel_id=1, source_target_pairs={{0,1},{1,0},{2,3},{3,2},{4,5},{5,4},{6,7},{7,6},{8,9},{9,8},{10,11... | collective-permute-start | bytes 1572872 | tf_op jit(solution)/shard_map/ppermute | solution.py:783
  119.7 19.3 %all-to-all-start.5 = ((bf16[8,2,256,128]{3,2,1,0:T(8,128)(2,1)}), bf16[8,2,256,128]{3,2,1,0:T(8,128)(2,1)S(1)}, u32[]{:S(2)}, u32[]{:S(2)}) async-start(bf16[8,2,256,128]{3,2,1,0:T(8,128)(2,1)} %merge.3), calls=%async_computation.5 | async-start | bytes 2097152 | tf_op jit(solution)/shard_map/all_to_all | solution.py:764
  139.0 1.0 copy-start.7
  140.0 24.4 %copy-start.3 = (s32[1,256]{1,0:T(1,128)S(1)}, s32[1,256]{1,0:T(1,128)}, u32[]{:S(2)}) copy-start(s32[1,256]{1,0:T(1,128)} %order_ref.3) | copy-start | bytes 3076

commit v6 on v5

--- a/solution.py
+++ b/solution.py
@@ -743,7 +743,7 @@
             pltpu.SemaphoreType.DMA((5,)),
         ],
         out_shape=jax.ShapeDtypeStruct((rows // 2, 2, width), BF16),
-        compiler_params=params(DENSE),
+        compiler_params=params(52),
         name="finish_kq",
     )(back, slope, history, start, cotangent, place, w_in)
 

time: 166 us -> 165 us (level)
  waiting for transfers between devices: 39.3 us -> 36.9 us
    all_to_all x4, waiting for transfers between devices: 24.4 us -> 22.5 us  [to_group(): lax.all_to_all(block, 'seq', split_axis=0, concat_axis=0, tiled=True, axi...]
    unnamed x18 -> x24, local copies, waits for them, and re-layouts: 3.62 us -> 4.51 us
  transfers between devices with their start and end apart: 9 -> 9, of which waited for: 9 -> 9; matrix products, arithmetic and copies ran while one was open for 2% -> 3% of each run, Pallas kernels for 20% -> 20%
where the time goes in v6:
time: 165 us; the launch traced here: 164 us
  Pallas kernels  59.3 us (36%)
  waiting for transfers between devices  36.9 us (22%)
  starting transfers between devices  30.3 us (18%)
  blocking collectives  27.3 us (17%)
  local copies, waits for them, and re-layouts  5.16 us (3%)
  matrix products  3.31 us (2%)
    all_to_all x4, waiting for transfers between devices, to_group(): lax.all_to_all(block, 'seq', split_axis=0, concat_axis=0, tiled=True, axi...  22.5 us
    all_to_all x1, blocking collectives, to_all(): lax.all_to_all(block, ('dp', 'seq'), split_axis=0, concat_axis=0, tiled=T...  17.5 us
    all_to_all x4, starting transfers between devices, to_group(): lax.all_to_all(block, 'seq', split_axis=0, concat_axis=0, tiled=True, axi...  15.6 us
    all_to_all x1, starting transfers between devices, to_all(): lax.all_to_all(block, ('dp', 'seq'), split_axis=0, concat_axis=0, tiled=T...  11.5 us
    all_to_all x1, blocking collectives, to_group(): lax.all_to_all(block, 'seq', split_axis=0, concat_axis=0, tiled=True, axi...  9.84 us
    pallas_call x1, Pallas kernels, back_kq(): pl.pallas_call(back_kq_kernel, out_shape=[jax.ShapeDtypeStruct((CHIPS, 2,...  9.31 us
    pallas_call x1, Pallas kernels, weigh(): pl.pallas_call(weigh_kernel, out_shape=[jax.ShapeDtypeStruct((TILES, KEY_...  8.6 us
    all_to_all x1, waiting for transfers between devices, to_all(): lax.all_to_all(block, ('dp', 'seq'), split_axis=0, concat_axis=0, tiled=T...  8.25 us
  transfers between devices with their start and end apart: 9, of which 9 were waited for; matrix products, arithmetic and copies ran while one was open for 3% of the time, Pallas kernels for 20%

profile of v6, /device:TPU:1, one launch (start us, length us, event | category | flops | bytes accessed | tf_op | source)
XLA Modules:
  0.0 164.5 jit_solution(15371045519554131535)
XLA Ops:
  0.7 2.2 %pick_rows.1 = bf16[128,2,1024]{2,1,0:T(2,128)(2,1)} custom-call(bf16[256,1024]{1,0:T(8,128)(2,1)} %rows_ref.1, s32[1,256]{1,0:T(1,128)} %order_ref.3), custom_call_target="tpu_custom_call" | custom-call | tf_op jit(solution)/shard_map/pick_rows/pallas_call | solution.py:81
  2.9 11.5 %all-to-all-start = ((bf16[128,2,1024]{2,1,0:T(2,128)(2,1)}), bf16[128,2,1024]{2,1,0:T(2,128)(2,1)S(1)}, u32[]{:S(2)}, u32[]{:S(2)}) async-start(bf16[128,2,1024]{2,1,0:T(2,128)(2,1)} %pick_rows.1), calls=%async_computation | async-start | bytes 1048576 | tf_op jit(solution)/shard_map/all_to_all | solution.py:761
  16.4 3.3 %fusion._.up_ref = f32[256,1024]{1,0:T(8,128)} fusion(bf16[256,1024]{1,0:T(8,128)(2,1)S(1)} %copy-done.1, bf16[1024,1024]{1,0:T(8,128)(2,1)} %w_out_ref.1), kind=kOutput, calls=%fused_computation.2 | convolution fusion | flops 536870912 | bytes 3670016 | tf_op jit(solution)/shard_map/dot_general | solution.py:768
  19.7 8.2 %all-to-all-done.arrived_ref = bf16[128,2,1024]{2,1,0:T(2,128)(2,1)S(1)} async-done(((bf16[128,2,1024]{2,1,0:T(2,128)(2,1)}), bf16[128,2,1024]{2,1,0:T(2,128)(2,1)S(1)}, u32[]{:S(2)}, u32[]{:S(2)}) %all-to-all-start) | async-done | bytes 524320 | tf_op jit(solution)/shard_map/all_to_all | solution.py:761
  28.7 5.8 %project_kq.1 = (bf16[256,1024]{1,0:T(8,128)(2,1)}, bf16[256,1024]{1,0:T(8,128)(2,1)}, bf16[2,256,1024]{2,1,0:T(8,128)(2,1)}, bf16[8,2,256,128]{3,2,1,0:T(8,128)(2,1)}) custom-call(s32[2]{0:T(128)} %pad_add_fusion.info, bf16[128,2,1024]{2,1,0:T(2,128)(2,1)} %copy-done.11, s32[1,256]{1,0:T(1,128)} %place_ref.3, bf16[1024,4096]{1,0:T(8,128)(2,1)} %w_hbm.7, ...), custom_call_target="tpu_custom_call" | custom-call | tf_op jit(solution)/shard_map/project_kq/pallas_call | solution.py:196
  34.5 3.6 %all-to-all-start.2 = ((bf16[8,2,256,128]{3,2,1,0:T(8,128)(2,1)}), bf16[8,2,256,128]{3,2,1,0:T(8,128)(2,1)S(1)}, u32[]{:S(2)}, u32[]{:S(2)}) async-start(bf16[8,2,256,128]{3,2,1,0:T(8,128)(2,1)} %get-tuple-element.24), calls=%async_computation.2 | async-start | bytes 2097152 | tf_op jit(solution)/shard_map/all_to_all | solution.py:764
  38.1 6.5 %project_vu.1 = (bf16[256,1024]{1,0:T(8,128)(2,1)}, bf16[2,256,1024]{2,1,0:T(8,128)(2,1)}, bf16[8,2,256,128]{3,2,1,0:T(8,128)(2,1)}, f32[8,128]{1,0:T(8,128)}) custom-call(bf16[256,1024]{1,0:T(8,128)(2,1)} %get-tuple-element.22.normed_ref, bf16[1024,4096]{1,0:T(8,128)(2,1)} %w_hbm.7, f32[256,1024]{1,0:T(8,128)} %fusion._.up_ref), custom_call_target="tpu_custom_call" | custom-call | tf_op jit(solution)/shard_map/project_vu/pallas_call | solution.py:214
  44.6 9.2 %all-to-all-done.2.pair_ref.kq_ref = bf16[8,2,256,128]{3,2,1,0:T(8,128)(2,1)S(1)} async-done(((bf16[8,2,256,128]{3,2,1,0:T(8,128)(2,1)}), bf16[8,2,256,128]{3,2,1,0:T(8,128)(2,1)S(1)}, u32[]{:S(2)}, u32[]{:S(2)}) %all-to-all-start.2) | async-done | bytes 1048608 | tf_op jit(solution)/shard_map/all_to_all | solution.py:764
  53.9 3.6 %all-to-all-start.1 = ((bf16[8,2,256,128]{3,2,1,0:T(8,128)(2,1)}), bf16[8,2,256,128]{3,2,1,0:T(8,128)(2,1)S(1)}, u32[]{:S(2)}, u32[]{:S(2)}) async-start(bf16[8,2,256,128]{3,2,1,0:T(8,128)(2,1)} %get-tuple-element.23), calls=%async_computation.1 | async-start | bytes 2097152 | tf_op jit(solution)/shard_map/all_to_all | solution.py:764
  57.5 0.9 collective-permute-start
  58.4 1.5 collective-permute-done.other_ref.other_key_ref
  59.9 8.6 %weigh.1 = (bf16[36,512,256]{2,1,0:T(8,128)(2,1)}, bf16[36,512,256]{2,1,0:T(8,128)(2,1)}, f32[8,128]{1,0:T(8,128)S(1)}) custom-call(s32[2]{0:T(128)S(1)} %copy-done.5, bf16[8,2,256,128]{3,2,1,0:T(8,128)(2,1)S(1)} %all-to-all-done.2.pair_ref.kq_ref, bf16[8,256,128]{2,1,0:T(8,128)(2,1)S(1)} %collective-permute-done.other_ref.other_key_ref, f32[8,128]{1,0:T(8,128)S(1)} %copy-done.6), custom_call_target="tpu_custom_call" | custom-call | flops 2415919104 | bytes 18874368 | tf_op jit(solution)/shard_map/weigh/pallas_call | solution.py:367
  69.4 3.8 %all-to-all-done.1.pair_ref.vu_ref = bf16[8,2,256,128]{3,2,1,0:T(8,128)(2,1)S(1)} async-done(((bf16[8,2,256,128]{3,2,1,0:T(8,128)(2,1)}), bf16[8,2,256,128]{3,2,1,0:T(8,128)(2,1)S(1)}, u32[]{:S(2)}, u32[]{:S(2)}) %all-to-all-start.1) | async-done | bytes 1048608 | tf_op jit(solution)/shard_map/all_to_all | solution.py:764
  74.1 1.5 collective-permute-done.1.other_ref
  75.7 5.1 %attend.1 = (f32[128,2048]{1,0:T(8,128)S(1)}, f32[8,4,2048]{2,1,0:T(4,128)S(1)}) custom-call(s32[2]{0:T(128)S(1)} %copy-done.5, bf16[8,2,256,128]{3,2,1,0:T(8,128)(2,1)S(1)} %all-to-all-done.1.pair_ref.vu_ref, bf16[8,256,128]{2,1,0:T(8,128)(2,1)S(1)} %collective-permute-done.1.other_ref, bf16[36,512,256]{2,1,0:T(8,128)(2,1)} %get-tuple-element.27.weight_hbm), custom_call_target="tpu_custom_call" | custom-call | flops 2415919104 | bytes 18874368 | tf_op jit(solution)/shard_map/attend/pallas_call | solution.py:435
  80.8 9.8 %all_to_all.35.stats_ref = f32[8,4,2048]{2,1,0:T(4,128)S(1)} all-to-all(f32[8,4,2048]{2,1,0:T(4,128)S(1)} %get-tuple-element.29), channel_id=1, replica_groups={{0,2,4,6,8,10,12,14},{1,3,5,7,9,11,13,15},{16,18,20,22,24,26,28,30},{17..., dimensions={0} | all-to-all | bytes 524288 | tf_op jit(solution)/shard_map/all_to_all | solution.py:764
  90.6 5.5 %back_v.1 = (bf16[8,2,256,128]{3,2,1,0:T(8,128)(2,1)S(1)}, bf16[8,256,128]{2,1,0:T(8,128)(2,1)S(1)}, bf16[128,2048]{1,0:T(8,128)(2,1)S(1)}) custom-call(s32[2]{0:T(128)S(1)} %copy-done.5, bf16[8,2,256,128]{3,2,1,0:T(8,128)(2,1)S(1)} %all-to-all-done.1.pair_ref.vu_ref, f32[128,2048]{1,0:T(8,128)S(1)} %get-tuple-element.28.att_ref, ...), custom_call_target="tpu_custom_call" | custom-call | flops 2415919104 | bytes 18874368 | tf_op jit(solution)/shard_map/back_v/pallas_call | solution.py:514
  97.0 1.5 collective-permute-done.2.sib_ref
  98.5 1.1 merge.2
  100.5 4.2 %all-to-all-start.4 = ((bf16[8,2,256,128]{3,2,1,0:T(8,128)(2,1)}), bf16[8,2,256,128]{3,2,1,0:T(8,128)(2,1)}, u32[]{:S(2)}, u32[]{:S(2)}) async-start(bf16[8,2,256,128]{3,2,1,0:T(8,128)(2,1)} %merge.2), calls=%async_computation.4 | async-start | bytes 2097152 | tf_op jit(solution)/shard_map/all_to_all | solution.py:764
  104.7 1.0 copy-done.4
  105.8 1.0 copy-done.10
  106.8 9.3 %back_kq.1 = (bf16[8,2,256,128]{3,2,1,0:T(8,128)(2,1)S(1)}, bf16[8,256,128]{2,1,0:T(8,128)(2,1)S(1)}) custom-call(s32[2]{0:T(128)S(1)} %copy-done.5, bf16[8,2,256,128]{3,2,1,0:T(8,128)(2,1)S(1)} %all-to-all-done.2.pair_ref.kq_ref, bf16[8,2,256,128]{3,2,1,0:T(8,128)(2,1)S(1)} %all-to-all-done.1.pair_ref.vu_ref, ...), custom_call_target="tpu_custom_call" | custom-call | flops 7247757312 | bytes 18874368 | tf_op jit(solution)/shard_map/back_kq/pallas_call | solution.py:588
  116.6 1.5 collective-permute-done.3.sib_ref
  118.1 1.1 merge.3
  119.3 1.4 all-to-all-done.4.back_ref
  120.6 4.2 %all-to-all-start.5 = ((bf16[8,2,256,128]{3,2,1,0:T(8,128)(2,1)}), bf16[8,2,256,128]{3,2,1,0:T(8,128)(2,1)}, u32[]{:S(2)}, u32[]{:S(2)}) async-start(bf16[8,2,256,128]{3,2,1,0:T(8,128)(2,1)} %merge.3), calls=%async_computation.5 | async-start | bytes 2097152 | tf_op jit(solution)/shard_map/all_to_all | solution.py:764
  124.9 7.8 %finish_vg.1 = (bf16[256,1024]{1,0:T(8,128)(2,1)}, f32[256,1024]{1,0:T(8,128)}) custom-call(bf16[8,2,256,128]{3,2,1,0:T(8,128)(2,1)} %all-to-all-done.4.back_ref, bf16[256,1024]{1,0:T(8,128)(2,1)} %get-tuple-element.33.gate_ref, bf16[2,256,1024]{2,1,0:T(8,128)(2,1)} %get-tuple-element.34.slope_ref, bf16[256,1024]{1,0:T(8,128)(2,1)} %get-tuple-element.35.hist_ref.hist_in, ...), custom_call_target="tpu_custom_call" | custom-call | tf_op jit(solution)/shard_map/finish_vg/pallas_call | solution.py:666
  132.7 8.1 %all-to-all-done.5.back_in = bf16[8,2,256,128]{3,2,1,0:T(8,128)(2,1)} async-done(((bf16[8,2,256,128]{3,2,1,0:T(8,128)(2,1)}), bf16[8,2,256,128]{3,2,1,0:T(8,128)(2,1)}, u32[]{:S(2)}, u32[]{:S(2)}) %all-to-all-start.5) | async-done | bytes 1048608 | tf_op jit(solution)/shard_map/all_to_all | solution.py:764
  140.8 4.9 %finish_kq.1 = bf16[128,2,1024]{2,1,0:T(2,128)(2,1)S(1)} custom-call(bf16[8,2,256,128]{3,2,1,0:T(8,128)(2,1)} %all-to-all-done.5.back_in, bf16[2,256,1024]{2,1,0:T(8,128)(2,1)} %get-tuple-element.40.slope_in, bf16[256,1024]{1,0:T(8,128)(2,1)S(1)} %copy-done.2, f32[256,1024]{1,0:T(8,128)} %get-tuple-element.41.start_in, bf16[256,1024]{1,0:T(8,128)(2,1)S(1)} %copy-done.1, ...), custom_call_target="tpu_custom_call" | custom-call | tf_op jit(solution)/shard_map/finish_kq/pallas_call | solution.py:732
  145.7 17.5 %all_to_all.36.rows_ref = bf16[128,2,1024]{2,1,0:T(2,128)(2,1)S(1)} all-to-all(bf16[128,2,1024]{2,1,0:T(2,128)(2,1)S(1)} %finish_kq.1), channel_id=1, replica_groups=mesh['dp'=4,'seq'=32] {'dp','seq'}, dimensions={0} | all-to-all | bytes 1048576 | tf_op jit(solution)/shard_map/all_to_all | solution.py:761
  163.2 1.3 unpick_rows.1
  (29 shorter events, 6.0 us)
Async XLA Ops:
  0.6 13.8 %copy-start = (s32[1,2]{1,0:T(1,128)S(1)}, s32[1,2]{1,0:T(1,128)}, u32[]{:S(2)}) copy-start(s32[1,2]{1,0:T(1,128)} %param.10) | copy-start | bytes 28
  0.6 15.7 %copy-start.1 = (bf16[256,1024]{1,0:T(8,128)(2,1)S(1)}, bf16[256,1024]{1,0:T(8,128)(2,1)}, u32[]{:S(2)}) copy-start(bf16[256,1024]{1,0:T(8,128)(2,1)} %cot_in.1) | copy-start | bytes 1572868
  2.9 25.0 %all-to-all-start = ((bf16[128,2,1024]{2,1,0:T(2,128)(2,1)}), bf16[128,2,1024]{2,1,0:T(2,128)(2,1)S(1)}, u32[]{:S(2)}, u32[]{:S(2)}) async-start(bf16[128,2,1024]{2,1,0:T(2,128)(2,1)} %pick_rows.1), calls=%async_computation | async-start | bytes 1048576 | tf_op jit(solution)/shard_map/all_to_all | solution.py:761
  27.9 0.8 copy-start.11
  34.5 19.3 %all-to-all-start.2 = ((bf16[8,2,256,128]{3,2,1,0:T(8,128)(2,1)}), bf16[8,2,256,128]{3,2,1,0:T(8,128)(2,1)S(1)}, u32[]{:S(2)}, u32[]{:S(2)}) async-start(bf16[8,2,256,128]{3,2,1,0:T(8,128)(2,1)} %get-tuple-element.24), calls=%async_computation.2 | async-start | bytes 2097152 | tf_op jit(solution)/shard_map/all_to_all | solution.py:764
  44.6 12.8 %copy-start.6 = (f32[8,128]{1,0:T(8,128)S(1)}, f32[8,128]{1,0:T(8,128)}, u32[]{:S(2)}) copy-start(f32[8,128]{1,0:T(8,128)} %get-tuple-element.25._) | copy-start | bytes 12292
  44.6 15.3 %copy-start.5 = (s32[2]{0:T(128)S(1)}, s32[2]{0:T(128)}, u32[]{:S(2)}) copy-start(s32[2]{0:T(128)} %pad_add_fusion.info) | copy-start | bytes 28
  53.9 19.3 %all-to-all-start.1 = ((bf16[8,2,256,128]{3,2,1,0:T(8,128)(2,1)}), bf16[8,2,256,128]{3,2,1,0:T(8,128)(2,1)S(1)}, u32[]{:S(2)}, u32[]{:S(2)}) async-start(bf16[8,2,256,128]{3,2,1,0:T(8,128)(2,1)} %get-tuple-element.23), calls=%async_computation.1 | async-start | bytes 2097152 | tf_op jit(solution)/shard_map/all_to_all | solution.py:764
  57.5 2.5 %collective-permute-start = (bf16[8,256,128]{2,1,0:T(8,128)(2,1)S(1)}, bf16[8,256,128]{2,1,0:T(8,128)(2,1)S(1)}, u32[]{:S(2)}, u32[]{:S(2)}) collective-permute-start(bf16[8,256,128]{2,1,0:T(8,128)(2,1)S(1)} %first_part.2), channel_id=1, source_target_pairs={{0,1},{1,0},{2,3},{3,2},{4,5},{5,4},{6,7},{7,6},{8,9},{9,8},{10,11... | collective-permute-start | bytes 1572872 | tf_op jit(solution)/shard_map/ppermute | solution.py:773
  68.6 0.8 copy-start.9
  73.2 2.4 %collective-permute-start.1 = (bf16[8,256,128]{2,1,0:T(8,128)(2,1)S(1)}, bf16[8,256,128]{2,1,0:T(8,128)(2,1)S(1)}, u32[]{:S(2)}, u32[]{:S(2)}) collective-permute-start(bf16[8,256,128]{2,1,0:T(8,128)(2,1)S(1)} %first_part.3), channel_id=1, source_target_pairs={{0,1},{1,0},{2,3},{3,2},{4,5},{5,4},{6,7},{7,6},{8,9},{9,8},{10,11... | collective-permute-start | bytes 1572872 | tf_op jit(solution)/shard_map/ppermute | solution.py:776
  96.1 2.4 %collective-permute-start.2 = (bf16[8,256,128]{2,1,0:T(8,128)(2,1)S(1)}, bf16[8,256,128]{2,1,0:T(8,128)(2,1)S(1)}, u32[]{:S(2)}, u32[]{:S(2)}) collective-permute-start(bf16[8,256,128]{2,1,0:T(8,128)(2,1)S(1)} %get-tuple-element.31), channel_id=1, source_target_pairs={{0,1},{1,0},{2,3},{3,2},{4,5},{5,4},{6,7},{7,6},{8,9},{9,8},{10,11... | collective-permute-start | bytes 1572872 | tf_op jit(solution)/shard_map/ppermute | solution.py:780
  99.7 0.8 copy-start.3
  100.5 20.2 %all-to-all-start.4 = ((bf16[8,2,256,128]{3,2,1,0:T(8,128)(2,1)}), bf16[8,2,256,128]{3,2,1,0:T(8,128)(2,1)}, u32[]{:S(2)}, u32[]{:S(2)}) async-start(bf16[8,2,256,128]{3,2,1,0:T(8,128)(2,1)} %merge.2), calls=%async_computation.4 | async-start | bytes 2097152 | tf_op jit(solution)/shard_map/all_to_all | solution.py:764
  104.7 1.0 copy-start.4
  105.8 1.0 copy-start.10
  116.1 2.0 %collective-permute-start.3 = (bf16[8,256,128]{2,1,0:T(8,128)(2,1)S(1)}, bf16[8,256,128]{2,1,0:T(8,128)(2,1)S(1)}, u32[]{:S(2)}, u32[]{:S(2)}) collective-permute-start(bf16[8,256,128]{2,1,0:T(8,128)(2,1)S(1)} %get-tuple-element.39), channel_id=1, source_target_pairs={{0,1},{1,0},{2,3},{3,2},{4,5},{5,4},{6,7},{7,6},{8,9},{9,8},{10,11... | collective-permute-start | bytes 1572872 | tf_op jit(solution)/shard_map/ppermute | solution.py:783
  120.6 20.1 %all-to-all-start.5 = ((bf16[8,2,256,128]{3,2,1,0:T(8,128)(2,1)}), bf16[8,2,256,128]{3,2,1,0:T(8,128)(2,1)}, u32[]{:S(2)}, u32[]{:S(2)}) async-start(bf16[8,2,256,128]{3,2,1,0:T(8,128)(2,1)} %merge.3), calls=%async_computation.5 | async-start | bytes 2097152 | tf_op jit(solution)/shard_map/all_to_all | solution.py:764
  124.9 15.9 %copy-start.2 = (bf16[256,1024]{1,0:T(8,128)(2,1)S(1)}, bf16[256,1024]{1,0:T(8,128)(2,1)}, u32[]{:S(2)}) copy-start(bf16[256,1024]{1,0:T(8,128)(2,1)} %get-tuple-element.35.hist_ref.hist_in) | copy-start | bytes 1572868
  124.9 15.9 %copy-start.8 = (s32[1,256]{1,0:T(1,128)S(1)}, s32[1,256]{1,0:T(1,128)}, u32[]{:S(2)}) copy-start(s32[1,256]{1,0:T(1,128)} %place_ref.3) | copy-start | bytes 3076
  140.8 22.4 %copy-start.7 = (s32[1,256]{1,0:T(1,128)S(1)}, s32[1,256]{1,0:T(1,128)}, u32[]{:S(2)}) copy-start(s32[1,256]{1,0:T(1,128)} %order_ref.3) | copy-start | bytes 3076
